TPU v7x, 256 devices: a whole 4x4x8 slice. The times are simulated.
256 devices in a mesh: row: 16 (over z, x_lo), col: 16 (over y, x_hi, core).
Axes of the slice: x: 4 (x_hi: 2, x_lo: 2; x = x_hi * 2 + x_lo), y: 4, z: 8, core: 2. Of those that a mesh axis runs over, the one named last changes fastest.
Arguments:
- a_matrix: bfloat16 [12288, 12288], P('row', 'col'), may hold values from -0.1875 to 0.1875
- prolong: bfloat16 [12288, 2048], P('row', 'col'), may hold values from -1 to 1
- a_pattern: int32 [96, 96], P('row', 'col'), may hold values from 0 to 1, as said below
- p_pattern: int32 [96, 16], P('row', 'col'), may hold values from 0 to 1, as said below
Outputs:
- coarse: float32 [2048, 2048], P('row', 'col')
Inputs may be any that keep to these rules, and one draw needn't show every extreme that they name: `a_pattern`: symmetric; every diagonal block is stored. `p_pattern`: every fine block row stores at least one coarse block.
All inputs are finite; a program needn't handle non-finite values.
Results may differ from a plain program's by a relative error of at most 0.0029.
Values may be sent and summed in bfloat16 or wider, within the bound.
No kernel may reach another device: no remote copies, remote signals or barrier semaphores. Data moves between devices by JAX's collectives and lax.ppermute only.
A program may use at most 128 MiB of HBM per device.

v0:
```python
import jax
import jax.numpy as jnp
from jax import lax
from jax.sharding import PartitionSpec as P

BLOCK = 128


def expand(pattern, width):
    return jnp.repeat(jnp.repeat(pattern, width, axis=0), width, axis=1).astype(jnp.bfloat16)


def local(a_matrix, prolong, a_pattern, p_pattern):
    a_eff = a_matrix * expand(a_pattern, BLOCK)
    p_eff = prolong * expand(p_pattern, BLOCK)
    p_cols = lax.all_gather(p_eff, "row", axis=0, tiled=True)
    w_tile = jnp.dot(
        lax.all_gather(a_eff, "col", axis=1, tiled=True), p_cols, preferred_element_type=jnp.float32
    ).astype(jnp.bfloat16)
    p_wide = lax.all_gather(p_eff, "col", axis=1, tiled=True)
    return lax.psum_scatter(
        lax.dot_general(
            p_wide, w_tile, (((0,), (0,)), ((), ())), preferred_element_type=jnp.float32
        ),
        "row",
        scatter_dimension=0,
        tiled=True,
    )


def solution(mesh):
    placed = (P("row", "col"), P("row", "col"), P("row", "col"), P("row", "col"))
    return jax.shard_map(
        local, mesh=mesh, in_specs=placed, out_specs=P("row", "col"), check_vma=False
    )
```

profile of v0, /device:TPU:2, one launch (start us, length us, event | category | flops | bytes accessed | tf_op | source)
XLA Modules:
  0.0 366.0 jit_solution(10982976130945202735)
XLA Ops:
  6.5 0.0 copy-start
  6.5 0.0 all-gather.4.cloned.1.call-start
  6.5 0.7 convert_bitcast_fusion
  7.2 0.1 broadcast_bitcast_fusion.1
  7.3 1.8 broadcast_multiply_fusion
  9.1 0.0 all-gather.4.cloned.1.call-update
  9.1 0.0 all-gather.8.cloned.1.call-start
  9.1 0.7 all-gather.8.cloned.1.call-update
  9.8 0.0 all-gather.6.cloned.1.call-start
  9.9 1.6 copy.6
  11.5 0.0 copy-done
  11.5 0.1 copy.5
  11.6 0.1 broadcast_bitcast_fusion
  11.7 1.2 bitcast_multiply_fusion
  12.9 0.0 all-gather.6.cloned.1.call-update
  12.9 0.0 reduce-scatter.2.cloned.1.call-start
  12.9 56.0 %all-gather.4.cloned.1.call-done = bf16[768,2048]{1,0:T(8,128)(2,1)} async-done(((bf16[768,128]{1,0:T(8,128)(2,1)}), bf16[768,2048]{1,0:T(8,128)(2,1)}) %all-gather.4.cloned.1.call-update) | async-done | bytes 3145744 | tf_op jit(solution)/shard_map/all_gather | solution.py:20
  68.9 81.0 %all-gather.8.cloned.1.call-done = bf16[12288,128]{1,0:T(8,128)(2,1)} async-done(((bf16[768,128]{1,0:T(8,128)(2,1)}), bf16[12288,128]{1,0:T(8,128)(2,1)}) %all-gather.8.cloned.1.call-update) | async-done | bytes 3145744 | tf_op jit(solution)/shard_map/all_gather | solution.py:16
  150.0 125.3 %all-gather.6.cloned.1.call-done = bf16[768,12288]{0,1:T(8,128)(2,1)} async-done(((bf16[768,768]{0,1:T(8,128)(2,1)}), bf16[768,12288]{0,1:T(8,128)(2,1)}) %all-gather.6.cloned.1.call-update) | async-done | bytes 18874384 | tf_op jit(solution)/shard_map/all_gather | solution.py:18
  275.2 16.7 %fusion = f32[2048,128]{1,0:T(8,128)} fusion(bf16[768,2048]{1,0:T(8,128)(2,1)} %all-gather.4.cloned.1.call-done, bf16[768,12288]{0,1:T(8,128)(2,1)} %all-gather.6.cloned.1.call-done, bf16[12288,128]{1,0:T(8,128)(2,1)} %all-gather.8.cloned.1.call-done), kind=kOutput, calls=%fused_computation.7 | convolution fusion | flops 2818670592 | bytes 26214400 | tf_op jit(solution)/shard_map/dot_general | solution.py:22
  291.9 0.0 reduce-scatter.2.cloned.1.call-update
  291.9 67.6 %reduce-scatter.2.cloned.1.call-done = f32[128,128]{1,0:T(8,128)} async-done(((f32[2048,128]{1,0:T(8,128)}), f32[128,128]{1,0:T(8,128)}) %reduce-scatter.2.cloned.1.call-update) | async-done | bytes 65552 | tf_op jit(solution)/shard_map/reduce_scatter | solution.py:21
  (2 shorter events, 0.0 us)
Async XLA Ops:
  6.5 4.9 %copy-start = (s32[6,6]{1,0:T(8,128)S(1)}, s32[6,6]{1,0:T(8,128)}, u32[]{:S(2)}) copy-start(s32[6,6]{1,0:T(8,128)} %param.6) | copy-start | bytes 436
  6.5 62.4 %all-gather.4.cloned.1.call-start = ((), (), s32[]{:S(2)}) async-start(), calls=%async_computation.1 | async-start | bytes 3342336 | tf_op jit(solution)/shard_map/all_gather | solution.py:20
  9.1 140.9 %all-gather.8.cloned.1.call-start = ((), (), s32[]{:S(2)}) async-start(), calls=%async_computation.3 | async-start | bytes 3342336 | tf_op jit(solution)/shard_map/all_gather | solution.py:16
  9.8 265.4 %all-gather.6.cloned.1.call-start = ((), (), s32[]{:S(2)}) async-start(), calls=%async_computation.2 | async-start | bytes 20054016 | tf_op jit(solution)/shard_map/all_gather | solution.py:18
  12.9 346.6 %reduce-scatter.2.cloned.1.call-start = ((), (), s32[]{:S(2)}) async-start(), calls=%async_computation.4 | async-start | bytes 1114112 | tf_op jit(solution)/shard_map/reduce_scatter | solution.py:21
Sparse Core Ops, SparseCore 0:
  10.0 58.8 all-gather.3
  70.7 79.2 all-gather.7
  152.7 122.4 all-gather.5
  292.1 67.3 reduce-scatter.1
where the time goes:
time: 369 us; the launch traced here: 366 us
  waiting for transfers between devices  331 us (90%)
  matrix products  16.7 us (5%)
  between operations  13.2 us (4%)
    all_gather x1, waiting for transfers between devices, local(): lax.all_gather(a_eff, 'col', axis=1, tiled=True)  125 us
    all_gather x1, waiting for transfers between devices, local(): p_cols = lax.all_gather(p_eff, 'row', axis=0, tiled=True)  81 us
    reduce_scatter x1, waiting for transfers between devices, local(): lax.psum_scatter(lax.dot_general(p_wide, w_tile, (((0,), (0,)), ((), ()))...  67.6 us
    all_gather x1, waiting for transfers between devices, local(): p_wide = lax.all_gather(p_eff, 'col', axis=1, tiled=True)  56 us
    dot_general x1, matrix products, local(): lax.dot_general(p_wide, w_tile, (((0,), (0,)), ((), ())), preferred_eleme...  16.7 us
  transfers between devices with their start and end apart: 4, of which 4 were waited for; matrix products, arithmetic and copies ran while one was open for 1% of the time, Pallas kernels for 0%

commit v1 on v0

v1 whole, which is shorter than its diff:
```python
import jax
import jax.numpy as jnp
from jax import lax
from jax.sharding import PartitionSpec as P

BLOCK = 128
AXES = ("row", "col")
PLANES, LANES = 8, 4


def place(z, xl, y, xh, k):
    return (2 * (z % PLANES) + xl) * 16 + 4 * (y % LANES) + 2 * xh + k


SPOTS = [
    (z, xl, y, xh, k)
    for z in range(PLANES)
    for xl in range(2)
    for y in range(LANES)
    for xh in range(2)
    for k in range(2)
]


def send(value, target):
    pairs = [(place(*spot), place(*target(*spot))) for spot in SPOTS]
    return lax.ppermute(value, AXES, pairs)


def turn(z, xl, y, xh, k):
    shift = (y - z // 2) % LANES
    return (z + shift if z % 2 else z - shift), xl, z // 2, xh, k


def z_up(z, xl, y, xh, k):
    return z + 1, xl, y, xh, k


def z_down(z, xl, y, xh, k):
    return z - 1, xl, y, xh, k


def y_up(z, xl, y, xh, k):
    return z, xl, y + 1, xh, k


def y_down(z, xl, y, xh, k):
    return z, xl, y - 1, xh, k


def far_x(z, xl, y, xh, k):
    return z, xl, y, 1 - xh, k


def other_core(z, xl, y, xh, k):
    return z, xl, y, xh, 1 - k


def swap(z, xl, y, xh, k):
    return z, k, y, xh, xl


def swap_far(z, xl, y, xh, k):
    return z, k, y, 1 - xh, xl


W_GROUPS = [
    [place(z, s ^ k, y, xh, k) for s in range(2) for y in range(LANES)]
    for z in range(PLANES)
    for xh in range(2)
    for k in range(2)
]


def coarse_row(y, xh, k, dk, dy, dx):
    i = 4 * ((y - dy) % LANES) + 2 * (xh ^ dx) + (k ^ dk)
    return i // 2, i % 2


C_GROUPS = [
    [
        place(*coarse_row(y, xh, k, dk, dy, dx), y, xh, k)
        for dk in range(2)
        for dy in range(LANES)
        for dx in range(2)
    ]
    for y in range(LANES)
    for xh in range(2)
    for k in range(2)
]


def expand(pattern, width):
    return jnp.repeat(jnp.repeat(pattern, width, axis=0), width, axis=1).astype(jnp.bfloat16)


def dot32(a, b, contract=((1,), (0,))):
    return lax.dot_general(a, b, (contract, ((), ())), preferred_element_type=jnp.float32)


def column_rows(pair):
    pairs = [pair]
    for _ in range(LANES - 1):
        pairs.append(send(pairs[-1], y_up))
    own = jnp.concatenate(pairs)
    return jnp.concatenate([own, send(own, other_core)])


def pack(c_part):
    top = jnp.maximum(jnp.max(jnp.abs(c_part)), 1e-30)
    power = jnp.ceil(jnp.log2(top)) - 14.0
    scaled = c_part * jnp.exp2(-power)
    tail = jnp.full((c_part.shape[0], 16, c_part.shape[2]), power)
    return jnp.concatenate([scaled, tail], axis=1).astype(jnp.float16)


def unpack(parts):
    parts = parts.astype(jnp.float32)
    return jnp.sum(parts[:, :BLOCK] * jnp.exp2(parts[:, BLOCK : BLOCK + 1, :1]), axis=0)


def fine_rows(first):
    half = first.shape[0] // 2
    up, down = [first], [first]
    for step in range(1, 4):
        both = lax.optimization_barrier((send(up[-1], z_up), send(down[-1], z_down)))
        up.append(both[0])
        down.append(both[1])
    far = jnp.concatenate([send(up[3][:half], z_up), send(down[3][half:], z_down)])
    return jnp.stack([first, down[1], down[2], down[3], far, up[3], up[2], up[1]])


def local(a_matrix, prolong, a_pattern, p_pattern):
    row, col = lax.axis_index("row"), lax.axis_index("col")
    z, y, xh = row // 2, col // 4, (col // 2) % 2
    p_eff = prolong * expand(p_pattern, BLOCK)
    p_eff, a_matrix = lax.optimization_barrier((p_eff, a_matrix))
    first = send(p_eff, turn)
    a_eff = a_matrix * expand(a_pattern, BLOCK)
    near, distant = send(a_eff, swap), send(a_eff, swap_far)
    pair = jnp.stack([p_eff, send(p_eff, far_x)])
    first, pair, _ = lax.optimization_barrier((first, pair, a_eff))
    blocks = fine_rows(first)
    near_2, distant_2 = send(near, other_core), send(distant, other_core)
    p_wide = column_rows(pair)

    def columns(flip):
        odd = flip ^ xh
        shifts = [lax.rem(yy - y + LANES, LANES) for yy in range(LANES)]
        picks = [2 * y + jnp.where(odd == 1, 1 + s, -s) - z for s in shifts]
        return jnp.stack(
            [lax.dynamic_index_in_dim(blocks, (i + 2 * PLANES) % PLANES, keepdims=False) for i in picks]
        )

    p_0, p_1 = columns(0), columns(1)

    def product(a, p):
        return jnp.einsum("rc,ycj->yrj", a, p, preferred_element_type=jnp.float32)

    w_part = jnp.concatenate(
        [
            (product(near, p_0) + product(distant, p_1)).astype(jnp.bfloat16),
            (product(near_2, p_0) + product(distant_2, p_1)).astype(jnp.bfloat16),
        ]
    )
    w_parts = lax.all_to_all(w_part, AXES, 0, 0, axis_index_groups=W_GROUPS, tiled=True)
    w = jnp.sum(w_parts.astype(jnp.float32), axis=0)
    w_high = lax.reduce_precision(w, 8, 7)
    w_both = jnp.concatenate([w_high, w - w_high], axis=1).astype(jnp.bfloat16)
    c_both = dot32(p_wide, w_both)
    c_part = c_both[..., :BLOCK] + c_both[..., BLOCK:]
    return unpack(lax.all_to_all(pack(c_part), AXES, 0, 0, axis_index_groups=C_GROUPS, tiled=True))


def solution(mesh):
    placed = (P("row", "col"),) * 4
    return jax.shard_map(
        local, mesh=mesh, in_specs=placed, out_specs=P("row", "col"), check_vma=False
    )
```

time: 369 us -> 127 us (0.34)
  waiting for transfers between devices: 331 us -> 32.5 us
  starting transfers between devices: 0.12 us -> 41.4 us
  blocking collectives: 0 us -> 24.7 us
  between operations: 13.2 us -> 1.29 us
  matrix products: 16.7 us -> 7.45 us
  local copies, waits for them, and re-layouts: 1.84 us -> 9.42 us
  other arithmetic: 3.63 us -> 9.31 us
    all_gather x3 -> x0, waiting for transfers between devices: 262 us -> none  [the longest x1 125 us: local(): lax.all_gather(a_eff, 'col', axis=1, tiled=True)]
    reduce_scatter x1 -> x0, waiting for transfers between devices: 67.6 us -> none  [local(): lax.psum_scatter(lax.dot_general(p_wide, w_tile, (((0,), (0,)), ((), ()))...]
    ppermute x0 -> x18, starting transfers between devices: none -> 35.9 us  [send(): return lax.ppermute(value, AXES, pairs)]
    all_to_all x0 -> x1, blocking collectives: none -> 24.7 us  [local(): lax.all_to_all(pack(c_part), AXES, 0, 0, axis_index_groups=C_GROUPS, tile...]
    ppermute x0 -> x18, waiting for transfers between devices: none -> 17.8 us  [send(): return lax.ppermute(value, AXES, pairs)]
    all_to_all x0 -> x1, waiting for transfers between devices: none -> 14.7 us  [local(): lax.all_to_all(w_part, AXES, 0, 0, axis_index_groups=W_GROUPS, tiled=True)]
    dot_general x1 -> x5, matrix products: 16.7 us -> 7.45 us  [the longest x4 4.58 us: product(): return jnp.einsum('rc,ycj->yrj', a, p, preferred_element_type=jnp.float32)]
    all_to_all x0 -> x1, starting transfers between devices: none -> 5.54 us  [local(): lax.all_to_all(w_part, AXES, 0, 0, axis_index_groups=W_GROUPS, tiled=True)]
  transfers between devices with their start and end apart: 4 -> 19, of which waited for: 4 -> 8; matrix products, arithmetic and copies ran while one was open for 1% -> 14% of each run, Pallas kernels for 0% -> 0%
where the time goes in v1:
time: 127 us; the launch traced here: 126 us
  starting transfers between devices  41.4 us (33%)
  waiting for transfers between devices  32.5 us (26%)
  blocking collectives  24.7 us (19%)
  local copies, waits for them, and re-layouts  9.42 us (7%)
  other arithmetic  9.31 us (7%)
  matrix products  7.45 us (6%)
  between operations  1.29 us (1%)
    ppermute x18, starting transfers between devices, send(): return lax.ppermute(value, AXES, pairs)  35.9 us
    all_to_all x1, blocking collectives, local(): lax.all_to_all(pack(c_part), AXES, 0, 0, axis_index_groups=C_GROUPS, tile...  24.7 us
    ppermute x18, waiting for transfers between devices, send(): return lax.ppermute(value, AXES, pairs)  17.8 us
    all_to_all x1, waiting for transfers between devices, local(): lax.all_to_all(w_part, AXES, 0, 0, axis_index_groups=W_GROUPS, tiled=True)  14.7 us
    unnamed x25, local copies, waits for them, and re-layouts  6.83 us
    all_to_all x1, starting transfers between devices, local(): lax.all_to_all(w_part, AXES, 0, 0, axis_index_groups=W_GROUPS, tiled=True)  5.54 us
    dot_general x4, matrix products, product(): return jnp.einsum('rc,ycj->yrj', a, p, preferred_element_type=jnp.float32)  4.58 us
    dot_general x1, matrix products, dot32(): lax.dot_general(a, b, (contract, ((), ())), preferred_element_type=jnp.fl...  2.88 us
  transfers between devices with their start and end apart: 19, of which 8 were waited for; matrix products, arithmetic and copies ran while one was open for 14% of the time, Pallas kernels for 0%

profile of v1, /device:TPU:2, one launch (start us, length us, event | category | flops | bytes accessed | tf_op | source)
XLA Modules:
  0.0 126.1 jit_solution(4356428119145827319)
XLA Ops:
  2.5 2.1 %collective-permute-start.1 = (bf16[768,128]{0,1:T(8,128)(2,1)}, bf16[768,128]{0,1:T(8,128)(2,1)}, u32[]{:S(2)}, u32[]{:S(2)}) collective-permute-start(bf16[768,128]{0,1:T(8,128)(2,1)} %broadcast_multiply_fusion), channel_id=1, source_target_pairs={{0,2},{1,3},{2,0},{3,1},{4,6},{5,7},{6,4},{7,5},{8,10},{9,11},{10,... | collective-permute-start | bytes 589832 | tf_op jit(solution)/shard_map/ppermute | solution.py:27
  4.6 3.0 %collective-permute-start = (bf16[768,128]{0,1:T(8,128)(2,1)}, bf16[768,128]{0,1:T(8,128)(2,1)}, u32[]{:S(2)}, u32[]{:S(2)}) collective-permute-start(bf16[768,128]{0,1:T(8,128)(2,1)} %broadcast_multiply_fusion), channel_id=1, source_target_pairs={{0,0},{1,1},{2,2},{3,3},{4,224},{5,225},{6,226},{7,227},{8,192},{9... | collective-permute-start | bytes 589832 | tf_op jit(solution)/shard_map/ppermute | solution.py:27
  11.1 4.2 %collective-permute-start.14 = (bf16[768,768]{1,0:T(8,128)(2,1)}, bf16[768,768]{1,0:T(8,128)(2,1)S(1)}, u32[]{:S(2)}, u32[]{:S(2)}) collective-permute-start(bf16[768,768]{1,0:T(8,128)(2,1)} %mul.33), channel_id=1, source_target_pairs={{0,0},{1,16},{2,2},{3,18},{4,4},{5,20},{6,6},{7,22},{8,8},{9,24},{... | collective-permute-start | bytes 3538952 | tf_op jit(solution)/shard_map/ppermute | solution.py:27
  16.6 2.0 %collective-permute-start.6 = (bf16[768,128]{0,1:T(8,128)(2,1)}, bf16[768,128]{0,1:T(8,128)(2,1)S(1)}, u32[]{:S(2)}, u32[]{:S(2)}) collective-permute-start(bf16[768,128]{0,1:T(8,128)(2,1)} %collective-permute-done), channel_id=1, source_target_pairs={{0,32},{1,33},{2,34},{3,35},{4,36},{5,37},{6,38},{7,39},{8,40},{9,... | collective-permute-start | bytes 589832 | tf_op jit(solution)/shard_map/ppermute | solution.py:27
  18.6 3.0 %collective-permute-start.7 = (bf16[768,128]{0,1:T(8,128)(2,1)}, bf16[768,128]{0,1:T(8,128)(2,1)S(1)}, u32[]{:S(2)}, u32[]{:S(2)}) collective-permute-start(bf16[768,128]{0,1:T(8,128)(2,1)} %collective-permute-done), channel_id=1, source_target_pairs={{0,224},{1,225},{2,226},{3,227},{4,228},{5,229},{6,230},{7,231},{8... | collective-permute-start | bytes 589832 | tf_op jit(solution)/shard_map/ppermute | solution.py:27
  21.6 4.6 %collective-permute-start.2 = (bf16[2,768,128]{1,2,0:T(8,128)(2,1)S(1)}, bf16[2,768,128]{1,2,0:T(8,128)(2,1)S(1)}, u32[]{:S(2)}, u32[]{:S(2)}) collective-permute-start(bf16[2,768,128]{1,2,0:T(8,128)(2,1)S(1)} %pad_maximum_fusion.4), channel_id=1, source_target_pairs={{0,4},{1,5},{2,6},{3,7},{4,8},{5,9},{6,10},{7,11},{8,12},{9,13},{1... | collective-permute-start | bytes 1179656 | tf_op jit(solution)/shard_map/ppermute | solution.py:27
  27.1 2.2 %collective-permute-done.7 = bf16[768,128]{0,1:T(8,128)(2,1)S(1)} collective-permute-done((bf16[768,128]{0,1:T(8,128)(2,1)}, bf16[768,128]{0,1:T(8,128)(2,1)S(1)}, u32[]{:S(2)}, u32[]{:S(2)}) %collective-permute-start.7) | collective-permute-done | bytes 196640 | tf_op jit(solution)/shard_map/ppermute | solution.py:27
  29.3 2.0 %collective-permute-start.8 = (bf16[768,128]{0,1:T(8,128)(2,1)S(1)}, bf16[768,128]{0,1:T(8,128)(2,1)S(1)}, u32[]{:S(2)}, u32[]{:S(2)}) collective-permute-start(bf16[768,128]{0,1:T(8,128)(2,1)S(1)} %collective-permute-done.6), channel_id=1, source_target_pairs={{0,32},{1,33},{2,34},{3,35},{4,36},{5,37},{6,38},{7,39},{8,40},{9,... | collective-permute-start | bytes 589832 | tf_op jit(solution)/shard_map/ppermute | solution.py:27
  32.6 3.6 %collective-permute-done.8 = bf16[768,128]{0,1:T(8,128)(2,1)S(1)} collective-permute-done((bf16[768,128]{0,1:T(8,128)(2,1)S(1)}, bf16[768,128]{0,1:T(8,128)(2,1)S(1)}, u32[]{:S(2)}, u32[]{:S(2)}) %collective-permute-start.8) | collective-permute-done | bytes 196640 | tf_op jit(solution)/shard_map/ppermute | solution.py:27
  38.4 1.9 %collective-permute-start.11 = (bf16[768,128]{0,1:T(8,128)(2,1)S(1)}, bf16[768,128]{0,1:T(8,128)(2,1)S(1)}, u32[]{:S(2)}, u32[]{:S(2)}) collective-permute-start(bf16[768,128]{0,1:T(8,128)(2,1)S(1)} %collective-permute-done.9), channel_id=1, source_target_pairs={{0,224},{1,225},{2,226},{3,227},{4,228},{5,229},{6,230},{7,231},{8... | collective-permute-start | bytes 589832 | tf_op jit(solution)/shard_map/ppermute | solution.py:27
  40.2 1.6 %collective-permute-start.3 = (bf16[2,768,128]{1,2,0:T(8,128)(2,1)S(1)}, bf16[2,768,128]{1,2,0:T(8,128)(2,1)S(1)}, u32[]{:S(2)}, u32[]{:S(2)}) collective-permute-start(bf16[2,768,128]{1,2,0:T(8,128)(2,1)S(1)} %collective-permute-done.2), channel_id=1, source_target_pairs={{0,4},{1,5},{2,6},{3,7},{4,8},{5,9},{6,10},{7,11},{8,12},{9,13},{1... | collective-permute-start | bytes 1179656 | tf_op jit(solution)/shard_map/ppermute | solution.py:27
  41.8 2.7 %collective-permute-done.10 = bf16[768,128]{0,1:T(8,128)(2,1)S(1)} collective-permute-done((bf16[768,128]{0,1:T(8,128)(2,1)S(1)}, bf16[768,128]{0,1:T(8,128)(2,1)S(1)}, u32[]{:S(2)}, u32[]{:S(2)}) %collective-permute-start.10) | collective-permute-done | bytes 196640 | tf_op jit(solution)/shard_map/ppermute | solution.py:27
  44.5 1.7 %collective-permute-start.12 = (bf16[384,128]{0,1:T(8,128)(2,1)S(1)}, bf16[384,128]{0,1:T(8,128)(2,1)S(1)}, u32[]{:S(2)}, u32[]{:S(2)}) collective-permute-start(bf16[384,128]{0,1:T(8,128)(2,1)S(1)} %slice.18), channel_id=1, source_target_pairs={{0,32},{1,33},{2,34},{3,35},{4,36},{5,37},{6,38},{7,39},{8,40},{9,... | collective-permute-start | bytes 294920 | tf_op jit(solution)/shard_map/ppermute | solution.py:27
  46.1 2.0 %collective-permute-start.13 = (bf16[384,128]{0,1:T(8,128)(2,1)S(1)}, bf16[384,128]{0,1:T(8,128)(2,1)S(1)}, u32[]{:S(2)}, u32[]{:S(2)}) collective-permute-start(bf16[384,128]{0,1:T(8,128)(2,1)S(1)} %slice.19), channel_id=1, source_target_pairs={{0,224},{1,225},{2,226},{3,227},{4,228},{5,229},{6,230},{7,231},{8... | collective-permute-start | bytes 294920 | tf_op jit(solution)/shard_map/ppermute | solution.py:27
  48.1 2.5 %collective-permute-done.12 = bf16[384,128]{0,1:T(8,128)(2,1)S(1)} collective-permute-done((bf16[384,128]{0,1:T(8,128)(2,1)S(1)}, bf16[384,128]{0,1:T(8,128)(2,1)S(1)}, u32[]{:S(2)}, u32[]{:S(2)}) %collective-permute-start.12) | collective-permute-done | bytes 98336 | tf_op jit(solution)/shard_map/ppermute | solution.py:27
  51.9 4.7 %collective-permute-start.4 = (bf16[2,768,128]{1,2,0:T(8,128)(2,1)S(1)}, bf16[2,768,128]{1,2,0:T(8,128)(2,1)S(1)}, u32[]{:S(2)}, u32[]{:S(2)}) collective-permute-start(bf16[2,768,128]{1,2,0:T(8,128)(2,1)S(1)} %collective-permute-done.3), channel_id=1, source_target_pairs={{0,4},{1,5},{2,6},{3,7},{4,8},{5,9},{6,10},{7,11},{8,12},{9,13},{1... | collective-permute-start | bytes 1179656 | tf_op jit(solution)/shard_map/ppermute | solution.py:27
  56.6 2.1 %fusion.5 = f32[4,128,768]{2,1,0:T(8,128)S(1)} fusion(bf16[768,768]{1,0:T(8,128)(2,1)} %collective-permute-done.15, bf16[1,768,128]{1,2,0:T(8,128)(2,1)S(1)} %get-tuple-element.26, bf16[1,768,128]{1,2,0:T(8,128)(2,1)S(1)} %get-tuple-element.27, bf16[1,768,128]{1,2,0:T(8,128)(2,1)S(1)} %get-tuple-element.28, bf16[1,768,128]{1,2,0:T(8,128)(2,1)S(1)} %get-tuple-element.29), kind=kOutput, calls=%fused_computation.10 | convolution fusion | flops 605159424 | bytes 3538944 | tf_op jit(solution)/shard_map/rc,ycj->yrj/dot_general | solution.py:158
  59.6 5.6 %collective-permute-done.4 = bf16[2,768,128]{1,2,0:T(8,128)(2,1)S(1)} collective-permute-done((bf16[2,768,128]{1,2,0:T(8,128)(2,1)S(1)}, bf16[2,768,128]{1,2,0:T(8,128)(2,1)S(1)}, u32[]{:S(2)}, u32[]{:S(2)}) %collective-permute-start.4) | collective-permute-done | bytes 393248 | tf_op jit(solution)/shard_map/ppermute | solution.py:27
  65.2 1.4 %pad_maximum_fusion = bf16[8,768,128]{1,2,0:T(8,128)(2,1)} fusion(bf16[2,768,128]{1,2,0:T(8,128)(2,1)S(1)} %collective-permute-done.4, bf16[2,768,128]{1,2,0:T(8,128)(2,1)S(1)} %collective-permute-done.3, bf16[2,768,128]{1,2,0:T(8,128)(2,1)S(1)} %collective-permute-done.2, bf16[2,768,128]{1,2,0:T(8,128)(2,1)S(1)} %pad_maximum_fusion.4), kind=kLoop, calls=%fused_computation.1 | loop fusion | flops 2359296 | bytes 3145728 | tf_op jit(solution)/shard_map/concatenate | solution.py:105
  69.6 5.5 %all-to-all-start = ((bf16[8,768,128]{1,2,0:T(8,128)(2,1)}), bf16[8,768,128]{1,2,0:T(8,128)(2,1)S(1)}, u32[]{:S(2)}, u32[]{:S(2)}) async-start(bf16[8,768,128]{1,2,0:T(8,128)(2,1)} %pad_maximum_fusion.1), calls=%async_computation | async-start | bytes 3145728 | tf_op jit(solution)/shard_map/all_to_all | solution.py:166
  76.0 1.8 %constant_dynamic-update-slice_fusion.3 = bf16[16,768,128]{1,2,0:T(8,128)(2,1)} fusion(bf16[16,768,128]{1,2,0:T(8,128)(2,1)} %constant_dynamic-update-slice_fusion.4, bf16[2,768,128]{1,2,0:T(8,128)(2,1)} %copy-done), kind=kLoop, calls=%fused_computation.41 | loop fusion | bytes 786432
  80.6 14.7 %all-to-all-done = bf16[8,768,128]{1,2,0:T(8,128)(2,1)S(1)} async-done(((bf16[8,768,128]{1,2,0:T(8,128)(2,1)}), bf16[8,768,128]{1,2,0:T(8,128)(2,1)S(1)}, u32[]{:S(2)}, u32[]{:S(2)}) %all-to-all-start) | async-done | bytes 1572896 | tf_op jit(solution)/shard_map/all_to_all | solution.py:166
  95.7 2.9 %fusion.10 = f32[16,128,256]{2,1,0:T(8,128)S(1)} fusion(bf16[16,768,128]{1,2,0:T(8,128)(2,1)} %constant_dynamic-update-slice_fusion, bf16[768,128]{1,0:T(8,128)(2,1)S(1)} %get-tuple-element.34, bf16[768,128]{1,0:T(8,128)(2,1)S(1)} %get-tuple-element.33), kind=kOutput, calls=%fused_computation.25 | convolution fusion | flops 806092800 | bytes 5636096 | tf_op jit(solution)/shard_map/dot_general | solution.py:98
  100.4 24.7 %all_to_all.10 = f16[16,144,128]{2,1,0:T(8,128)(2,1)S(1)} all-to-all(f16[16,144,128]{2,1,0:T(8,128)(2,1)S(1)} %concatenate.25), channel_id=1, replica_groups={{0,32,192,224,128,160,64,96,16,48,208,240,144,176,80,112},{17,49,209,24..., dimensions={0} | all-to-all | bytes 1179648 | tf_op jit(solution)/shard_map/all_to_all | solution.py:172
  (71 shorter events, 22.6 us)
Async XLA Ops:
  2.5 13.0 %collective-permute-start.1 = (bf16[768,128]{0,1:T(8,128)(2,1)}, bf16[768,128]{0,1:T(8,128)(2,1)}, u32[]{:S(2)}, u32[]{:S(2)}) collective-permute-start(bf16[768,128]{0,1:T(8,128)(2,1)} %broadcast_multiply_fusion), channel_id=1, source_target_pairs={{0,2},{1,3},{2,0},{3,1},{4,6},{5,7},{6,4},{7,5},{8,10},{9,11},{10,... | collective-permute-start | bytes 589832 | tf_op jit(solution)/shard_map/ppermute | solution.py:27
  4.6 12.0 %collective-permute-start = (bf16[768,128]{0,1:T(8,128)(2,1)}, bf16[768,128]{0,1:T(8,128)(2,1)}, u32[]{:S(2)}, u32[]{:S(2)}) collective-permute-start(bf16[768,128]{0,1:T(8,128)(2,1)} %broadcast_multiply_fusion), channel_id=1, source_target_pairs={{0,0},{1,1},{2,2},{3,3},{4,224},{5,225},{6,226},{7,227},{8,192},{9... | collective-permute-start | bytes 589832 | tf_op jit(solution)/shard_map/ppermute | solution.py:27
  11.1 40.0 %collective-permute-start.15 = (bf16[768,768]{1,0:T(8,128)(2,1)}, bf16[768,768]{1,0:T(8,128)(2,1)}, u32[]{:S(2)}, u32[]{:S(2)}) collective-permute-start(bf16[768,768]{1,0:T(8,128)(2,1)} %mul.33), channel_id=1, source_target_pairs={{0,2},{1,18},{2,0},{3,16},{4,6},{5,22},{6,4},{7,20},{8,10},{9,26},... | collective-permute-start | bytes 3538952 | tf_op jit(solution)/shard_map/ppermute | solution.py:27
  11.1 40.1 %collective-permute-start.14 = (bf16[768,768]{1,0:T(8,128)(2,1)}, bf16[768,768]{1,0:T(8,128)(2,1)S(1)}, u32[]{:S(2)}, u32[]{:S(2)}) collective-permute-start(bf16[768,768]{1,0:T(8,128)(2,1)} %mul.33), channel_id=1, source_target_pairs={{0,0},{1,16},{2,2},{3,18},{4,4},{5,20},{6,6},{7,22},{8,8},{9,24},{... | collective-permute-start | bytes 3538952 | tf_op jit(solution)/shard_map/ppermute | solution.py:27
  16.6 10.5 %collective-permute-start.6 = (bf16[768,128]{0,1:T(8,128)(2,1)}, bf16[768,128]{0,1:T(8,128)(2,1)S(1)}, u32[]{:S(2)}, u32[]{:S(2)}) collective-permute-start(bf16[768,128]{0,1:T(8,128)(2,1)} %collective-permute-done), channel_id=1, source_target_pairs={{0,32},{1,33},{2,34},{3,35},{4,36},{5,37},{6,38},{7,39},{8,40},{9,... | collective-permute-start | bytes 589832 | tf_op jit(solution)/shard_map/ppermute | solution.py:27
  18.6 10.7 %collective-permute-start.7 = (bf16[768,128]{0,1:T(8,128)(2,1)}, bf16[768,128]{0,1:T(8,128)(2,1)S(1)}, u32[]{:S(2)}, u32[]{:S(2)}) collective-permute-start(bf16[768,128]{0,1:T(8,128)(2,1)} %collective-permute-done), channel_id=1, source_target_pairs={{0,224},{1,225},{2,226},{3,227},{4,228},{5,229},{6,230},{7,231},{8... | collective-permute-start | bytes 589832 | tf_op jit(solution)/shard_map/ppermute | solution.py:27
  21.6 18.6 %collective-permute-start.2 = (bf16[2,768,128]{1,2,0:T(8,128)(2,1)S(1)}, bf16[2,768,128]{1,2,0:T(8,128)(2,1)S(1)}, u32[]{:S(2)}, u32[]{:S(2)}) collective-permute-start(bf16[2,768,128]{1,2,0:T(8,128)(2,1)S(1)} %pad_maximum_fusion.4), channel_id=1, source_target_pairs={{0,4},{1,5},{2,6},{3,7},{4,8},{5,9},{6,10},{7,11},{8,12},{9,13},{1... | collective-permute-start | bytes 1179656 | tf_op jit(solution)/shard_map/ppermute | solution.py:27
  29.3 6.9 %collective-permute-start.8 = (bf16[768,128]{0,1:T(8,128)(2,1)S(1)}, bf16[768,128]{0,1:T(8,128)(2,1)S(1)}, u32[]{:S(2)}, u32[]{:S(2)}) collective-permute-start(bf16[768,128]{0,1:T(8,128)(2,1)S(1)} %collective-permute-done.6), channel_id=1, source_target_pairs={{0,32},{1,33},{2,34},{3,35},{4,36},{5,37},{6,38},{7,39},{8,40},{9,... | collective-permute-start | bytes 589832 | tf_op jit(solution)/shard_map/ppermute | solution.py:27
  31.3 5.7 %collective-permute-start.9 = (bf16[768,128]{0,1:T(8,128)(2,1)S(1)}, bf16[768,128]{0,1:T(8,128)(2,1)S(1)}, u32[]{:S(2)}, u32[]{:S(2)}) collective-permute-start(bf16[768,128]{0,1:T(8,128)(2,1)S(1)} %collective-permute-done.7), channel_id=1, source_target_pairs={{0,224},{1,225},{2,226},{3,227},{4,228},{5,229},{6,230},{7,231},{8... | collective-permute-start | bytes 589832 | tf_op jit(solution)/shard_map/ppermute | solution.py:27
  37.0 7.5 %collective-permute-start.10 = (bf16[768,128]{0,1:T(8,128)(2,1)S(1)}, bf16[768,128]{0,1:T(8,128)(2,1)S(1)}, u32[]{:S(2)}, u32[]{:S(2)}) collective-permute-start(bf16[768,128]{0,1:T(8,128)(2,1)S(1)} %collective-permute-done.8), channel_id=1, source_target_pairs={{0,32},{1,33},{2,34},{3,35},{4,36},{5,37},{6,38},{7,39},{8,40},{9,... | collective-permute-start | bytes 589832 | tf_op jit(solution)/shard_map/ppermute | solution.py:27
  38.4 6.1 %collective-permute-start.11 = (bf16[768,128]{0,1:T(8,128)(2,1)S(1)}, bf16[768,128]{0,1:T(8,128)(2,1)S(1)}, u32[]{:S(2)}, u32[]{:S(2)}) collective-permute-start(bf16[768,128]{0,1:T(8,128)(2,1)S(1)} %collective-permute-done.9), channel_id=1, source_target_pairs={{0,224},{1,225},{2,226},{3,227},{4,228},{5,229},{6,230},{7,231},{8... | collective-permute-start | bytes 589832 | tf_op jit(solution)/shard_map/ppermute | solution.py:27
  40.2 25.0 %copy-start = (bf16[2,768,128]{1,2,0:T(8,128)(2,1)}, bf16[2,768,128]{1,2,0:T(8,128)(2,1)S(1)}, u32[]{:S(2)}) copy-start(bf16[2,768,128]{1,2,0:T(8,128)(2,1)S(1)} %collective-permute-done.2) | copy-start | bytes 1179652
  40.2 11.7 %collective-permute-start.3 = (bf16[2,768,128]{1,2,0:T(8,128)(2,1)S(1)}, bf16[2,768,128]{1,2,0:T(8,128)(2,1)S(1)}, u32[]{:S(2)}, u32[]{:S(2)}) collective-permute-start(bf16[2,768,128]{1,2,0:T(8,128)(2,1)S(1)} %collective-permute-done.2), channel_id=1, source_target_pairs={{0,4},{1,5},{2,6},{3,7},{4,8},{5,9},{6,10},{7,11},{8,12},{9,13},{1... | collective-permute-start | bytes 1179656 | tf_op jit(solution)/shard_map/ppermute | solution.py:27
  44.5 6.1 %collective-permute-start.12 = (bf16[384,128]{0,1:T(8,128)(2,1)S(1)}, bf16[384,128]{0,1:T(8,128)(2,1)S(1)}, u32[]{:S(2)}, u32[]{:S(2)}) collective-permute-start(bf16[384,128]{0,1:T(8,128)(2,1)S(1)} %slice.18), channel_id=1, source_target_pairs={{0,32},{1,33},{2,34},{3,35},{4,36},{5,37},{6,38},{7,39},{8,40},{9,... | collective-permute-start | bytes 294920 | tf_op jit(solution)/shard_map/ppermute | solution.py:27
  46.1 4.9 %collective-permute-start.13 = (bf16[384,128]{0,1:T(8,128)(2,1)S(1)}, bf16[384,128]{0,1:T(8,128)(2,1)S(1)}, u32[]{:S(2)}, u32[]{:S(2)}) collective-permute-start(bf16[384,128]{0,1:T(8,128)(2,1)S(1)} %slice.19), channel_id=1, source_target_pairs={{0,224},{1,225},{2,226},{3,227},{4,228},{5,229},{6,230},{7,231},{8... | collective-permute-start | bytes 294920 | tf_op jit(solution)/shard_map/ppermute | solution.py:27
  51.1 15.6 %collective-permute-start.17 = (bf16[768,768]{1,0:T(8,128)(2,1)}, bf16[768,768]{1,0:T(8,128)(2,1)S(1)}, u32[]{:S(2)}, u32[]{:S(2)}) collective-permute-start(bf16[768,768]{1,0:T(8,128)(2,1)} %collective-permute-done.15), channel_id=1, source_target_pairs={{0,1},{1,0},{2,3},{3,2},{4,5},{5,4},{6,7},{7,6},{8,9},{9,8},{10,11... | collective-permute-start | bytes 3538952 | tf_op jit(solution)/shard_map/ppermute | solution.py:27
  51.2 16.3 %collective-permute-start.16 = (bf16[768,768]{1,0:T(8,128)(2,1)S(1)}, bf16[768,768]{1,0:T(8,128)(2,1)S(1)}, u32[]{:S(2)}, u32[]{:S(2)}) collective-permute-start(bf16[768,768]{1,0:T(8,128)(2,1)S(1)} %collective-permute-done.14), channel_id=1, source_target_pairs={{0,1},{1,0},{2,3},{3,2},{4,5},{5,4},{6,7},{7,6},{8,9},{9,8},{10,11... | collective-permute-start | bytes 3538952 | tf_op jit(solution)/shard_map/ppermute | solution.py:27
  51.9 13.3 %copy-start.1 = (bf16[2,768,128]{1,2,0:T(8,128)(2,1)}, bf16[2,768,128]{1,2,0:T(8,128)(2,1)S(1)}, u32[]{:S(2)}) copy-start(bf16[2,768,128]{1,2,0:T(8,128)(2,1)S(1)} %collective-permute-done.3) | copy-start | bytes 1179652
  51.9 13.3 %collective-permute-start.4 = (bf16[2,768,128]{1,2,0:T(8,128)(2,1)S(1)}, bf16[2,768,128]{1,2,0:T(8,128)(2,1)S(1)}, u32[]{:S(2)}, u32[]{:S(2)}) collective-permute-start(bf16[2,768,128]{1,2,0:T(8,128)(2,1)S(1)} %collective-permute-done.3), channel_id=1, source_target_pairs={{0,4},{1,5},{2,6},{3,7},{4,8},{5,9},{6,10},{7,11},{8,12},{9,13},{1... | collective-permute-start | bytes 1179656 | tf_op jit(solution)/shard_map/ppermute | solution.py:27
  65.2 2.2 %copy-start.3 = (bf16[2,768,128]{1,2,0:T(8,128)(2,1)}, bf16[2,768,128]{1,2,0:T(8,128)(2,1)S(1)}, u32[]{:S(2)}) copy-start(bf16[2,768,128]{1,2,0:T(8,128)(2,1)S(1)} %collective-permute-done.4) | copy-start | bytes 1179652
  66.6 12.7 %collective-permute-start.5 = (bf16[8,768,128]{1,2,0:T(8,128)(2,1)}, bf16[8,768,128]{1,2,0:T(8,128)(2,1)S(1)}, u32[]{:S(2)}, u32[]{:S(2)}) collective-permute-start(bf16[8,768,128]{1,2,0:T(8,128)(2,1)} %pad_maximum_fusion), channel_id=1, source_target_pairs={{0,1},{1,0},{2,3},{3,2},{4,5},{5,4},{6,7},{7,6},{8,9},{9,8},{10,11... | collective-permute-start | bytes 4718600 | tf_op jit(solution)/shard_map/ppermute | solution.py:27
  69.6 25.7 %all-to-all-start = ((bf16[8,768,128]{1,2,0:T(8,128)(2,1)}), bf16[8,768,128]{1,2,0:T(8,128)(2,1)S(1)}, u32[]{:S(2)}, u32[]{:S(2)}) async-start(bf16[8,768,128]{1,2,0:T(8,128)(2,1)} %pad_maximum_fusion.1), calls=%async_computation | async-start | bytes 3145728 | tf_op jit(solution)/shard_map/all_to_all | solution.py:166
  75.2 2.6 %copy-start.2 = (bf16[2,768,128]{1,2,0:T(8,128)(2,1)S(1)}, bf16[2,768,128]{1,2,0:T(8,128)(2,1)}, u32[]{:S(2)}) copy-start(bf16[2,768,128]{1,2,0:T(8,128)(2,1)} %copy-done.1) | copy-start | bytes 1179652
  75.2 3.4 %copy-start.4 = (bf16[2,768,128]{1,2,0:T(8,128)(2,1)S(1)}, bf16[2,768,128]{1,2,0:T(8,128)(2,1)}, u32[]{:S(2)}) copy-start(bf16[2,768,128]{1,2,0:T(8,128)(2,1)} %copy-done.3) | copy-start | bytes 1179652
  (1 other events, 1.3 us)

commit v2 on v1

v2 whole, which is shorter than its diff:
```python
import functools

import jax
import jax.numpy as jnp
from jax import lax
from jax.experimental import pallas as pl
from jax.experimental.pallas import tpu as pltpu
from jax.sharding import PartitionSpec as P

BLOCK = 128
AXES = ("row", "col")
PLANES, LANES = 8, 4


def place(z, xl, y, xh, k):
    return (2 * (z % PLANES) + xl) * 16 + 4 * (y % LANES) + 2 * xh + k


SPOTS = [
    (z, xl, y, xh, k)
    for z in range(PLANES)
    for xl in range(2)
    for y in range(LANES)
    for xh in range(2)
    for k in range(2)
]


def send(value, target):
    pairs = [(place(*spot), place(*target(*spot))) for spot in SPOTS]
    return lax.ppermute(value, AXES, pairs)


def turn(z, xl, y, xh, k):
    shift = (y - z // 2) % LANES
    return (z + shift if z % 2 else z - shift), xl, z // 2, xh, k


def z_up(z, xl, y, xh, k):
    return z + 1, xl, y, xh, k


def z_down(z, xl, y, xh, k):
    return z - 1, xl, y, xh, k


def y_up(z, xl, y, xh, k):
    return z, xl, y + 1, xh, k


def y_down(z, xl, y, xh, k):
    return z, xl, y - 1, xh, k


def far_x(z, xl, y, xh, k):
    return z, xl, y, 1 - xh, k


def other_core(z, xl, y, xh, k):
    return z, xl, y, xh, 1 - k


def swap(z, xl, y, xh, k):
    return z, k, y, xh, xl


def swap_far(z, xl, y, xh, k):
    return z, k, y, 1 - xh, xl


W_GROUPS = [
    [place(z, s ^ k, y, xh, k) for s in range(2) for y in range(LANES)]
    for z in range(PLANES)
    for xh in range(2)
    for k in range(2)
]


def coarse_row(y, xh, k, dk, dy, dx):
    i = 4 * ((y - dy) % LANES) + 2 * (xh ^ dx) + (k ^ dk)
    return i // 2, i % 2


C_GROUPS = [
    [
        place(*coarse_row(y, xh, k, dk, dy, dx), y, xh, k)
        for dk in range(2)
        for dy in range(LANES)
        for dx in range(2)
    ]
    for y in range(LANES)
    for xh in range(2)
    for k in range(2)
]


VMEM = pl.BlockSpec(memory_space=pltpu.VMEM)
SMEM = pl.BlockSpec(memory_space=pltpu.SMEM)


def on_device(kernel, shape, dtype, specs, scratch=(), cost=None, grant=1):
    return pl.pallas_call(
        kernel,
        out_shape=jax.ShapeDtypeStruct(shape, dtype),
        in_specs=specs,
        out_specs=VMEM,
        scratch_shapes=scratch,
        compiler_params=pltpu.CompilerParams(vmem_limit_bytes=grant << 20),
        cost_estimate=cost,
    )


def dot32(a, b):
    return jnp.dot(a, b, preferred_element_type=jnp.float32)


def masked(value, pattern):
    wide = jnp.repeat(jnp.repeat(pattern, BLOCK, axis=0), BLOCK, axis=1)
    return value * wide.astype(value.dtype)


def mask_kernel(pattern_ref, value_ref, out_ref):
    for i in range(pattern_ref.shape[0]):
        for j in range(pattern_ref.shape[1]):
            spot = (slice(i * BLOCK, (i + 1) * BLOCK), slice(j * BLOCK, (j + 1) * BLOCK))
            value = value_ref[spot]
            out_ref[spot] = jnp.where(pattern_ref[i, j] != 0, value, jnp.zeros_like(value))


def masked_tile(value, pattern):
    cost = pl.CostEstimate(flops=value.size, bytes_accessed=4 * value.size, transcendentals=0)
    return on_device(mask_kernel, value.shape, value.dtype, [SMEM, VMEM], cost=cost)(pattern, value)


def pair_kernel(one, two, out_ref):
    out_ref[0] = one[...]
    out_ref[1] = two[...]


def paired(one, two):
    cost = pl.CostEstimate(flops=0, bytes_accessed=8 * one.size, transcendentals=0)
    return on_device(pair_kernel, (2, *one.shape), one.dtype, [VMEM] * 2, cost=cost)(one, two)


def line_up_kernel(spot_ref, *refs):
    blocks, p_ref = refs[:9], refs[9]
    z, y, xh = spot_ref[0], spot_ref[1], spot_ref[2]
    half = blocks[4].shape[0]
    for d in range(PLANES):
        place_in = lax.rem(z + d - 2 * y - 1 + 2 * PLANES, PLANES)
        odd = (place_in < LANES).astype(jnp.int32)
        shift = jnp.where(odd == 1, place_in, PLANES - 1 - place_in)
        side = lax.rem(odd + xh, 2)
        column = pl.multiple_of(lax.rem(y + shift, LANES) * BLOCK, BLOCK)
        if d < 4:
            p_ref[side, :, pl.ds(column, BLOCK)] = blocks[d][...]
        elif d == 4:
            p_ref[side, :half, pl.ds(column, BLOCK)] = blocks[4][...]
            p_ref[side, half:, pl.ds(column, BLOCK)] = blocks[5][...]
        else:
            p_ref[side, :, pl.ds(column, BLOCK)] = blocks[d + 1][...]


def line_up(spot, blocks):
    size = blocks[0].shape[0]
    return on_device(
        line_up_kernel, (2, size, LANES * BLOCK), jnp.bfloat16, [SMEM] + [VMEM] * len(blocks),
        cost=pl.CostEstimate(flops=0, bytes_accessed=4 << 20, transcendentals=0),
    )(spot, *blocks)


def w_kernel(base, p_ref, one, two, *rest):
    out_ref = rest[-1]
    if base:
        out_ref[:base] = rest[0][...]
    size = one.shape[0]
    step = size // 3
    for c in range(0, LANES, 2):
        columns = slice(c * BLOCK, (c + 2) * BLOCK)
        for start in range(0, size, step):
            rows = slice(start, start + step)
            total = dot32(one[rows], p_ref[0, :, columns]) + dot32(two[rows], p_ref[1, :, columns])
            total = total.astype(jnp.bfloat16)
            out_ref[base + c, rows] = total[:, :BLOCK]
            out_ref[base + c + 1, rows] = total[:, BLOCK:]


def w_products(p_all, one, two, *before):
    size = one.shape[0]
    return on_device(
        functools.partial(w_kernel, LANES * len(before)),
        (LANES * (1 + len(before)), size, BLOCK),
        jnp.bfloat16,
        [VMEM] * (3 + len(before)),
        cost=pl.CostEstimate(flops=4 * size * size * LANES * BLOCK, bytes_accessed=6 << 20, transcendentals=0),
        grant=6,
    )(p_all, one, two, *before)


def c_kernel(parts_ref, *refs):
    pairs, (out_ref, w_ref) = refs[: 2 * LANES], refs[2 * LANES :]
    w = parts_ref[0].astype(jnp.float32)
    for i in range(1, parts_ref.shape[0]):
        w += parts_ref[i].astype(jnp.float32)
    turned = w.T
    high = turned.astype(jnp.bfloat16)
    w_ref[:BLOCK] = high
    w_ref[BLOCK:] = (turned - high.astype(jnp.float32)).astype(jnp.bfloat16)
    units = [pair.at[i] for pair in pairs for i in range(2)]
    top = jnp.zeros((BLOCK, BLOCK), jnp.float32)
    for i, unit in enumerate(units):
        both = dot32(w_ref[...], unit[...])
        part = both[:BLOCK] + both[BLOCK:]
        out_ref[i, :BLOCK] = part
        top = jnp.maximum(top, jnp.abs(part))
    top = jnp.max(jnp.max(top, axis=0, keepdims=True), axis=1, keepdims=True)
    power = jnp.ceil(jnp.log2(jnp.maximum(top, 1e-30))) - 14.0
    scale = jnp.exp2(-power)
    for i in range(len(units)):
        out_ref[i, :BLOCK] = out_ref[i, :BLOCK] * scale
        out_ref[i, BLOCK:] = jnp.broadcast_to(power, (8, BLOCK))


def c_products(parts, pairs):
    size = parts.shape[1]
    return on_device(
        c_kernel,
        (4 * LANES, BLOCK + 8, BLOCK),
        jnp.float32,
        [VMEM] * (2 * LANES + 1),
        [pltpu.VMEM((2 * BLOCK, size), jnp.bfloat16)],
        pl.CostEstimate(flops=16 * LANES * size * BLOCK * BLOCK, bytes_accessed=6 << 20, transcendentals=0),
        grant=8,
    )(parts, *pairs)


def unpack(parts):
    parts = parts.astype(jnp.float32)
    return jnp.sum(parts[:, :BLOCK] * jnp.exp2(parts[:, BLOCK : BLOCK + 1, :1]), axis=0).T


def both(*values):
    return lax.optimization_barrier(values)


def local(a_matrix, prolong, a_pattern, p_pattern):
    row, col = lax.axis_index("row"), lax.axis_index("col")
    spot = jnp.stack([row // 2, col // 4, (col // 2) % 2]).astype(jnp.int32)
    p_eff = masked(prolong, p_pattern)
    p_eff, a_matrix = both(p_eff, a_matrix)
    first, across = send(p_eff, turn), send(p_eff, far_x)
    a_eff = masked_tile(a_matrix, a_pattern)
    near, distant = send(a_eff, swap), send(a_eff, swap_far)
    first, p_eff, across, spot, _ = both(first, p_eff, across, spot, a_eff)
    pair = paired(p_eff, across)
    up_1, down_1 = both(send(first, z_up), send(first, z_down))
    below = send(pair, y_up)
    up_2, down_2 = both(send(up_1, z_up), send(down_1, z_down))
    up_2, down_2, below = both(up_2, down_2, below)
    beyond = send(below, y_up)
    up_3, down_3 = both(send(up_2, z_up), send(down_2, z_down))
    up_3, down_3, beyond = both(up_3, down_3, beyond)
    half = first.shape[0] // 2
    far = [send(up_3[:half], z_up), send(down_3[half:], z_down)]
    above = send(beyond, y_up)
    *far, near, distant, above = both(*far, near, distant, above)
    p_all = line_up(spot, [first, down_1, down_2, down_3, *far, up_3, up_2, up_1])
    near_2, distant_2 = send(near, other_core), send(distant, other_core)
    w_part = w_products(p_all, near, distant)
    w_part = w_products(p_all, near_2, distant_2, w_part)
    w_part, *pairs = both(w_part, pair, below, beyond, above)
    pairs += [send(p, other_core) for p in pairs]
    w_parts = lax.all_to_all(w_part, AXES, 0, 0, axis_index_groups=W_GROUPS, tiled=True)
    c_part = c_products(w_parts, pairs).astype(jnp.float16)
    return unpack(lax.all_to_all(c_part, AXES, 0, 0, axis_index_groups=C_GROUPS, tiled=True))


def solution(mesh):
    placed = (P("row", "col"),) * 4
    return jax.shard_map(
        local, mesh=mesh, in_specs=placed, out_specs=P("row", "col"), check_vma=False
    )
```

time: 127 us -> 124 us (0.976)
  Pallas kernels: 0 us -> 7.79 us
  matrix products: 7.45 us -> 0 us
  other arithmetic: 9.31 us -> 2.32 us
  waiting for transfers between devices: 32.5 us -> 36.9 us
  starting transfers between devices: 41.4 us -> 45.4 us
  blocking collectives: 24.7 us -> 22.4 us
  local copies, waits for them, and re-layouts: 9.42 us -> 8.04 us
    pallas_call x0 -> x6, Pallas kernels: none -> 7.79 us  [the longest x2 3.93 us: w_products(): on_device(functools.partial(w_kernel, LANES * len(before)), (LANES * (1 +...]
    dot_general x5 -> x0, matrix products: 7.45 us -> none  [the longest x4 4.58 us: product(): return jnp.einsum('rc,ycj->yrj', a, p, preferred_element_type=jnp.float32)]
    ppermute x18 -> x21, waiting for transfers between devices: 17.8 us -> 21.8 us  [send(): return lax.ppermute(value, AXES, pairs)]
    ppermute x18 -> x21, starting transfers between devices: 35.9 us -> 39 us  [send(): return lax.ppermute(value, AXES, pairs)]
    concatenate x2 -> x0, other arithmetic: 2.69 us -> none  [the longest x1 1.4 us: column_rows(): own = jnp.concatenate(pairs)]
    all_to_all x1, blocking collectives: 24.7 us -> 22.4 us  [local(): lax.all_to_all(c_part, AXES, 0, 0, axis_index_groups=C_GROUPS, tiled=True)]
    concatenate x2 -> x0, local copies, waits for them, and re-layouts: 1.38 us -> none  [the longest x1 1.26 us: column_rows(): return jnp.concatenate([own, send(own, other_core)])]
    unnamed x25 -> x16, local copies, waits for them, and re-layouts: 6.83 us -> 7.23 us
  transfers between devices with their start and end apart: 19 -> 22, of which waited for: 8 -> 13; matrix products, arithmetic and copies ran while one was open for 14% -> 0% of each run, Pallas kernels for 0% -> 3%
where the time goes in v2:
time: 124 us; the launch traced here: 123 us
  starting transfers between devices  45.4 us (37%)
  waiting for transfers between devices  36.9 us (30%)
  blocking collectives  22.4 us (18%)
  local copies, waits for them, and re-layouts  8.04 us (6%)
  Pallas kernels  7.79 us (6%)
  other arithmetic  2.32 us (2%)
    ppermute x21, starting transfers between devices, send(): return lax.ppermute(value, AXES, pairs)  39 us
    all_to_all x1, blocking collectives, local(): lax.all_to_all(c_part, AXES, 0, 0, axis_index_groups=C_GROUPS, tiled=True)  22.4 us
    ppermute x21, waiting for transfers between devices, send(): return lax.ppermute(value, AXES, pairs)  21.8 us
    all_to_all x1, waiting for transfers between devices, local(): lax.all_to_all(w_part, AXES, 0, 0, axis_index_groups=W_GROUPS, tiled=True)  15.1 us
    unnamed x16, local copies, waits for them, and re-layouts  7.23 us
    all_to_all x1, starting transfers between devices, local(): lax.all_to_all(w_part, AXES, 0, 0, axis_index_groups=W_GROUPS, tiled=True)  6.33 us
    pallas_call x2, Pallas kernels, w_products(): on_device(functools.partial(w_kernel, LANES * len(before)), (LANES * (1 +...  3.93 us
  transfers between devices with their start and end apart: 22, of which 13 were waited for; matrix products, arithmetic and copies ran while one was open for 0% of the time, Pallas kernels for 3%

profile of v2, /device:TPU:2, one launch (start us, length us, event | category | flops | bytes accessed | tf_op | source)
XLA Modules:
  0.0 123.0 jit_solution(1804226301277700733)
XLA Ops:
  0.7 1.1 broadcast_multiply_fusion.one
  1.8 2.2 %collective-permute-start.1 = (bf16[768,128]{1,0:T(8,128)(2,1)S(1)}, bf16[768,128]{1,0:T(8,128)(2,1)S(1)}, u32[]{:S(2)}, u32[]{:S(2)}) collective-permute-start(bf16[768,128]{1,0:T(8,128)(2,1)S(1)} %broadcast_multiply_fusion.one), channel_id=1, source_target_pairs={{0,2},{1,3},{2,0},{3,1},{4,6},{5,7},{6,4},{7,5},{8,10},{9,11},{10,... | collective-permute-start | bytes 589832 | tf_op jit(solution)/shard_map/ppermute | solution.py:31
  4.8 1.3 %copy-done = bf16[768,768]{1,0:T(8,128)(2,1)S(1)} copy-done((bf16[768,768]{1,0:T(8,128)(2,1)S(1)}, bf16[768,768]{1,0:T(8,128)(2,1)}, u32[]{:S(2)}) %copy-start) | copy-done | bytes 1179672
  7.7 2.4 %collective-permute-done.1.two = bf16[768,128]{1,0:T(8,128)(2,1)S(1)} collective-permute-done((bf16[768,128]{1,0:T(8,128)(2,1)S(1)}, bf16[768,128]{1,0:T(8,128)(2,1)S(1)}, u32[]{:S(2)}, u32[]{:S(2)}) %collective-permute-start.1) | collective-permute-done | bytes 196640 | tf_op jit(solution)/shard_map/ppermute | solution.py:31
  10.1 10.2 %collective-permute-start.3 = (bf16[768,128]{1,0:T(8,128)(2,1)S(1)}, bf16[768,128]{1,0:T(8,128)(2,1)S(1)}, u32[]{:S(2)}, u32[]{:S(2)}) collective-permute-start(bf16[768,128]{1,0:T(8,128)(2,1)S(1)} %collective-permute-done.refs_0_), channel_id=1, source_target_pairs={{0,224},{1,225},{2,226},{3,227},{4,228},{5,229},{6,230},{7,231},{8... | collective-permute-start | bytes 589832 | tf_op jit(solution)/shard_map/ppermute | solution.py:31
  20.3 4.5 %collective-permute-start.6 = (bf16[2,768,128]{2,1,0:T(8,128)(2,1)S(1)}, bf16[2,768,128]{2,1,0:T(8,128)(2,1)S(1)}, u32[]{:S(2)}, u32[]{:S(2)}) collective-permute-start(bf16[2,768,128]{2,1,0:T(8,128)(2,1)S(1)} %shard_map.47.refs_0_), channel_id=1, source_target_pairs={{0,4},{1,5},{2,6},{3,7},{4,8},{5,9},{6,10},{7,11},{8,12},{9,13},{1... | collective-permute-start | bytes 1179656 | tf_op jit(solution)/shard_map/ppermute | solution.py:31
  24.8 4.2 %collective-permute-start.12 = (bf16[768,768]{1,0:T(8,128)(2,1)S(1)}, bf16[768,768]{1,0:T(8,128)(2,1)S(1)}, u32[]{:S(2)}, u32[]{:S(2)}) collective-permute-start(bf16[768,768]{1,0:T(8,128)(2,1)S(1)} %shard_map.46), channel_id=1, source_target_pairs={{0,0},{1,16},{2,2},{3,18},{4,4},{5,20},{6,6},{7,22},{8,8},{9,24},{... | collective-permute-start | bytes 3538952 | tf_op jit(solution)/shard_map/ppermute | solution.py:31
  29.0 3.3 %collective-permute-start.5 = (bf16[768,128]{1,0:T(8,128)(2,1)S(1)}, bf16[768,128]{1,0:T(8,128)(2,1)S(1)}, u32[]{:S(2)}, u32[]{:S(2)}) collective-permute-start(bf16[768,128]{1,0:T(8,128)(2,1)S(1)} %collective-permute-done.3.refs_1_), channel_id=1, source_target_pairs={{0,224},{1,225},{2,226},{3,227},{4,228},{5,229},{6,230},{7,231},{8... | collective-permute-start | bytes 589832 | tf_op jit(solution)/shard_map/ppermute | solution.py:31
  32.3 3.2 %collective-permute-done.5.refs_2_ = bf16[768,128]{1,0:T(8,128)(2,1)S(1)} collective-permute-done((bf16[768,128]{1,0:T(8,128)(2,1)S(1)}, bf16[768,128]{1,0:T(8,128)(2,1)S(1)}, u32[]{:S(2)}, u32[]{:S(2)}) %collective-permute-start.5) | collective-permute-done | bytes 196640 | tf_op jit(solution)/shard_map/ppermute | solution.py:31
  35.5 3.7 %collective-permute-done.4.refs_7_ = bf16[768,128]{1,0:T(8,128)(2,1)S(1)} collective-permute-done((bf16[768,128]{1,0:T(8,128)(2,1)S(1)}, bf16[768,128]{1,0:T(8,128)(2,1)S(1)}, u32[]{:S(2)}, u32[]{:S(2)}) %collective-permute-start.4) | collective-permute-done | bytes 196640 | tf_op jit(solution)/shard_map/ppermute | solution.py:31
  39.2 4.6 %collective-permute-start.9 = (bf16[2,768,128]{2,1,0:T(8,128)(2,1)S(1)}, bf16[2,768,128]{2,1,0:T(8,128)(2,1)S(1)}, u32[]{:S(2)}, u32[]{:S(2)}) collective-permute-start(bf16[2,768,128]{2,1,0:T(8,128)(2,1)S(1)} %collective-permute-done.6.refs_1_), channel_id=1, source_target_pairs={{0,4},{1,5},{2,6},{3,7},{4,8},{5,9},{6,10},{7,11},{8,12},{9,13},{1... | collective-permute-start | bytes 1179656 | tf_op jit(solution)/shard_map/ppermute | solution.py:31
  43.8 2.0 %collective-permute-start.7 = (bf16[768,128]{1,0:T(8,128)(2,1)S(1)}, bf16[768,128]{1,0:T(8,128)(2,1)S(1)}, u32[]{:S(2)}, u32[]{:S(2)}) collective-permute-start(bf16[768,128]{1,0:T(8,128)(2,1)S(1)} %collective-permute-done.4.refs_7_), channel_id=1, source_target_pairs={{0,32},{1,33},{2,34},{3,35},{4,36},{5,37},{6,38},{7,39},{8,40},{9,... | collective-permute-start | bytes 589832 | tf_op jit(solution)/shard_map/ppermute | solution.py:31
  45.9 4.7 %collective-permute-done.8.refs_3_ = bf16[768,128]{1,0:T(8,128)(2,1)S(1)} collective-permute-done((bf16[768,128]{1,0:T(8,128)(2,1)S(1)}, bf16[768,128]{1,0:T(8,128)(2,1)S(1)}, u32[]{:S(2)}, u32[]{:S(2)}) %collective-permute-start.8) | collective-permute-done | bytes 196640 | tf_op jit(solution)/shard_map/ppermute | solution.py:31
  50.5 1.3 %collective-permute-done.7.refs_6_ = bf16[768,128]{1,0:T(8,128)(2,1)S(1)} collective-permute-done((bf16[768,128]{1,0:T(8,128)(2,1)S(1)}, bf16[768,128]{1,0:T(8,128)(2,1)S(1)}, u32[]{:S(2)}, u32[]{:S(2)}) %collective-permute-start.7) | collective-permute-done | bytes 196640 | tf_op jit(solution)/shard_map/ppermute | solution.py:31
  52.2 2.5 %collective-permute-start.14 = (bf16[2,768,128]{2,1,0:T(8,128)(2,1)S(1)}, bf16[2,768,128]{2,1,0:T(8,128)(2,1)S(1)}, u32[]{:S(2)}, u32[]{:S(2)}) collective-permute-start(bf16[2,768,128]{2,1,0:T(8,128)(2,1)S(1)} %collective-permute-done.9.refs_2_), channel_id=1, source_target_pairs={{0,4},{1,5},{2,6},{3,7},{4,8},{5,9},{6,10},{7,11},{8,12},{9,13},{1... | collective-permute-start | bytes 1179656 | tf_op jit(solution)/shard_map/ppermute | solution.py:31
  54.8 3.2 %collective-permute-start.11 = (bf16[384,128]{1,0:T(8,128)(2,1)S(1)}, bf16[384,128]{1,0:T(8,128)(2,1)S(1)}, u32[]{:S(2)}, u32[]{:S(2)}) collective-permute-start(bf16[384,128]{1,0:T(8,128)(2,1)S(1)} %slice.13), channel_id=1, source_target_pairs={{0,224},{1,225},{2,226},{3,227},{4,228},{5,229},{6,230},{7,231},{8... | collective-permute-start | bytes 294920 | tf_op jit(solution)/shard_map/ppermute | solution.py:31
  58.0 2.6 %collective-permute-done.10.refs_4_ = bf16[384,128]{1,0:T(8,128)(2,1)S(1)} collective-permute-done((bf16[384,128]{1,0:T(8,128)(2,1)S(1)}, bf16[384,128]{1,0:T(8,128)(2,1)S(1)}, u32[]{:S(2)}, u32[]{:S(2)}) %collective-permute-start.10) | collective-permute-done | bytes 98336 | tf_op jit(solution)/shard_map/ppermute | solution.py:31
  62.5 1.4 %shard_map.49.rest_0_ = bf16[4,768,128]{2,1,0:T(8,128)(2,1)S(1)} custom-call(bf16[2,768,512]{2,1,0:T(8,128)(2,1)S(1)} %shard_map.48.p_ref, bf16[768,768]{1,0:T(8,128)(2,1)S(1)} %collective-permute-done.12.one, bf16[768,768]{1,0:T(8,128)(2,1)S(1)} %collective-permute-done.13.two), custom_call_target="tpu_custom_call" | custom-call | flops 1207959552 | bytes 6291456 | tf_op jit(solution)/shard_map/pallas_call | solution.py:190
  64.0 1.7 %collective-permute-done.16.two = bf16[768,768]{1,0:T(8,128)(2,1)S(1)} collective-permute-done((bf16[768,768]{1,0:T(8,128)(2,1)S(1)}, bf16[768,768]{1,0:T(8,128)(2,1)S(1)}, u32[]{:S(2)}, u32[]{:S(2)}) %collective-permute-start.16) | collective-permute-done | bytes 1179680 | tf_op jit(solution)/shard_map/ppermute | solution.py:31
  65.7 2.6 %shard_map.50 = bf16[8,768,128]{2,1,0:T(8,128)(2,1)} custom-call(bf16[2,768,512]{2,1,0:T(8,128)(2,1)S(1)} %shard_map.48.p_ref, bf16[768,768]{1,0:T(8,128)(2,1)S(1)} %collective-permute-done.15.one, bf16[768,768]{1,0:T(8,128)(2,1)S(1)} %collective-permute-done.16.two, bf16[4,768,128]{2,1,0:T(8,128)(2,1)S(1)} %shard_map.49.rest_0_), custom_call_target="tpu_custom_call" | custom-call | flops 1207959552 | bytes 6291456 | tf_op jit(solution)/shard_map/pallas_call | solution.py:190
  68.2 6.3 %all-to-all-start = ((bf16[8,768,128]{2,1,0:T(8,128)(2,1)}), bf16[8,768,128]{2,1,0:T(8,128)(2,1)S(1)}, u32[]{:S(2)}, u32[]{:S(2)}) async-start(bf16[8,768,128]{2,1,0:T(8,128)(2,1)} %shard_map.50), calls=%async_computation | async-start | bytes 3145728 | tf_op jit(solution)/shard_map/all_to_all | solution.py:273
  79.1 15.1 %all-to-all-done.parts_ref = bf16[8,768,128]{2,1,0:T(8,128)(2,1)S(1)} async-done(((bf16[8,768,128]{2,1,0:T(8,128)(2,1)}), bf16[8,768,128]{2,1,0:T(8,128)(2,1)S(1)}, u32[]{:S(2)}, u32[]{:S(2)}) %all-to-all-start) | async-done | bytes 1572896 | tf_op jit(solution)/shard_map/all_to_all | solution.py:273
  97.3 2.1 %shard_map.51 = f32[16,136,128]{2,1,0:T(8,128)S(1)} custom-call(bf16[8,768,128]{2,1,0:T(8,128)(2,1)S(1)} %all-to-all-done.parts_ref, bf16[2,768,128]{2,1,0:T(8,128)(2,1)S(1)} %shard_map.47.refs_0_, bf16[2,768,128]{2,1,0:T(8,128)(2,1)S(1)} %collective-permute-done.6.refs_1_, bf16[2,768,128]{2,1,0:T(8,128)(2,1)S(1)} %collective-permute-done.9.refs_2_, ...), custom_call_target="tpu_custom_call" | custom-call | flops 805306368 | bytes 6291456 | tf_op jit(solution)/shard_map/pallas_call | solution.py:226
  99.5 22.4 %all_to_all.10 = f16[16,136,128]{2,1,0:T(8,128)(2,1)S(1)} all-to-all(f16[16,136,128]{2,1,0:T(8,128)(2,1)S(1)} %convert_element_type.20), channel_id=1, replica_groups={{0,32,192,224,128,160,64,96,16,48,208,240,144,176,80,112},{17,49,209,24..., dimensions={0} | all-to-all | bytes 1114112 | tf_op jit(solution)/shard_map/all_to_all | solution.py:275
  (54 shorter events, 14.4 us)
Async XLA Ops:
  1.8 8.2 %collective-permute-start.1 = (bf16[768,128]{1,0:T(8,128)(2,1)S(1)}, bf16[768,128]{1,0:T(8,128)(2,1)S(1)}, u32[]{:S(2)}, u32[]{:S(2)}) collective-permute-start(bf16[768,128]{1,0:T(8,128)(2,1)S(1)} %broadcast_multiply_fusion.one), channel_id=1, source_target_pairs={{0,2},{1,3},{2,0},{3,1},{4,6},{5,7},{6,4},{7,5},{8,10},{9,11},{10,... | collective-permute-start | bytes 589832 | tf_op jit(solution)/shard_map/ppermute | solution.py:31
  4.0 6.0 %collective-permute-start = (bf16[768,128]{1,0:T(8,128)(2,1)S(1)}, bf16[768,128]{1,0:T(8,128)(2,1)S(1)}, u32[]{:S(2)}, u32[]{:S(2)}) collective-permute-start(bf16[768,128]{1,0:T(8,128)(2,1)S(1)} %broadcast_multiply_fusion.one), channel_id=1, source_target_pairs={{0,0},{1,1},{2,2},{3,3},{4,224},{5,225},{6,226},{7,227},{8,192},{9... | collective-permute-start | bytes 589832 | tf_op jit(solution)/shard_map/ppermute | solution.py:31
  4.8 1.3 %copy-start = (bf16[768,768]{1,0:T(8,128)(2,1)S(1)}, bf16[768,768]{1,0:T(8,128)(2,1)}, u32[]{:S(2)}) copy-start(bf16[768,768]{1,0:T(8,128)(2,1)} %value_ref) | copy-start | bytes 3538948
  10.1 18.9 %collective-permute-start.3 = (bf16[768,128]{1,0:T(8,128)(2,1)S(1)}, bf16[768,128]{1,0:T(8,128)(2,1)S(1)}, u32[]{:S(2)}, u32[]{:S(2)}) collective-permute-start(bf16[768,128]{1,0:T(8,128)(2,1)S(1)} %collective-permute-done.refs_0_), channel_id=1, source_target_pairs={{0,224},{1,225},{2,226},{3,227},{4,228},{5,229},{6,230},{7,231},{8... | collective-permute-start | bytes 589832 | tf_op jit(solution)/shard_map/ppermute | solution.py:31
  20.3 8.8 %collective-permute-start.2 = (bf16[768,128]{1,0:T(8,128)(2,1)S(1)}, bf16[768,128]{1,0:T(8,128)(2,1)S(1)}, u32[]{:S(2)}, u32[]{:S(2)}) collective-permute-start(bf16[768,128]{1,0:T(8,128)(2,1)S(1)} %collective-permute-done.refs_0_), channel_id=1, source_target_pairs={{0,32},{1,33},{2,34},{3,35},{4,36},{5,37},{6,38},{7,39},{8,40},{9,... | collective-permute-start | bytes 589832 | tf_op jit(solution)/shard_map/ppermute | solution.py:31
  20.3 18.9 %collective-permute-start.6 = (bf16[2,768,128]{2,1,0:T(8,128)(2,1)S(1)}, bf16[2,768,128]{2,1,0:T(8,128)(2,1)S(1)}, u32[]{:S(2)}, u32[]{:S(2)}) collective-permute-start(bf16[2,768,128]{2,1,0:T(8,128)(2,1)S(1)} %shard_map.47.refs_0_), channel_id=1, source_target_pairs={{0,4},{1,5},{2,6},{3,7},{4,8},{5,9},{6,10},{7,11},{8,12},{9,13},{1... | collective-permute-start | bytes 1179656 | tf_op jit(solution)/shard_map/ppermute | solution.py:31
  24.8 35.8 %collective-permute-start.13 = (bf16[768,768]{1,0:T(8,128)(2,1)S(1)}, bf16[768,768]{1,0:T(8,128)(2,1)S(1)}, u32[]{:S(2)}, u32[]{:S(2)}) collective-permute-start(bf16[768,768]{1,0:T(8,128)(2,1)S(1)} %shard_map.46), channel_id=1, source_target_pairs={{0,2},{1,18},{2,0},{3,16},{4,6},{5,22},{6,4},{7,20},{8,10},{9,26},... | collective-permute-start | bytes 3538952 | tf_op jit(solution)/shard_map/ppermute | solution.py:31
  24.8 35.8 %collective-permute-start.12 = (bf16[768,768]{1,0:T(8,128)(2,1)S(1)}, bf16[768,768]{1,0:T(8,128)(2,1)S(1)}, u32[]{:S(2)}, u32[]{:S(2)}) collective-permute-start(bf16[768,768]{1,0:T(8,128)(2,1)S(1)} %shard_map.46), channel_id=1, source_target_pairs={{0,0},{1,16},{2,2},{3,18},{4,4},{5,20},{6,6},{7,22},{8,8},{9,24},{... | collective-permute-start | bytes 3538952 | tf_op jit(solution)/shard_map/ppermute | solution.py:31
  29.0 6.5 %collective-permute-start.5 = (bf16[768,128]{1,0:T(8,128)(2,1)S(1)}, bf16[768,128]{1,0:T(8,128)(2,1)S(1)}, u32[]{:S(2)}, u32[]{:S(2)}) collective-permute-start(bf16[768,128]{1,0:T(8,128)(2,1)S(1)} %collective-permute-done.3.refs_1_), channel_id=1, source_target_pairs={{0,224},{1,225},{2,226},{3,227},{4,228},{5,229},{6,230},{7,231},{8... | collective-permute-start | bytes 589832 | tf_op jit(solution)/shard_map/ppermute | solution.py:31
  32.3 6.9 %collective-permute-start.4 = (bf16[768,128]{1,0:T(8,128)(2,1)S(1)}, bf16[768,128]{1,0:T(8,128)(2,1)S(1)}, u32[]{:S(2)}, u32[]{:S(2)}) collective-permute-start(bf16[768,128]{1,0:T(8,128)(2,1)S(1)} %collective-permute-done.2.refs_8_), channel_id=1, source_target_pairs={{0,32},{1,33},{2,34},{3,35},{4,36},{5,37},{6,38},{7,39},{8,40},{9,... | collective-permute-start | bytes 589832 | tf_op jit(solution)/shard_map/ppermute | solution.py:31
  39.2 12.9 %collective-permute-start.9 = (bf16[2,768,128]{2,1,0:T(8,128)(2,1)S(1)}, bf16[2,768,128]{2,1,0:T(8,128)(2,1)S(1)}, u32[]{:S(2)}, u32[]{:S(2)}) collective-permute-start(bf16[2,768,128]{2,1,0:T(8,128)(2,1)S(1)} %collective-permute-done.6.refs_1_), channel_id=1, source_target_pairs={{0,4},{1,5},{2,6},{3,7},{4,8},{5,9},{6,10},{7,11},{8,12},{9,13},{1... | collective-permute-start | bytes 1179656 | tf_op jit(solution)/shard_map/ppermute | solution.py:31
  43.8 6.7 %collective-permute-start.8 = (bf16[768,128]{1,0:T(8,128)(2,1)S(1)}, bf16[768,128]{1,0:T(8,128)(2,1)S(1)}, u32[]{:S(2)}, u32[]{:S(2)}) collective-permute-start(bf16[768,128]{1,0:T(8,128)(2,1)S(1)} %collective-permute-done.5.refs_2_), channel_id=1, source_target_pairs={{0,224},{1,225},{2,226},{3,227},{4,228},{5,229},{6,230},{7,231},{8... | collective-permute-start | bytes 589832 | tf_op jit(solution)/shard_map/ppermute | solution.py:31
  43.8 7.9 %collective-permute-start.7 = (bf16[768,128]{1,0:T(8,128)(2,1)S(1)}, bf16[768,128]{1,0:T(8,128)(2,1)S(1)}, u32[]{:S(2)}, u32[]{:S(2)}) collective-permute-start(bf16[768,128]{1,0:T(8,128)(2,1)S(1)} %collective-permute-done.4.refs_7_), channel_id=1, source_target_pairs={{0,32},{1,33},{2,34},{3,35},{4,36},{5,37},{6,38},{7,39},{8,40},{9,... | collective-permute-start | bytes 589832 | tf_op jit(solution)/shard_map/ppermute | solution.py:31
  52.2 9.0 %collective-permute-start.14 = (bf16[2,768,128]{2,1,0:T(8,128)(2,1)S(1)}, bf16[2,768,128]{2,1,0:T(8,128)(2,1)S(1)}, u32[]{:S(2)}, u32[]{:S(2)}) collective-permute-start(bf16[2,768,128]{2,1,0:T(8,128)(2,1)S(1)} %collective-permute-done.9.refs_2_), channel_id=1, source_target_pairs={{0,4},{1,5},{2,6},{3,7},{4,8},{5,9},{6,10},{7,11},{8,12},{9,13},{1... | collective-permute-start | bytes 1179656 | tf_op jit(solution)/shard_map/ppermute | solution.py:31
  54.7 5.9 %collective-permute-start.10 = (bf16[384,128]{1,0:T(8,128)(2,1)S(1)}, bf16[384,128]{1,0:T(8,128)(2,1)S(1)}, u32[]{:S(2)}, u32[]{:S(2)}) collective-permute-start(bf16[384,128]{1,0:T(8,128)(2,1)S(1)} %slice.12), channel_id=1, source_target_pairs={{0,32},{1,33},{2,34},{3,35},{4,36},{5,37},{6,38},{7,39},{8,40},{9,... | collective-permute-start | bytes 294920 | tf_op jit(solution)/shard_map/ppermute | solution.py:31
  54.8 5.8 %collective-permute-start.11 = (bf16[384,128]{1,0:T(8,128)(2,1)S(1)}, bf16[384,128]{1,0:T(8,128)(2,1)S(1)}, u32[]{:S(2)}, u32[]{:S(2)}) collective-permute-start(bf16[384,128]{1,0:T(8,128)(2,1)S(1)} %slice.13), channel_id=1, source_target_pairs={{0,224},{1,225},{2,226},{3,227},{4,228},{5,229},{6,230},{7,231},{8... | collective-permute-start | bytes 294920 | tf_op jit(solution)/shard_map/ppermute | solution.py:31
  61.1 2.8 %collective-permute-start.15 = (bf16[768,768]{1,0:T(8,128)(2,1)S(1)}, bf16[768,768]{1,0:T(8,128)(2,1)S(1)}, u32[]{:S(2)}, u32[]{:S(2)}) collective-permute-start(bf16[768,768]{1,0:T(8,128)(2,1)S(1)} %collective-permute-done.12.one), channel_id=1, source_target_pairs={{0,1},{1,0},{2,3},{3,2},{4,5},{5,4},{6,7},{7,6},{8,9},{9,8},{10,11... | collective-permute-start | bytes 3538952 | tf_op jit(solution)/shard_map/ppermute | solution.py:31
  61.1 4.5 %collective-permute-start.16 = (bf16[768,768]{1,0:T(8,128)(2,1)S(1)}, bf16[768,768]{1,0:T(8,128)(2,1)S(1)}, u32[]{:S(2)}, u32[]{:S(2)}) collective-permute-start(bf16[768,768]{1,0:T(8,128)(2,1)S(1)} %collective-permute-done.13.two), channel_id=1, source_target_pairs={{0,1},{1,0},{2,3},{3,2},{4,5},{5,4},{6,7},{7,6},{8,9},{9,8},{10,11... | collective-permute-start | bytes 3538952 | tf_op jit(solution)/shard_map/ppermute | solution.py:31
  68.2 26.1 %all-to-all-start = ((bf16[8,768,128]{2,1,0:T(8,128)(2,1)}), bf16[8,768,128]{2,1,0:T(8,128)(2,1)S(1)}, u32[]{:S(2)}, u32[]{:S(2)}) async-start(bf16[8,768,128]{2,1,0:T(8,128)(2,1)} %shard_map.50), calls=%async_computation | async-start | bytes 3145728 | tf_op jit(solution)/shard_map/all_to_all | solution.py:273
  74.6 1.7 %collective-permute-start.17 = (bf16[2,768,128]{2,1,0:T(8,128)(2,1)S(1)}, bf16[2,768,128]{2,1,0:T(8,128)(2,1)S(1)}, u32[]{:S(2)}, u32[]{:S(2)}) collective-permute-start(bf16[2,768,128]{2,1,0:T(8,128)(2,1)S(1)} %shard_map.47.refs_0_), channel_id=1, source_target_pairs={{0,1},{1,0},{2,3},{3,2},{4,5},{5,4},{6,7},{7,6},{8,9},{9,8},{10,11... | collective-permute-start | bytes 1179656 | tf_op jit(solution)/shard_map/ppermute | solution.py:31
  74.6 2.3 %collective-permute-start.18 = (bf16[2,768,128]{2,1,0:T(8,128)(2,1)S(1)}, bf16[2,768,128]{2,1,0:T(8,128)(2,1)S(1)}, u32[]{:S(2)}, u32[]{:S(2)}) collective-permute-start(bf16[2,768,128]{2,1,0:T(8,128)(2,1)S(1)} %collective-permute-done.6.refs_1_), channel_id=1, source_target_pairs={{0,1},{1,0},{2,3},{3,2},{4,5},{5,4},{6,7},{7,6},{8,9},{9,8},{10,11... | collective-permute-start | bytes 1179656 | tf_op jit(solution)/shard_map/ppermute | solution.py:31
  75.1 2.6 %collective-permute-start.19 = (bf16[2,768,128]{2,1,0:T(8,128)(2,1)S(1)}, bf16[2,768,128]{2,1,0:T(8,128)(2,1)S(1)}, u32[]{:S(2)}, u32[]{:S(2)}) collective-permute-start(bf16[2,768,128]{2,1,0:T(8,128)(2,1)S(1)} %collective-permute-done.9.refs_2_), channel_id=1, source_target_pairs={{0,1},{1,0},{2,3},{3,2},{4,5},{5,4},{6,7},{7,6},{8,9},{9,8},{10,11... | collective-permute-start | bytes 1179656 | tf_op jit(solution)/shard_map/ppermute | solution.py:31
  75.1 3.3 %collective-permute-start.20 = (bf16[2,768,128]{2,1,0:T(8,128)(2,1)S(1)}, bf16[2,768,128]{2,1,0:T(8,128)(2,1)S(1)}, u32[]{:S(2)}, u32[]{:S(2)}) collective-permute-start(bf16[2,768,128]{2,1,0:T(8,128)(2,1)S(1)} %collective-permute-done.14.refs_3_), channel_id=1, source_target_pairs={{0,1},{1,0},{2,3},{3,2},{4,5},{5,4},{6,7},{7,6},{8,9},{9,8},{10,11... | collective-permute-start | bytes 1179656 | tf_op jit(solution)/shard_map/ppermute | solution.py:31
  94.3 1.0 copy-start.2
  (6 other events, 5.0 us)

commit v3 on v2

--- a/solution.py
+++ b/solution.py
@@ -34,6 +34,11 @@
 def turn(z, xl, y, xh, k):
     shift = (y - z // 2) % LANES
     return (z + shift if z % 2 else z - shift), xl, z // 2, xh, k
+
+
+def turn_far(z, xl, y, xh, k):
+    z_to, *rest = turn(z, xl, y, xh, k)
+    return z_to + PLANES // 2, *rest
 
 
 def z_up(z, xl, y, xh, k):
@@ -119,7 +124,7 @@
     return value * wide.astype(value.dtype)
 
 
-def mask_kernel(pattern_ref, value_ref, out_ref):
+def mask_kernel(token_ref, pattern_ref, value_ref, out_ref):
     for i in range(pattern_ref.shape[0]):
         for j in range(pattern_ref.shape[1]):
             spot = (slice(i * BLOCK, (i + 1) * BLOCK), slice(j * BLOCK, (j + 1) * BLOCK))
@@ -127,9 +132,9 @@
             out_ref[spot] = jnp.where(pattern_ref[i, j] != 0, value, jnp.zeros_like(value))
 
 
-def masked_tile(value, pattern):
+def masked_tile(token, value, pattern):
     cost = pl.CostEstimate(flops=value.size, bytes_accessed=4 * value.size, transcendentals=0)
-    return on_device(mask_kernel, value.shape, value.dtype, [SMEM, VMEM], cost=cost)(pattern, value)
+    return on_device(mask_kernel, value.shape, value.dtype, [SMEM, SMEM, VMEM], cost=cost)(token, pattern, value)
 
 
 def pair_kernel(one, two, out_ref):
@@ -142,27 +147,20 @@
     return on_device(pair_kernel, (2, *one.shape), one.dtype, [VMEM] * 2, cost=cost)(one, two)
 
 
-def line_up_kernel(spot_ref, *refs):
-    blocks, p_ref = refs[:9], refs[9]
+def line_up_kernel(spot_ref, own, above, below, up_two, down_two, p_ref):
     z, y, xh = spot_ref[0], spot_ref[1], spot_ref[2]
-    half = blocks[4].shape[0]
-    for d in range(PLANES):
+    blocks = [own.at[0], above.at[0], down_two, below.at[1], own.at[1], above.at[1], up_two, below.at[0]]
+    for d, block in enumerate(blocks):
         place_in = lax.rem(z + d - 2 * y - 1 + 2 * PLANES, PLANES)
         odd = (place_in < LANES).astype(jnp.int32)
         shift = jnp.where(odd == 1, place_in, PLANES - 1 - place_in)
         side = lax.rem(odd + xh, 2)
         column = pl.multiple_of(lax.rem(y + shift, LANES) * BLOCK, BLOCK)
-        if d < 4:
-            p_ref[side, :, pl.ds(column, BLOCK)] = blocks[d][...]
-        elif d == 4:
-            p_ref[side, :half, pl.ds(column, BLOCK)] = blocks[4][...]
-            p_ref[side, half:, pl.ds(column, BLOCK)] = blocks[5][...]
-        else:
-            p_ref[side, :, pl.ds(column, BLOCK)] = blocks[d + 1][...]
-
-
-def line_up(spot, blocks):
-    size = blocks[0].shape[0]
+        p_ref[side, :, pl.ds(column, BLOCK)] = block[...]
+
+
+def line_up(spot, *blocks):
+    size = blocks[0].shape[1]
     return on_device(
         line_up_kernel, (2, size, LANES * BLOCK), jnp.bfloat16, [SMEM] + [VMEM] * len(blocks),
         cost=pl.CostEstimate(flops=0, bytes_accessed=4 << 20, transcendentals=0),
@@ -193,19 +191,21 @@
         jnp.bfloat16,
         [VMEM] * (3 + len(before)),
         cost=pl.CostEstimate(flops=4 * size * size * LANES * BLOCK, bytes_accessed=6 << 20, transcendentals=0),
-        grant=6,
+        grant=3,
     )(p_all, one, two, *before)
 
 
 def c_kernel(parts_ref, *refs):
     pairs, (out_ref, w_ref) = refs[: 2 * LANES], refs[2 * LANES :]
-    w = parts_ref[0].astype(jnp.float32)
-    for i in range(1, parts_ref.shape[0]):
-        w += parts_ref[i].astype(jnp.float32)
-    turned = w.T
-    high = turned.astype(jnp.bfloat16)
-    w_ref[:BLOCK] = high
-    w_ref[BLOCK:] = (turned - high.astype(jnp.float32)).astype(jnp.bfloat16)
+    for start in range(0, parts_ref.shape[1], BLOCK):
+        rows = slice(start, start + BLOCK)
+        w = parts_ref[0, rows].astype(jnp.float32)
+        for i in range(1, parts_ref.shape[0]):
+            w += parts_ref[i, rows].astype(jnp.float32)
+        turned = w.T
+        high = turned.astype(jnp.bfloat16)
+        w_ref[:BLOCK, rows] = high
+        w_ref[BLOCK:, rows] = (turned - high.astype(jnp.float32)).astype(jnp.bfloat16)
     units = [pair.at[i] for pair in pairs for i in range(2)]
     top = jnp.zeros((BLOCK, BLOCK), jnp.float32)
     for i, unit in enumerate(units):
@@ -230,7 +230,7 @@
         [VMEM] * (2 * LANES + 1),
         [pltpu.VMEM((2 * BLOCK, size), jnp.bfloat16)],
         pl.CostEstimate(flops=16 * LANES * size * BLOCK * BLOCK, bytes_accessed=6 << 20, transcendentals=0),
-        grant=8,
+        grant=2,
     )(parts, *pairs)
 
 
@@ -247,28 +247,25 @@
     row, col = lax.axis_index("row"), lax.axis_index("col")
     spot = jnp.stack([row // 2, col // 4, (col // 2) % 2]).astype(jnp.int32)
     p_eff = masked(prolong, p_pattern)
-    p_eff, a_matrix = both(p_eff, a_matrix)
-    first, across = send(p_eff, turn), send(p_eff, far_x)
-    a_eff = masked_tile(a_matrix, a_pattern)
+    p_eff, spot = both(p_eff, spot)
+    first, second = send(p_eff, turn), send(p_eff, turn_far)
+    across = send(p_eff, far_x)
+    a_eff = masked_tile(spot, a_matrix, a_pattern)
+    a_eff, across = both(a_eff, across)
     near, distant = send(a_eff, swap), send(a_eff, swap_far)
-    first, p_eff, across, spot, _ = both(first, p_eff, across, spot, a_eff)
     pair = paired(p_eff, across)
-    up_1, down_1 = both(send(first, z_up), send(first, z_down))
-    below = send(pair, y_up)
-    up_2, down_2 = both(send(up_1, z_up), send(down_1, z_down))
-    up_2, down_2, below = both(up_2, down_2, below)
-    beyond = send(below, y_up)
-    up_3, down_3 = both(send(up_2, z_up), send(down_2, z_down))
-    up_3, down_3, beyond = both(up_3, down_3, beyond)
-    half = first.shape[0] // 2
-    far = [send(up_3[:half], z_up), send(down_3[half:], z_down)]
-    above = send(beyond, y_up)
-    *far, near, distant, above = both(*far, near, distant, above)
-    p_all = line_up(spot, [first, down_1, down_2, down_3, *far, up_3, up_2, up_1])
+    first, second, _ = both(first, second, a_eff)
+    own = paired(first, second)
+    below, above, pair_1 = both(send(own, z_up), send(own, z_down), send(pair, y_up))
+    pair_2 = send(pair_1, y_up)
+    up_two, down_two = send(below[0], z_up), send(above[0], z_down)
+    up_two, down_two, near, distant, pair_2 = both(up_two, down_two, near, distant, pair_2)
+    pair_3 = send(pair_2, y_up)
+    p_all = line_up(spot, own, above, below, up_two, down_two)
     near_2, distant_2 = send(near, other_core), send(distant, other_core)
     w_part = w_products(p_all, near, distant)
     w_part = w_products(p_all, near_2, distant_2, w_part)
-    w_part, *pairs = both(w_part, pair, below, beyond, above)
+    w_part, *pairs = both(w_part, pair, pair_1, pair_2, pair_3)
     pairs += [send(p, other_core) for p in pairs]
     w_parts = lax.all_to_all(w_part, AXES, 0, 0, axis_index_groups=W_GROUPS, tiled=True)
     c_part = c_products(w_parts, pairs).astype(jnp.float16)

time: 124 us -> 117 us (0.944)
  starting transfers between devices: 45.4 us -> 38.3 us
    ppermute x21 -> x18, starting transfers between devices: 39 us -> 31.4 us  [send(): return lax.ppermute(value, AXES, pairs)]
    ppermute x21 -> x18, waiting for transfers between devices: 21.8 us -> 21.9 us  [send(): return lax.ppermute(value, AXES, pairs)]
  transfers between devices with their start and end apart: 22 -> 19, of which waited for: 13 -> 11; matrix products, arithmetic and copies ran while one was open for 0% -> 0% of each run, Pallas kernels for 3% -> 5%
where the time goes in v3:
time: 117 us
  starting transfers between devices  38.3 us (33%)
  waiting for transfers between devices  36.4 us (31%)
  blocking collectives  23.6 us (20%)
  local copies, waits for them, and re-layouts  8.04 us (7%)
  Pallas kernels  7.85 us (7%)
  other arithmetic  2.32 us (2%)
    ppermute x18, starting transfers between devices, send(): return lax.ppermute(value, AXES, pairs)  31.4 us
    all_to_all x1, blocking collectives, local(): lax.all_to_all(c_part, AXES, 0, 0, axis_index_groups=C_GROUPS, tiled=True)  23.6 us
    ppermute x18, waiting for transfers between devices, send(): return lax.ppermute(value, AXES, pairs)  21.9 us
    all_to_all x1, waiting for transfers between devices, local(): lax.all_to_all(w_part, AXES, 0, 0, axis_index_groups=W_GROUPS, tiled=True)  14.5 us
    unnamed x16, local copies, waits for them, and re-layouts  7.21 us
    all_to_all x1, starting transfers between devices, local(): lax.all_to_all(w_part, AXES, 0, 0, axis_index_groups=W_GROUPS, tiled=True)  6.89 us
    pallas_call x2, Pallas kernels, w_products(): on_device(functools.partial(w_kernel, LANES * len(before)), (LANES * (1 +...  3.93 us
  transfers between devices with their start and end apart: 19, of which 11 were waited for; matrix products, arithmetic and copies ran while one was open for 0% of the time, Pallas kernels for 5%

profile of v3, /device:TPU:2, one launch (start us, length us, event | category | flops | bytes accessed | tf_op | source)
XLA Modules:
  0.0 116.6 jit_solution(1719435703219098384)
XLA Ops:
  0.7 1.1 broadcast_multiply_fusion.one
  1.9 2.2 %collective-permute-start.2 = (bf16[768,128]{1,0:T(8,128)(2,1)S(1)}, bf16[768,128]{1,0:T(8,128)(2,1)S(1)}, u32[]{:S(2)}, u32[]{:S(2)}) collective-permute-start(bf16[768,128]{1,0:T(8,128)(2,1)S(1)} %broadcast_multiply_fusion.one), channel_id=1, source_target_pairs={{0,2},{1,3},{2,0},{3,1},{4,6},{5,7},{6,4},{7,5},{8,10},{9,11},{10,... | collective-permute-start | bytes 589832 | tf_op jit(solution)/shard_map/ppermute | solution.py:31
  4.7 10.8 %collective-permute-start.1 = (bf16[768,128]{1,0:T(8,128)(2,1)S(1)}, bf16[768,128]{1,0:T(8,128)(2,1)S(1)}, u32[]{:S(2)}, u32[]{:S(2)}) collective-permute-start(bf16[768,128]{1,0:T(8,128)(2,1)S(1)} %broadcast_multiply_fusion.one), channel_id=1, source_target_pairs={{0,128},{1,129},{2,130},{3,131},{4,96},{5,97},{6,98},{7,99},{8,64}... | collective-permute-start | bytes 589832 | tf_op jit(solution)/shard_map/ppermute | solution.py:31
  15.5 1.3 %copy-done = bf16[768,768]{1,0:T(8,128)(2,1)S(1)} copy-done((bf16[768,768]{1,0:T(8,128)(2,1)S(1)}, bf16[768,768]{1,0:T(8,128)(2,1)}, u32[]{:S(2)}) %copy-start) | copy-done | bytes 1179672
  18.4 1.9 %collective-permute-start.8 = (bf16[768,768]{1,0:T(8,128)(2,1)S(1)}, bf16[768,768]{1,0:T(8,128)(2,1)S(1)}, u32[]{:S(2)}, u32[]{:S(2)}) collective-permute-start(bf16[768,768]{1,0:T(8,128)(2,1)S(1)} %shard_map.46), channel_id=1, source_target_pairs={{0,0},{1,16},{2,2},{3,18},{4,4},{5,20},{6,6},{7,22},{8,8},{9,24},{... | collective-permute-start | bytes 3538952 | tf_op jit(solution)/shard_map/ppermute | solution.py:31
  20.3 1.7 %collective-permute-start.9 = (bf16[768,768]{1,0:T(8,128)(2,1)S(1)}, bf16[768,768]{1,0:T(8,128)(2,1)S(1)}, u32[]{:S(2)}, u32[]{:S(2)}) collective-permute-start(bf16[768,768]{1,0:T(8,128)(2,1)S(1)} %shard_map.46), channel_id=1, source_target_pairs={{0,2},{1,18},{2,0},{3,16},{4,6},{5,22},{6,4},{7,20},{8,10},{9,26},... | collective-permute-start | bytes 3538952 | tf_op jit(solution)/shard_map/ppermute | solution.py:31
  22.1 1.7 %collective-permute-start.5 = (bf16[2,768,128]{2,1,0:T(8,128)(2,1)S(1)}, bf16[2,768,128]{2,1,0:T(8,128)(2,1)S(1)}, u32[]{:S(2)}, u32[]{:S(2)}) collective-permute-start(bf16[2,768,128]{2,1,0:T(8,128)(2,1)S(1)} %shard_map.48.refs_0_), channel_id=1, source_target_pairs={{0,4},{1,5},{2,6},{3,7},{4,8},{5,9},{6,10},{7,11},{8,12},{9,13},{1... | collective-permute-start | bytes 1179656 | tf_op jit(solution)/shard_map/ppermute | solution.py:31
  23.9 1.6 %collective-permute-start.3 = (bf16[2,768,128]{2,1,0:T(8,128)(2,1)S(1)}, bf16[2,768,128]{2,1,0:T(8,128)(2,1)S(1)}, u32[]{:S(2)}, u32[]{:S(2)}) collective-permute-start(bf16[2,768,128]{2,1,0:T(8,128)(2,1)S(1)} %shard_map.47.own), channel_id=1, source_target_pairs={{0,32},{1,33},{2,34},{3,35},{4,36},{5,37},{6,38},{7,39},{8,40},{9,... | collective-permute-start | bytes 1179656 | tf_op jit(solution)/shard_map/ppermute | solution.py:31
  25.5 1.9 %collective-permute-start.4 = (bf16[2,768,128]{2,1,0:T(8,128)(2,1)S(1)}, bf16[2,768,128]{2,1,0:T(8,128)(2,1)S(1)}, u32[]{:S(2)}, u32[]{:S(2)}) collective-permute-start(bf16[2,768,128]{2,1,0:T(8,128)(2,1)S(1)} %shard_map.47.own), channel_id=1, source_target_pairs={{0,224},{1,225},{2,226},{3,227},{4,228},{5,229},{6,230},{7,231},{8... | collective-permute-start | bytes 1179656 | tf_op jit(solution)/shard_map/ppermute | solution.py:31
  27.4 4.3 %collective-permute-done.5.refs_1_ = bf16[2,768,128]{2,1,0:T(8,128)(2,1)S(1)} collective-permute-done((bf16[2,768,128]{2,1,0:T(8,128)(2,1)S(1)}, bf16[2,768,128]{2,1,0:T(8,128)(2,1)S(1)}, u32[]{:S(2)}, u32[]{:S(2)}) %collective-permute-start.5) | collective-permute-done | bytes 393248 | tf_op jit(solution)/shard_map/ppermute | solution.py:31
  31.7 3.5 %collective-permute-done.3.below = bf16[2,768,128]{2,1,0:T(8,128)(2,1)S(1)} collective-permute-done((bf16[2,768,128]{2,1,0:T(8,128)(2,1)S(1)}, bf16[2,768,128]{2,1,0:T(8,128)(2,1)S(1)}, u32[]{:S(2)}, u32[]{:S(2)}) %collective-permute-start.3) | collective-permute-done | bytes 393248 | tf_op jit(solution)/shard_map/ppermute | solution.py:31
  35.8 2.3 %collective-permute-start.10 = (bf16[2,768,128]{2,1,0:T(8,128)(2,1)S(1)}, bf16[2,768,128]{2,1,0:T(8,128)(2,1)S(1)}, u32[]{:S(2)}, u32[]{:S(2)}) collective-permute-start(bf16[2,768,128]{2,1,0:T(8,128)(2,1)S(1)} %collective-permute-done.5.refs_1_), channel_id=1, source_target_pairs={{0,4},{1,5},{2,6},{3,7},{4,8},{5,9},{6,10},{7,11},{8,12},{9,13},{1... | collective-permute-start | bytes 1179656 | tf_op jit(solution)/shard_map/ppermute | solution.py:31
  38.7 2.8 %collective-permute-start.7 = (bf16[768,128]{1,0:T(8,128)(2,1)S(1)}, bf16[768,128]{1,0:T(8,128)(2,1)S(1)}, u32[]{:S(2)}, u32[]{:S(2)}) collective-permute-start(bf16[768,128]{1,0:T(8,128)(2,1)S(1)} %slice_bitcast_fusion), channel_id=1, source_target_pairs={{0,224},{1,225},{2,226},{3,227},{4,228},{5,229},{6,230},{7,231},{8... | collective-permute-start | bytes 589832 | tf_op jit(solution)/shard_map/ppermute | solution.py:31
  41.5 3.8 %collective-permute-done.6.up_two = bf16[768,128]{1,0:T(8,128)(2,1)S(1)} collective-permute-done((bf16[768,128]{1,0:T(8,128)(2,1)S(1)}, bf16[768,128]{1,0:T(8,128)(2,1)S(1)}, u32[]{:S(2)}, u32[]{:S(2)}) %collective-permute-start.6) | collective-permute-done | bytes 196640 | tf_op jit(solution)/shard_map/ppermute | solution.py:31
  45.3 2.0 %collective-permute-done.10.refs_2_ = bf16[2,768,128]{2,1,0:T(8,128)(2,1)S(1)} collective-permute-done((bf16[2,768,128]{2,1,0:T(8,128)(2,1)S(1)}, bf16[2,768,128]{2,1,0:T(8,128)(2,1)S(1)}, u32[]{:S(2)}, u32[]{:S(2)}) %collective-permute-start.10) | collective-permute-done | bytes 393248 | tf_op jit(solution)/shard_map/ppermute | solution.py:31
  48.5 1.7 %collective-permute-start.13 = (bf16[2,768,128]{2,1,0:T(8,128)(2,1)S(1)}, bf16[2,768,128]{2,1,0:T(8,128)(2,1)S(1)}, u32[]{:S(2)}, u32[]{:S(2)}) collective-permute-start(bf16[2,768,128]{2,1,0:T(8,128)(2,1)S(1)} %collective-permute-done.10.refs_2_), channel_id=1, source_target_pairs={{0,4},{1,5},{2,6},{3,7},{4,8},{5,9},{6,10},{7,11},{8,12},{9,13},{1... | collective-permute-start | bytes 1179656 | tf_op jit(solution)/shard_map/ppermute | solution.py:31
  51.0 1.4 %shard_map.50.rest_0_ = bf16[4,768,128]{2,1,0:T(8,128)(2,1)S(1)} custom-call(bf16[2,768,512]{2,1,0:T(8,128)(2,1)S(1)} %shard_map.49.p_ref, bf16[768,768]{1,0:T(8,128)(2,1)S(1)} %collective-permute-done.8.one, bf16[768,768]{1,0:T(8,128)(2,1)S(1)} %collective-permute-done.9.two), custom_call_target="tpu_custom_call" | custom-call | flops 1207959552 | bytes 6291456 | tf_op jit(solution)/shard_map/pallas_call | solution.py:188
  52.5 2.5 %shard_map.51 = bf16[8,768,128]{2,1,0:T(8,128)(2,1)} custom-call(bf16[2,768,512]{2,1,0:T(8,128)(2,1)S(1)} %shard_map.49.p_ref, bf16[768,768]{1,0:T(8,128)(2,1)S(1)} %collective-permute-done.11.one, bf16[768,768]{1,0:T(8,128)(2,1)S(1)} %collective-permute-done.12.two, bf16[4,768,128]{2,1,0:T(8,128)(2,1)S(1)} %shard_map.50.rest_0_), custom_call_target="tpu_custom_call" | custom-call | flops 1207959552 | bytes 6291456 | tf_op jit(solution)/shard_map/pallas_call | solution.py:188
  55.0 5.7 %collective-permute-done.13.refs_3_ = bf16[2,768,128]{2,1,0:T(8,128)(2,1)S(1)} collective-permute-done((bf16[2,768,128]{2,1,0:T(8,128)(2,1)S(1)}, bf16[2,768,128]{2,1,0:T(8,128)(2,1)S(1)}, u32[]{:S(2)}, u32[]{:S(2)}) %collective-permute-start.13) | collective-permute-done | bytes 393248 | tf_op jit(solution)/shard_map/ppermute | solution.py:31
  60.7 6.9 %all-to-all-start = ((bf16[8,768,128]{2,1,0:T(8,128)(2,1)}), bf16[8,768,128]{2,1,0:T(8,128)(2,1)S(1)}, u32[]{:S(2)}, u32[]{:S(2)}) async-start(bf16[8,768,128]{2,1,0:T(8,128)(2,1)} %shard_map.51), calls=%async_computation | async-start | bytes 3145728 | tf_op jit(solution)/shard_map/all_to_all | solution.py:270
  72.2 14.5 %all-to-all-done.parts_ref = bf16[8,768,128]{2,1,0:T(8,128)(2,1)S(1)} async-done(((bf16[8,768,128]{2,1,0:T(8,128)(2,1)}), bf16[8,768,128]{2,1,0:T(8,128)(2,1)S(1)}, u32[]{:S(2)}, u32[]{:S(2)}) %all-to-all-start) | async-done | bytes 1572896 | tf_op jit(solution)/shard_map/all_to_all | solution.py:270
  86.6 1.0 copy-done.2
  89.6 2.2 %shard_map.52 = f32[16,136,128]{2,1,0:T(8,128)S(1)} custom-call(bf16[8,768,128]{2,1,0:T(8,128)(2,1)S(1)} %all-to-all-done.parts_ref, bf16[2,768,128]{2,1,0:T(8,128)(2,1)S(1)} %shard_map.48.refs_0_, bf16[2,768,128]{2,1,0:T(8,128)(2,1)S(1)} %collective-permute-done.5.refs_1_, bf16[2,768,128]{2,1,0:T(8,128)(2,1)S(1)} %collective-permute-done.10.refs_2_, ...), custom_call_target="tpu_custom_call" | custom-call | flops 805306368 | bytes 6291456 | tf_op jit(solution)/shard_map/pallas_call | solution.py:226
  91.9 23.6 %all_to_all.10 = f16[16,136,128]{2,1,0:T(8,128)(2,1)S(1)} all-to-all(f16[16,136,128]{2,1,0:T(8,128)(2,1)S(1)} %convert_element_type.20), channel_id=1, replica_groups={{0,32,192,224,128,160,64,96,16,48,208,240,144,176,80,112},{17,49,209,24..., dimensions={0} | all-to-all | bytes 1114112 | tf_op jit(solution)/shard_map/all_to_all | solution.py:272
  (49 shorter events, 14.2 us)
Async XLA Ops:
  1.9 16.4 %collective-permute-start.2 = (bf16[768,128]{1,0:T(8,128)(2,1)S(1)}, bf16[768,128]{1,0:T(8,128)(2,1)S(1)}, u32[]{:S(2)}, u32[]{:S(2)}) collective-permute-start(bf16[768,128]{1,0:T(8,128)(2,1)S(1)} %broadcast_multiply_fusion.one), channel_id=1, source_target_pairs={{0,2},{1,3},{2,0},{3,1},{4,6},{5,7},{6,4},{7,5},{8,10},{9,11},{10,... | collective-permute-start | bytes 589832 | tf_op jit(solution)/shard_map/ppermute | solution.py:31
  4.1 19.8 %collective-permute-start = (bf16[768,128]{1,0:T(8,128)(2,1)S(1)}, bf16[768,128]{1,0:T(8,128)(2,1)S(1)}, u32[]{:S(2)}, u32[]{:S(2)}) collective-permute-start(bf16[768,128]{1,0:T(8,128)(2,1)S(1)} %broadcast_multiply_fusion.one), channel_id=1, source_target_pairs={{0,0},{1,1},{2,2},{3,3},{4,224},{5,225},{6,226},{7,227},{8,192},{9... | collective-permute-start | bytes 589832 | tf_op jit(solution)/shard_map/ppermute | solution.py:31
  4.7 19.1 %collective-permute-start.1 = (bf16[768,128]{1,0:T(8,128)(2,1)S(1)}, bf16[768,128]{1,0:T(8,128)(2,1)S(1)}, u32[]{:S(2)}, u32[]{:S(2)}) collective-permute-start(bf16[768,128]{1,0:T(8,128)(2,1)S(1)} %broadcast_multiply_fusion.one), channel_id=1, source_target_pairs={{0,128},{1,129},{2,130},{3,131},{4,96},{5,97},{6,98},{7,99},{8,64}... | collective-permute-start | bytes 589832 | tf_op jit(solution)/shard_map/ppermute | solution.py:31
  15.5 1.3 %copy-start = (bf16[768,768]{1,0:T(8,128)(2,1)S(1)}, bf16[768,768]{1,0:T(8,128)(2,1)}, u32[]{:S(2)}) copy-start(bf16[768,768]{1,0:T(8,128)(2,1)} %value_ref.1) | copy-start | bytes 3538948
  18.4 29.6 %collective-permute-start.8 = (bf16[768,768]{1,0:T(8,128)(2,1)S(1)}, bf16[768,768]{1,0:T(8,128)(2,1)S(1)}, u32[]{:S(2)}, u32[]{:S(2)}) collective-permute-start(bf16[768,768]{1,0:T(8,128)(2,1)S(1)} %shard_map.46), channel_id=1, source_target_pairs={{0,0},{1,16},{2,2},{3,18},{4,4},{5,20},{6,6},{7,22},{8,8},{9,24},{... | collective-permute-start | bytes 3538952 | tf_op jit(solution)/shard_map/ppermute | solution.py:31
  20.3 27.6 %collective-permute-start.9 = (bf16[768,768]{1,0:T(8,128)(2,1)S(1)}, bf16[768,768]{1,0:T(8,128)(2,1)S(1)}, u32[]{:S(2)}, u32[]{:S(2)}) collective-permute-start(bf16[768,768]{1,0:T(8,128)(2,1)S(1)} %shard_map.46), channel_id=1, source_target_pairs={{0,2},{1,18},{2,0},{3,16},{4,6},{5,22},{6,4},{7,20},{8,10},{9,26},... | collective-permute-start | bytes 3538952 | tf_op jit(solution)/shard_map/ppermute | solution.py:31
  22.1 9.6 %collective-permute-start.5 = (bf16[2,768,128]{2,1,0:T(8,128)(2,1)S(1)}, bf16[2,768,128]{2,1,0:T(8,128)(2,1)S(1)}, u32[]{:S(2)}, u32[]{:S(2)}) collective-permute-start(bf16[2,768,128]{2,1,0:T(8,128)(2,1)S(1)} %shard_map.48.refs_0_), channel_id=1, source_target_pairs={{0,4},{1,5},{2,6},{3,7},{4,8},{5,9},{6,10},{7,11},{8,12},{9,13},{1... | collective-permute-start | bytes 1179656 | tf_op jit(solution)/shard_map/ppermute | solution.py:31
  23.9 11.3 %collective-permute-start.3 = (bf16[2,768,128]{2,1,0:T(8,128)(2,1)S(1)}, bf16[2,768,128]{2,1,0:T(8,128)(2,1)S(1)}, u32[]{:S(2)}, u32[]{:S(2)}) collective-permute-start(bf16[2,768,128]{2,1,0:T(8,128)(2,1)S(1)} %shard_map.47.own), channel_id=1, source_target_pairs={{0,32},{1,33},{2,34},{3,35},{4,36},{5,37},{6,38},{7,39},{8,40},{9,... | collective-permute-start | bytes 1179656 | tf_op jit(solution)/shard_map/ppermute | solution.py:31
  25.5 10.3 %collective-permute-start.4 = (bf16[2,768,128]{2,1,0:T(8,128)(2,1)S(1)}, bf16[2,768,128]{2,1,0:T(8,128)(2,1)S(1)}, u32[]{:S(2)}, u32[]{:S(2)}) collective-permute-start(bf16[2,768,128]{2,1,0:T(8,128)(2,1)S(1)} %shard_map.47.own), channel_id=1, source_target_pairs={{0,224},{1,225},{2,226},{3,227},{4,228},{5,229},{6,230},{7,231},{8... | collective-permute-start | bytes 1179656 | tf_op jit(solution)/shard_map/ppermute | solution.py:31
  35.8 11.5 %collective-permute-start.10 = (bf16[2,768,128]{2,1,0:T(8,128)(2,1)S(1)}, bf16[2,768,128]{2,1,0:T(8,128)(2,1)S(1)}, u32[]{:S(2)}, u32[]{:S(2)}) collective-permute-start(bf16[2,768,128]{2,1,0:T(8,128)(2,1)S(1)} %collective-permute-done.5.refs_1_), channel_id=1, source_target_pairs={{0,4},{1,5},{2,6},{3,7},{4,8},{5,9},{6,10},{7,11},{8,12},{9,13},{1... | collective-permute-start | bytes 1179656 | tf_op jit(solution)/shard_map/ppermute | solution.py:31
  38.1 7.2 %collective-permute-start.6 = (bf16[768,128]{1,0:T(8,128)(2,1)S(1)}, bf16[768,128]{1,0:T(8,128)(2,1)S(1)}, u32[]{:S(2)}, u32[]{:S(2)}) collective-permute-start(bf16[768,128]{1,0:T(8,128)(2,1)S(1)} %slice_bitcast_fusion.1), channel_id=1, source_target_pairs={{0,32},{1,33},{2,34},{3,35},{4,36},{5,37},{6,38},{7,39},{8,40},{9,... | collective-permute-start | bytes 589832 | tf_op jit(solution)/shard_map/ppermute | solution.py:31
  38.7 6.6 %collective-permute-start.7 = (bf16[768,128]{1,0:T(8,128)(2,1)S(1)}, bf16[768,128]{1,0:T(8,128)(2,1)S(1)}, u32[]{:S(2)}, u32[]{:S(2)}) collective-permute-start(bf16[768,128]{1,0:T(8,128)(2,1)S(1)} %slice_bitcast_fusion), channel_id=1, source_target_pairs={{0,224},{1,225},{2,226},{3,227},{4,228},{5,229},{6,230},{7,231},{8... | collective-permute-start | bytes 589832 | tf_op jit(solution)/shard_map/ppermute | solution.py:31
  48.0 4.4 %collective-permute-start.11 = (bf16[768,768]{1,0:T(8,128)(2,1)S(1)}, bf16[768,768]{1,0:T(8,128)(2,1)S(1)}, u32[]{:S(2)}, u32[]{:S(2)}) collective-permute-start(bf16[768,768]{1,0:T(8,128)(2,1)S(1)} %collective-permute-done.8.one), channel_id=1, source_target_pairs={{0,1},{1,0},{2,3},{3,2},{4,5},{5,4},{6,7},{7,6},{8,9},{9,8},{10,11... | collective-permute-start | bytes 3538952 | tf_op jit(solution)/shard_map/ppermute | solution.py:31
  48.0 4.5 %collective-permute-start.12 = (bf16[768,768]{1,0:T(8,128)(2,1)S(1)}, bf16[768,768]{1,0:T(8,128)(2,1)S(1)}, u32[]{:S(2)}, u32[]{:S(2)}) collective-permute-start(bf16[768,768]{1,0:T(8,128)(2,1)S(1)} %collective-permute-done.9.two), channel_id=1, source_target_pairs={{0,1},{1,0},{2,3},{3,2},{4,5},{5,4},{6,7},{7,6},{8,9},{9,8},{10,11... | collective-permute-start | bytes 3538952 | tf_op jit(solution)/shard_map/ppermute | solution.py:31
  48.5 12.2 %collective-permute-start.13 = (bf16[2,768,128]{2,1,0:T(8,128)(2,1)S(1)}, bf16[2,768,128]{2,1,0:T(8,128)(2,1)S(1)}, u32[]{:S(2)}, u32[]{:S(2)}) collective-permute-start(bf16[2,768,128]{2,1,0:T(8,128)(2,1)S(1)} %collective-permute-done.10.refs_2_), channel_id=1, source_target_pairs={{0,4},{1,5},{2,6},{3,7},{4,8},{5,9},{6,10},{7,11},{8,12},{9,13},{1... | collective-permute-start | bytes 1179656 | tf_op jit(solution)/shard_map/ppermute | solution.py:31
  60.7 25.9 %all-to-all-start = ((bf16[8,768,128]{2,1,0:T(8,128)(2,1)}), bf16[8,768,128]{2,1,0:T(8,128)(2,1)S(1)}, u32[]{:S(2)}, u32[]{:S(2)}) async-start(bf16[8,768,128]{2,1,0:T(8,128)(2,1)} %shard_map.51), calls=%async_computation | async-start | bytes 3145728 | tf_op jit(solution)/shard_map/all_to_all | solution.py:270
  67.6 1.7 %collective-permute-start.14 = (bf16[2,768,128]{2,1,0:T(8,128)(2,1)S(1)}, bf16[2,768,128]{2,1,0:T(8,128)(2,1)S(1)}, u32[]{:S(2)}, u32[]{:S(2)}) collective-permute-start(bf16[2,768,128]{2,1,0:T(8,128)(2,1)S(1)} %shard_map.48.refs_0_), channel_id=1, source_target_pairs={{0,1},{1,0},{2,3},{3,2},{4,5},{5,4},{6,7},{7,6},{8,9},{9,8},{10,11... | collective-permute-start | bytes 1179656 | tf_op jit(solution)/shard_map/ppermute | solution.py:31
  67.6 2.3 %collective-permute-start.15 = (bf16[2,768,128]{2,1,0:T(8,128)(2,1)S(1)}, bf16[2,768,128]{2,1,0:T(8,128)(2,1)S(1)}, u32[]{:S(2)}, u32[]{:S(2)}) collective-permute-start(bf16[2,768,128]{2,1,0:T(8,128)(2,1)S(1)} %collective-permute-done.5.refs_1_), channel_id=1, source_target_pairs={{0,1},{1,0},{2,3},{3,2},{4,5},{5,4},{6,7},{7,6},{8,9},{9,8},{10,11... | collective-permute-start | bytes 1179656 | tf_op jit(solution)/shard_map/ppermute | solution.py:31
  68.1 2.5 %collective-permute-start.16 = (bf16[2,768,128]{2,1,0:T(8,128)(2,1)S(1)}, bf16[2,768,128]{2,1,0:T(8,128)(2,1)S(1)}, u32[]{:S(2)}, u32[]{:S(2)}) collective-permute-start(bf16[2,768,128]{2,1,0:T(8,128)(2,1)S(1)} %collective-permute-done.10.refs_2_), channel_id=1, source_target_pairs={{0,1},{1,0},{2,3},{3,2},{4,5},{5,4},{6,7},{7,6},{8,9},{9,8},{10,11... | collective-permute-start | bytes 1179656 | tf_op jit(solution)/shard_map/ppermute | solution.py:31
  68.1 3.3 %collective-permute-start.17 = (bf16[2,768,128]{2,1,0:T(8,128)(2,1)S(1)}, bf16[2,768,128]{2,1,0:T(8,128)(2,1)S(1)}, u32[]{:S(2)}, u32[]{:S(2)}) collective-permute-start(bf16[2,768,128]{2,1,0:T(8,128)(2,1)S(1)} %collective-permute-done.13.refs_3_), channel_id=1, source_target_pairs={{0,1},{1,0},{2,3},{3,2},{4,5},{5,4},{6,7},{7,6},{8,9},{9,8},{10,11... | collective-permute-start | bytes 1179656 | tf_op jit(solution)/shard_map/ppermute | solution.py:31
  71.4 0.8 copy-start.5
  86.6 1.0 copy-start.2
  87.6 1.0 copy-start.4
  88.6 1.0 copy-start.6
  (3 other events, 2.2 us)

commit v4 on v3

--- a/solution.py
+++ b/solution.py
@@ -101,6 +101,7 @@
 
 VMEM = pl.BlockSpec(memory_space=pltpu.VMEM)
 SMEM = pl.BlockSpec(memory_space=pltpu.SMEM)
+ANY = pl.BlockSpec(memory_space=pl.ANY)
 
 
 def on_device(kernel, shape, dtype, specs, scratch=(), cost=None, grant=1):
@@ -119,22 +120,37 @@
     return jnp.dot(a, b, preferred_element_type=jnp.float32)
 
 
-def masked(value, pattern):
-    wide = jnp.repeat(jnp.repeat(pattern, BLOCK, axis=0), BLOCK, axis=1)
-    return value * wide.astype(value.dtype)
-
-
-def mask_kernel(token_ref, pattern_ref, value_ref, out_ref):
-    for i in range(pattern_ref.shape[0]):
-        for j in range(pattern_ref.shape[1]):
-            spot = (slice(i * BLOCK, (i + 1) * BLOCK), slice(j * BLOCK, (j + 1) * BLOCK))
-            value = value_ref[spot]
-            out_ref[spot] = jnp.where(pattern_ref[i, j] != 0, value, jnp.zeros_like(value))
-
-
-def masked_tile(token, value, pattern):
-    cost = pl.CostEstimate(flops=value.size, bytes_accessed=4 * value.size, transcendentals=0)
-    return on_device(mask_kernel, value.shape, value.dtype, [SMEM, SMEM, VMEM], cost=cost)(token, pattern, value)
+def mask_kernel(p_any, a_any, p_pattern, a_pattern, p_out, a_out, p_stored, a_stored, sems):
+    moves = [(p_pattern, p_stored), (p_any, p_out), (a_pattern, a_stored), (a_any, a_out)]
+    copies = [pltpu.make_async_copy(*move, sems.at[i]) for i, move in enumerate(moves)]
+    for copy in copies:
+        copy.start()
+    for first, stored, out_ref in ((0, p_stored, p_out), (2, a_stored, a_out)):
+        copies[first].wait()
+        copies[first + 1].wait()
+        for i in range(out_ref.shape[0] // BLOCK):
+            rows = slice(i * BLOCK, (i + 1) * BLOCK)
+            for j in range(out_ref.shape[1] // BLOCK):
+                columns = slice(j * BLOCK, (j + 1) * BLOCK)
+                kept = stored[:, i : i + 1] if first == 0 else stored[i : i + 1, j : j + 1]
+                kept = jnp.broadcast_to(kept.astype(jnp.float32), (BLOCK, BLOCK))
+                out_ref[rows, columns] = out_ref[rows, columns] * kept.astype(out_ref.dtype)
+
+
+def masked(prolong, a_matrix, p_pattern, a_pattern):
+    return pl.pallas_call(
+        mask_kernel,
+        out_shape=[jax.ShapeDtypeStruct(v.shape, v.dtype) for v in (prolong, a_matrix)],
+        in_specs=[ANY] * 4,
+        out_specs=[VMEM, VMEM],
+        scratch_shapes=[
+            pltpu.VMEM(p_pattern.shape[::-1], p_pattern.dtype),
+            pltpu.VMEM(a_pattern.shape, a_pattern.dtype),
+            pltpu.SemaphoreType.DMA((4,)),
+        ],
+        compiler_params=pltpu.CompilerParams(vmem_limit_bytes=61 << 20),
+        cost_estimate=pl.CostEstimate(flops=a_matrix.size, bytes_accessed=4 << 20, transcendentals=0),
+    )(prolong, a_matrix, p_pattern.T, a_pattern)
 
 
 def pair_kernel(one, two, out_ref):
@@ -246,15 +262,12 @@
 def local(a_matrix, prolong, a_pattern, p_pattern):
     row, col = lax.axis_index("row"), lax.axis_index("col")
     spot = jnp.stack([row // 2, col // 4, (col // 2) % 2]).astype(jnp.int32)
-    p_eff = masked(prolong, p_pattern)
-    p_eff, spot = both(p_eff, spot)
+    p_eff, a_eff = masked(prolong, a_matrix, p_pattern, a_pattern)
     first, second = send(p_eff, turn), send(p_eff, turn_far)
     across = send(p_eff, far_x)
-    a_eff = masked_tile(spot, a_matrix, a_pattern)
-    a_eff, across = both(a_eff, across)
     near, distant = send(a_eff, swap), send(a_eff, swap_far)
     pair = paired(p_eff, across)
-    first, second, _ = both(first, second, a_eff)
+    first, second, spot = both(first, second, spot)
     own = paired(first, second)
     below, above, pair_1 = both(send(own, z_up), send(own, z_down), send(pair, y_up))
     pair_2 = send(pair_1, y_up)

time: 117 us -> 118 us (level)
  waiting for transfers between devices: 36.4 us -> 42.8 us
  starting transfers between devices: 38.3 us -> 33.2 us
  Pallas kernels: 7.85 us -> 10.8 us
  local copies, waits for them, and re-layouts: 8.04 us -> 5.19 us
  other arithmetic: 2.32 us -> 0.57 us
  blocking collectives: 23.6 us -> 25.1 us
    ppermute x18, waiting for transfers between devices: 21.9 us -> 28.3 us  [send(): return lax.ppermute(value, AXES, pairs)]
    unnamed x16 -> x14, local copies, waits for them, and re-layouts: 7.21 us -> 4.44 us
    all_to_all x1, starting transfers between devices: 6.89 us -> 4.17 us  [local(): lax.all_to_all(w_part, AXES, 0, 0, axis_index_groups=W_GROUPS, tiled=True)]
    ppermute x18, starting transfers between devices: 31.4 us -> 29 us  [send(): return lax.ppermute(value, AXES, pairs)]
    pallas_call x1, Pallas kernels: 0.87 us -> 2.79 us  [masked(): pl.pallas_call(mask_kernel, out_shape=[jax.ShapeDtypeStruct(v.shape, v.dt...]
    all_to_all x1, blocking collectives: 23.6 us -> 25.1 us  [local(): lax.all_to_all(c_part, AXES, 0, 0, axis_index_groups=C_GROUPS, tiled=True)]
  transfers between devices with their start and end apart: 19 -> 19, of which waited for: 11 -> 12; matrix products, arithmetic and copies ran while one was open for 0% -> 0% of each run, Pallas kernels for 5% -> 4%
where the time goes in v4:
time: 118 us
  waiting for transfers between devices  42.8 us (36%)
  starting transfers between devices  33.2 us (28%)
  blocking collectives  25.1 us (21%)
  Pallas kernels  10.8 us (9%)
  local copies, waits for them, and re-layouts  5.19 us (4%)
    ppermute x18, starting transfers between devices, send(): return lax.ppermute(value, AXES, pairs)  29 us
    ppermute x18, waiting for transfers between devices, send(): return lax.ppermute(value, AXES, pairs)  28.3 us
    all_to_all x1, blocking collectives, local(): lax.all_to_all(c_part, AXES, 0, 0, axis_index_groups=C_GROUPS, tiled=True)  25.1 us
    all_to_all x1, waiting for transfers between devices, local(): lax.all_to_all(w_part, AXES, 0, 0, axis_index_groups=W_GROUPS, tiled=True)  14.5 us
    unnamed x14, local copies, waits for them, and re-layouts  4.44 us
    all_to_all x1, starting transfers between devices, local(): lax.all_to_all(w_part, AXES, 0, 0, axis_index_groups=W_GROUPS, tiled=True)  4.17 us
    pallas_call x2, Pallas kernels, w_products(): on_device(functools.partial(w_kernel, LANES * len(before)), (LANES * (1 +...  3.93 us
    pallas_call x1, Pallas kernels, c_products(): on_device(c_kernel, (4 * LANES, BLOCK + 8, BLOCK), jnp.float32, [VMEM] *...  3.17 us
  transfers between devices with their start and end apart: 19, of which 12 were waited for; matrix products, arithmetic and copies ran while one was open for 0% of the time, Pallas kernels for 4%

profile of v4, /device:TPU:2, one launch (start us, length us, event | category | flops | bytes accessed | tf_op | source)
XLA Modules:
  0.0 117.7 jit_solution(4633330652376400379)
XLA Ops:
  0.0 2.8 %shard_map.46 = (bf16[768,128]{1,0:T(8,128)(2,1)}, bf16[768,768]{1,0:T(8,128)(2,1)}) custom-call(bf16[768,128]{1,0:T(8,128)(2,1)} %p_any.1, bf16[768,768]{1,0:T(8,128)(2,1)} %a_any.1, s32[1,6]{1,0:T(1,128)} %bitcast.10, s32[6,6]{1,0:T(8,128)} %a_pattern.1), custom_call_target="tpu_custom_call" | custom-call | flops 589824 | bytes 4194304 | tf_op jit(solution)/shard_map/pallas_call | solution.py:141
  2.8 1.6 %collective-permute-start = (bf16[768,128]{1,0:T(8,128)(2,1)}, bf16[768,128]{1,0:T(8,128)(2,1)S(1)}, u32[]{:S(2)}, u32[]{:S(2)}) collective-permute-start(bf16[768,128]{1,0:T(8,128)(2,1)} %get-tuple-element.23.one), channel_id=1, source_target_pairs={{0,0},{1,1},{2,2},{3,3},{4,224},{5,225},{6,226},{7,227},{8,192},{9... | collective-permute-start | bytes 589832 | tf_op jit(solution)/shard_map/ppermute | solution.py:31
  4.4 9.9 %collective-permute-start.1 = (bf16[768,128]{1,0:T(8,128)(2,1)}, bf16[768,128]{1,0:T(8,128)(2,1)S(1)}, u32[]{:S(2)}, u32[]{:S(2)}) collective-permute-start(bf16[768,128]{1,0:T(8,128)(2,1)} %get-tuple-element.23.one), channel_id=1, source_target_pairs={{0,128},{1,129},{2,130},{3,131},{4,96},{5,97},{6,98},{7,99},{8,64}... | collective-permute-start | bytes 589832 | tf_op jit(solution)/shard_map/ppermute | solution.py:31
  14.3 2.1 %collective-permute-start.4 = (bf16[768,128]{1,0:T(8,128)(2,1)}, bf16[768,128]{1,0:T(8,128)(2,1)S(1)}, u32[]{:S(2)}, u32[]{:S(2)}) collective-permute-start(bf16[768,128]{1,0:T(8,128)(2,1)} %get-tuple-element.23.one), channel_id=1, source_target_pairs={{0,2},{1,3},{2,0},{3,1},{4,6},{5,7},{6,4},{7,5},{8,10},{9,11},{10,... | collective-permute-start | bytes 589832 | tf_op jit(solution)/shard_map/ppermute | solution.py:31
  16.4 1.9 %collective-permute-start.8 = (bf16[768,768]{1,0:T(8,128)(2,1)}, bf16[768,768]{1,0:T(8,128)(2,1)S(1)}, u32[]{:S(2)}, u32[]{:S(2)}) collective-permute-start(bf16[768,768]{1,0:T(8,128)(2,1)} %get-tuple-element.29), channel_id=1, source_target_pairs={{0,0},{1,16},{2,2},{3,18},{4,4},{5,20},{6,6},{7,22},{8,8},{9,24},{... | collective-permute-start | bytes 3538952 | tf_op jit(solution)/shard_map/ppermute | solution.py:31
  18.3 1.7 %collective-permute-start.9 = (bf16[768,768]{1,0:T(8,128)(2,1)}, bf16[768,768]{1,0:T(8,128)(2,1)S(1)}, u32[]{:S(2)}, u32[]{:S(2)}) collective-permute-start(bf16[768,768]{1,0:T(8,128)(2,1)} %get-tuple-element.29), channel_id=1, source_target_pairs={{0,2},{1,18},{2,0},{3,16},{4,6},{5,22},{6,4},{7,20},{8,10},{9,26},... | collective-permute-start | bytes 3538952 | tf_op jit(solution)/shard_map/ppermute | solution.py:31
  20.1 2.5 %collective-permute-done.1.two = bf16[768,128]{1,0:T(8,128)(2,1)S(1)} collective-permute-done((bf16[768,128]{1,0:T(8,128)(2,1)}, bf16[768,128]{1,0:T(8,128)(2,1)S(1)}, u32[]{:S(2)}, u32[]{:S(2)}) %collective-permute-start.1) | collective-permute-done | bytes 196640 | tf_op jit(solution)/shard_map/ppermute | solution.py:31
  22.7 1.2 %collective-permute-start.2 = (bf16[2,768,128]{2,1,0:T(8,128)(2,1)S(1)}, bf16[2,768,128]{2,1,0:T(8,128)(2,1)S(1)}, u32[]{:S(2)}, u32[]{:S(2)}) collective-permute-start(bf16[2,768,128]{2,1,0:T(8,128)(2,1)S(1)} %shard_map.47.own), channel_id=1, source_target_pairs={{0,32},{1,33},{2,34},{3,35},{4,36},{5,37},{6,38},{7,39},{8,40},{9,... | collective-permute-start | bytes 1179656 | tf_op jit(solution)/shard_map/ppermute | solution.py:31
  23.9 2.5 %collective-permute-start.3 = (bf16[2,768,128]{2,1,0:T(8,128)(2,1)S(1)}, bf16[2,768,128]{2,1,0:T(8,128)(2,1)S(1)}, u32[]{:S(2)}, u32[]{:S(2)}) collective-permute-start(bf16[2,768,128]{2,1,0:T(8,128)(2,1)S(1)} %shard_map.47.own), channel_id=1, source_target_pairs={{0,224},{1,225},{2,226},{3,227},{4,228},{5,229},{6,230},{7,231},{8... | collective-permute-start | bytes 1179656 | tf_op jit(solution)/shard_map/ppermute | solution.py:31
  27.7 7.0 %collective-permute-done.2.below = bf16[2,768,128]{2,1,0:T(8,128)(2,1)S(1)} collective-permute-done((bf16[2,768,128]{2,1,0:T(8,128)(2,1)S(1)}, bf16[2,768,128]{2,1,0:T(8,128)(2,1)S(1)}, u32[]{:S(2)}, u32[]{:S(2)}) %collective-permute-start.2) | collective-permute-done | bytes 393248 | tf_op jit(solution)/shard_map/ppermute | solution.py:31
  35.1 3.7 %collective-permute-done.5.refs_1_ = bf16[2,768,128]{2,1,0:T(8,128)(2,1)S(1)} collective-permute-done((bf16[2,768,128]{2,1,0:T(8,128)(2,1)S(1)}, bf16[2,768,128]{2,1,0:T(8,128)(2,1)S(1)}, u32[]{:S(2)}, u32[]{:S(2)}) %collective-permute-start.5) | collective-permute-done | bytes 393248 | tf_op jit(solution)/shard_map/ppermute | solution.py:31
  38.8 2.0 %collective-permute-start.10 = (bf16[2,768,128]{2,1,0:T(8,128)(2,1)S(1)}, bf16[2,768,128]{2,1,0:T(8,128)(2,1)S(1)}, u32[]{:S(2)}, u32[]{:S(2)}) collective-permute-start(bf16[2,768,128]{2,1,0:T(8,128)(2,1)S(1)} %collective-permute-done.5.refs_1_), channel_id=1, source_target_pairs={{0,4},{1,5},{2,6},{3,7},{4,8},{5,9},{6,10},{7,11},{8,12},{9,13},{1... | collective-permute-start | bytes 1179656 | tf_op jit(solution)/shard_map/ppermute | solution.py:31
  41.0 3.3 %collective-permute-start.7 = (bf16[768,128]{1,0:T(8,128)(2,1)S(1)}, bf16[768,128]{1,0:T(8,128)(2,1)S(1)}, u32[]{:S(2)}, u32[]{:S(2)}) collective-permute-start(bf16[768,128]{1,0:T(8,128)(2,1)S(1)} %slice_bitcast_fusion), channel_id=1, source_target_pairs={{0,224},{1,225},{2,226},{3,227},{4,228},{5,229},{6,230},{7,231},{8... | collective-permute-start | bytes 589832 | tf_op jit(solution)/shard_map/ppermute | solution.py:31
  44.3 3.5 %collective-permute-done.6.up_two = bf16[768,128]{1,0:T(8,128)(2,1)S(1)} collective-permute-done((bf16[768,128]{1,0:T(8,128)(2,1)S(1)}, bf16[768,128]{1,0:T(8,128)(2,1)S(1)}, u32[]{:S(2)}, u32[]{:S(2)}) %collective-permute-start.6) | collective-permute-done | bytes 196640 | tf_op jit(solution)/shard_map/ppermute | solution.py:31
  47.8 1.8 %collective-permute-done.10.refs_2_ = bf16[2,768,128]{2,1,0:T(8,128)(2,1)S(1)} collective-permute-done((bf16[2,768,128]{2,1,0:T(8,128)(2,1)S(1)}, bf16[2,768,128]{2,1,0:T(8,128)(2,1)S(1)}, u32[]{:S(2)}, u32[]{:S(2)}) %collective-permute-start.10) | collective-permute-done | bytes 393248 | tf_op jit(solution)/shard_map/ppermute | solution.py:31
  51.8 1.4 %shard_map.50.rest_0_ = bf16[4,768,128]{2,1,0:T(8,128)(2,1)S(1)} custom-call(bf16[2,768,512]{2,1,0:T(8,128)(2,1)S(1)} %shard_map.49.p_ref, bf16[768,768]{1,0:T(8,128)(2,1)S(1)} %collective-permute-done.8.one, bf16[768,768]{1,0:T(8,128)(2,1)S(1)} %collective-permute-done.9.two), custom_call_target="tpu_custom_call" | custom-call | flops 1207959552 | bytes 6291456 | tf_op jit(solution)/shard_map/pallas_call | solution.py:204
  53.2 1.1 collective-permute-done.12.two
  54.2 2.5 %shard_map.51 = bf16[8,768,128]{2,1,0:T(8,128)(2,1)} custom-call(bf16[2,768,512]{2,1,0:T(8,128)(2,1)S(1)} %shard_map.49.p_ref, bf16[768,768]{1,0:T(8,128)(2,1)S(1)} %collective-permute-done.11.one, bf16[768,768]{1,0:T(8,128)(2,1)S(1)} %collective-permute-done.12.two, bf16[4,768,128]{2,1,0:T(8,128)(2,1)S(1)} %shard_map.50.rest_0_), custom_call_target="tpu_custom_call" | custom-call | flops 1207959552 | bytes 6291456 | tf_op jit(solution)/shard_map/pallas_call | solution.py:204
  56.8 5.9 %collective-permute-done.13.refs_3_ = bf16[2,768,128]{2,1,0:T(8,128)(2,1)} collective-permute-done((bf16[2,768,128]{2,1,0:T(8,128)(2,1)S(1)}, bf16[2,768,128]{2,1,0:T(8,128)(2,1)}, u32[]{:S(2)}, u32[]{:S(2)}) %collective-permute-start.13) | collective-permute-done | bytes 393248 | tf_op jit(solution)/shard_map/ppermute | solution.py:31
  62.6 4.2 %all-to-all-start = ((bf16[8,768,128]{2,1,0:T(8,128)(2,1)}), bf16[8,768,128]{2,1,0:T(8,128)(2,1)S(1)}, u32[]{:S(2)}, u32[]{:S(2)}) async-start(bf16[8,768,128]{2,1,0:T(8,128)(2,1)} %shard_map.51), calls=%async_computation | async-start | bytes 3145728 | tf_op jit(solution)/shard_map/all_to_all | solution.py:283
  68.5 1.1 collective-permute-done.15.refs_5_
  71.7 14.5 %all-to-all-done.parts_ref = bf16[8,768,128]{2,1,0:T(8,128)(2,1)S(1)} async-done(((bf16[8,768,128]{2,1,0:T(8,128)(2,1)}), bf16[8,768,128]{2,1,0:T(8,128)(2,1)S(1)}, u32[]{:S(2)}, u32[]{:S(2)}) %all-to-all-start) | async-done | bytes 1572896 | tf_op jit(solution)/shard_map/all_to_all | solution.py:283
  88.3 3.2 %shard_map.52 = f32[16,136,128]{2,1,0:T(8,128)S(1)} custom-call(bf16[8,768,128]{2,1,0:T(8,128)(2,1)S(1)} %all-to-all-done.parts_ref, bf16[2,768,128]{2,1,0:T(8,128)(2,1)S(1)} %shard_map.48.refs_0_, bf16[2,768,128]{2,1,0:T(8,128)(2,1)S(1)} %collective-permute-done.5.refs_1_, bf16[2,768,128]{2,1,0:T(8,128)(2,1)S(1)} %copy-done.1, ...), custom_call_target="tpu_custom_call" | custom-call | flops 805306368 | bytes 6291456 | tf_op jit(solution)/shard_map/pallas_call | solution.py:242
  91.5 25.1 %all_to_all.10 = f16[16,136,128]{2,1,0:T(8,128)(2,1)S(1)} all-to-all(f16[16,136,128]{2,1,0:T(8,128)(2,1)S(1)} %convert_element_type.6), channel_id=1, replica_groups={{0,32,192,224,128,160,64,96,16,48,208,240,144,176,80,112},{17,49,209,24..., dimensions={0} | all-to-all | bytes 1114112 | tf_op jit(solution)/shard_map/all_to_all | solution.py:285
  (44 shorter events, 11.1 us)
Async XLA Ops:
  2.8 17.4 %collective-permute-start = (bf16[768,128]{1,0:T(8,128)(2,1)}, bf16[768,128]{1,0:T(8,128)(2,1)S(1)}, u32[]{:S(2)}, u32[]{:S(2)}) collective-permute-start(bf16[768,128]{1,0:T(8,128)(2,1)} %get-tuple-element.23.one), channel_id=1, source_target_pairs={{0,0},{1,1},{2,2},{3,3},{4,224},{5,225},{6,226},{7,227},{8,192},{9... | collective-permute-start | bytes 589832 | tf_op jit(solution)/shard_map/ppermute | solution.py:31
  4.4 18.3 %collective-permute-start.1 = (bf16[768,128]{1,0:T(8,128)(2,1)}, bf16[768,128]{1,0:T(8,128)(2,1)S(1)}, u32[]{:S(2)}, u32[]{:S(2)}) collective-permute-start(bf16[768,128]{1,0:T(8,128)(2,1)} %get-tuple-element.23.one), channel_id=1, source_target_pairs={{0,128},{1,129},{2,130},{3,131},{4,96},{5,97},{6,98},{7,99},{8,64}... | collective-permute-start | bytes 589832 | tf_op jit(solution)/shard_map/ppermute | solution.py:31
  14.3 12.2 %collective-permute-start.4 = (bf16[768,128]{1,0:T(8,128)(2,1)}, bf16[768,128]{1,0:T(8,128)(2,1)S(1)}, u32[]{:S(2)}, u32[]{:S(2)}) collective-permute-start(bf16[768,128]{1,0:T(8,128)(2,1)} %get-tuple-element.23.one), channel_id=1, source_target_pairs={{0,2},{1,3},{2,0},{3,1},{4,6},{5,7},{6,4},{7,5},{8,10},{9,11},{10,... | collective-permute-start | bytes 589832 | tf_op jit(solution)/shard_map/ppermute | solution.py:31
  16.4 33.2 %collective-permute-start.8 = (bf16[768,768]{1,0:T(8,128)(2,1)}, bf16[768,768]{1,0:T(8,128)(2,1)S(1)}, u32[]{:S(2)}, u32[]{:S(2)}) collective-permute-start(bf16[768,768]{1,0:T(8,128)(2,1)} %get-tuple-element.29), channel_id=1, source_target_pairs={{0,0},{1,16},{2,2},{3,18},{4,4},{5,20},{6,6},{7,22},{8,8},{9,24},{... | collective-permute-start | bytes 3538952 | tf_op jit(solution)/shard_map/ppermute | solution.py:31
  18.3 31.3 %collective-permute-start.9 = (bf16[768,768]{1,0:T(8,128)(2,1)}, bf16[768,768]{1,0:T(8,128)(2,1)S(1)}, u32[]{:S(2)}, u32[]{:S(2)}) collective-permute-start(bf16[768,768]{1,0:T(8,128)(2,1)} %get-tuple-element.29), channel_id=1, source_target_pairs={{0,2},{1,18},{2,0},{3,16},{4,6},{5,22},{6,4},{7,20},{8,10},{9,26},... | collective-permute-start | bytes 3538952 | tf_op jit(solution)/shard_map/ppermute | solution.py:31
  22.7 12.0 %collective-permute-start.2 = (bf16[2,768,128]{2,1,0:T(8,128)(2,1)S(1)}, bf16[2,768,128]{2,1,0:T(8,128)(2,1)S(1)}, u32[]{:S(2)}, u32[]{:S(2)}) collective-permute-start(bf16[2,768,128]{2,1,0:T(8,128)(2,1)S(1)} %shard_map.47.own), channel_id=1, source_target_pairs={{0,32},{1,33},{2,34},{3,35},{4,36},{5,37},{6,38},{7,39},{8,40},{9,... | collective-permute-start | bytes 1179656 | tf_op jit(solution)/shard_map/ppermute | solution.py:31
  23.9 11.2 %collective-permute-start.3 = (bf16[2,768,128]{2,1,0:T(8,128)(2,1)S(1)}, bf16[2,768,128]{2,1,0:T(8,128)(2,1)S(1)}, u32[]{:S(2)}, u32[]{:S(2)}) collective-permute-start(bf16[2,768,128]{2,1,0:T(8,128)(2,1)S(1)} %shard_map.47.own), channel_id=1, source_target_pairs={{0,224},{1,225},{2,226},{3,227},{4,228},{5,229},{6,230},{7,231},{8... | collective-permute-start | bytes 1179656 | tf_op jit(solution)/shard_map/ppermute | solution.py:31
  26.5 0.9 copy-start.6
  27.4 11.4 %collective-permute-start.5 = (bf16[2,768,128]{2,1,0:T(8,128)(2,1)S(1)}, bf16[2,768,128]{2,1,0:T(8,128)(2,1)S(1)}, u32[]{:S(2)}, u32[]{:S(2)}) collective-permute-start(bf16[2,768,128]{2,1,0:T(8,128)(2,1)S(1)} %shard_map.48.refs_0_), channel_id=1, source_target_pairs={{0,4},{1,5},{2,6},{3,7},{4,8},{5,9},{6,10},{7,11},{8,12},{9,13},{1... | collective-permute-start | bytes 1179656 | tf_op jit(solution)/shard_map/ppermute | solution.py:31
  38.8 10.8 %collective-permute-start.10 = (bf16[2,768,128]{2,1,0:T(8,128)(2,1)S(1)}, bf16[2,768,128]{2,1,0:T(8,128)(2,1)S(1)}, u32[]{:S(2)}, u32[]{:S(2)}) collective-permute-start(bf16[2,768,128]{2,1,0:T(8,128)(2,1)S(1)} %collective-permute-done.5.refs_1_), channel_id=1, source_target_pairs={{0,4},{1,5},{2,6},{3,7},{4,8},{5,9},{6,10},{7,11},{8,12},{9,13},{1... | collective-permute-start | bytes 1179656 | tf_op jit(solution)/shard_map/ppermute | solution.py:31
  40.9 7.0 %collective-permute-start.6 = (bf16[768,128]{1,0:T(8,128)(2,1)S(1)}, bf16[768,128]{1,0:T(8,128)(2,1)S(1)}, u32[]{:S(2)}, u32[]{:S(2)}) collective-permute-start(bf16[768,128]{1,0:T(8,128)(2,1)S(1)} %slice_bitcast_fusion.1), channel_id=1, source_target_pairs={{0,32},{1,33},{2,34},{3,35},{4,36},{5,37},{6,38},{7,39},{8,40},{9,... | collective-permute-start | bytes 589832 | tf_op jit(solution)/shard_map/ppermute | solution.py:31
  41.0 6.8 %collective-permute-start.7 = (bf16[768,128]{1,0:T(8,128)(2,1)S(1)}, bf16[768,128]{1,0:T(8,128)(2,1)S(1)}, u32[]{:S(2)}, u32[]{:S(2)}) collective-permute-start(bf16[768,128]{1,0:T(8,128)(2,1)S(1)} %slice_bitcast_fusion), channel_id=1, source_target_pairs={{0,224},{1,225},{2,226},{3,227},{4,228},{5,229},{6,230},{7,231},{8... | collective-permute-start | bytes 589832 | tf_op jit(solution)/shard_map/ppermute | solution.py:31
  49.6 2.2 %copy-start = (bf16[2,768,128]{2,1,0:T(8,128)(2,1)}, bf16[2,768,128]{2,1,0:T(8,128)(2,1)S(1)}, u32[]{:S(2)}) copy-start(bf16[2,768,128]{2,1,0:T(8,128)(2,1)S(1)} %collective-permute-done.10.refs_2_) | copy-start | bytes 1179652
  49.6 3.6 %collective-permute-start.11 = (bf16[768,768]{1,0:T(8,128)(2,1)S(1)}, bf16[768,768]{1,0:T(8,128)(2,1)S(1)}, u32[]{:S(2)}, u32[]{:S(2)}) collective-permute-start(bf16[768,768]{1,0:T(8,128)(2,1)S(1)} %collective-permute-done.8.one), channel_id=1, source_target_pairs={{0,1},{1,0},{2,3},{3,2},{4,5},{5,4},{6,7},{7,6},{8,9},{9,8},{10,11... | collective-permute-start | bytes 3538952 | tf_op jit(solution)/shard_map/ppermute | solution.py:31
  49.7 4.5 %collective-permute-start.12 = (bf16[768,768]{1,0:T(8,128)(2,1)S(1)}, bf16[768,768]{1,0:T(8,128)(2,1)S(1)}, u32[]{:S(2)}, u32[]{:S(2)}) collective-permute-start(bf16[768,768]{1,0:T(8,128)(2,1)S(1)} %collective-permute-done.9.two), channel_id=1, source_target_pairs={{0,1},{1,0},{2,3},{3,2},{4,5},{5,4},{6,7},{7,6},{8,9},{9,8},{10,11... | collective-permute-start | bytes 3538952 | tf_op jit(solution)/shard_map/ppermute | solution.py:31
  50.2 12.4 %collective-permute-start.13 = (bf16[2,768,128]{2,1,0:T(8,128)(2,1)S(1)}, bf16[2,768,128]{2,1,0:T(8,128)(2,1)}, u32[]{:S(2)}, u32[]{:S(2)}) collective-permute-start(bf16[2,768,128]{2,1,0:T(8,128)(2,1)S(1)} %collective-permute-done.10.refs_2_), channel_id=1, source_target_pairs={{0,4},{1,5},{2,6},{3,7},{4,8},{5,9},{6,10},{7,11},{8,12},{9,13},{1... | collective-permute-start | bytes 1179656 | tf_op jit(solution)/shard_map/ppermute | solution.py:31
  56.8 10.5 %copy-start.1 = (bf16[2,768,128]{2,1,0:T(8,128)(2,1)S(1)}, bf16[2,768,128]{2,1,0:T(8,128)(2,1)}, u32[]{:S(2)}) copy-start(bf16[2,768,128]{2,1,0:T(8,128)(2,1)} %copy-done) | copy-start | bytes 1179652
  62.6 23.6 %all-to-all-start = ((bf16[8,768,128]{2,1,0:T(8,128)(2,1)}), bf16[8,768,128]{2,1,0:T(8,128)(2,1)S(1)}, u32[]{:S(2)}, u32[]{:S(2)}) async-start(bf16[8,768,128]{2,1,0:T(8,128)(2,1)} %shard_map.51), calls=%async_computation | async-start | bytes 3145728 | tf_op jit(solution)/shard_map/all_to_all | solution.py:283
  66.8 1.7 %collective-permute-start.14 = (bf16[2,768,128]{2,1,0:T(8,128)(2,1)S(1)}, bf16[2,768,128]{2,1,0:T(8,128)(2,1)S(1)}, u32[]{:S(2)}, u32[]{:S(2)}) collective-permute-start(bf16[2,768,128]{2,1,0:T(8,128)(2,1)S(1)} %shard_map.48.refs_0_), channel_id=1, source_target_pairs={{0,1},{1,0},{2,3},{3,2},{4,5},{5,4},{6,7},{7,6},{8,9},{9,8},{10,11... | collective-permute-start | bytes 1179656 | tf_op jit(solution)/shard_map/ppermute | solution.py:31
  66.8 2.8 %collective-permute-start.15 = (bf16[2,768,128]{2,1,0:T(8,128)(2,1)S(1)}, bf16[2,768,128]{2,1,0:T(8,128)(2,1)S(1)}, u32[]{:S(2)}, u32[]{:S(2)}) collective-permute-start(bf16[2,768,128]{2,1,0:T(8,128)(2,1)S(1)} %collective-permute-done.5.refs_1_), channel_id=1, source_target_pairs={{0,1},{1,0},{2,3},{3,2},{4,5},{5,4},{6,7},{7,6},{8,9},{9,8},{10,11... | collective-permute-start | bytes 1179656 | tf_op jit(solution)/shard_map/ppermute | solution.py:31
  67.3 2.9 %collective-permute-start.16 = (bf16[2,768,128]{2,1,0:T(8,128)(2,1)S(1)}, bf16[2,768,128]{2,1,0:T(8,128)(2,1)S(1)}, u32[]{:S(2)}, u32[]{:S(2)}) collective-permute-start(bf16[2,768,128]{2,1,0:T(8,128)(2,1)S(1)} %copy-done.1), channel_id=1, source_target_pairs={{0,1},{1,0},{2,3},{3,2},{4,5},{5,4},{6,7},{7,6},{8,9},{9,8},{10,11... | collective-permute-start | bytes 1179656 | tf_op jit(solution)/shard_map/ppermute | solution.py:31
  67.3 3.6 %collective-permute-start.17 = (bf16[2,768,128]{2,1,0:T(8,128)(2,1)}, bf16[2,768,128]{2,1,0:T(8,128)(2,1)S(1)}, u32[]{:S(2)}, u32[]{:S(2)}) collective-permute-start(bf16[2,768,128]{2,1,0:T(8,128)(2,1)} %collective-permute-done.13.refs_3_), channel_id=1, source_target_pairs={{0,1},{1,0},{2,3},{3,2},{4,5},{5,4},{6,7},{7,6},{8,9},{9,8},{10,11... | collective-permute-start | bytes 1179656 | tf_op jit(solution)/shard_map/ppermute | solution.py:31
  86.3 1.0 copy-start.3
  87.3 1.0 copy-start.5
  (2 other events, 1.5 us)

commit v5 on v4

--- a/solution.py
+++ b/solution.py
@@ -267,18 +267,18 @@
     across = send(p_eff, far_x)
     near, distant = send(a_eff, swap), send(a_eff, swap_far)
     pair = paired(p_eff, across)
-    first, second, spot = both(first, second, spot)
+    first, second, spot, pair = both(first, second, spot, pair)
     own = paired(first, second)
     below, above, pair_1 = both(send(own, z_up), send(own, z_down), send(pair, y_up))
-    pair_2 = send(pair_1, y_up)
+    pair_3 = send(pair, y_down)
     up_two, down_two = send(below[0], z_up), send(above[0], z_down)
-    up_two, down_two, near, distant, pair_2 = both(up_two, down_two, near, distant, pair_2)
-    pair_3 = send(pair_2, y_up)
+    up_two, down_two, near, distant, pair_3, pair_1 = both(up_two, down_two, near, distant, pair_3, pair_1)
+    beyond = send(pair_1[0], y_up), send(pair_3[1], y_down)
     p_all = line_up(spot, own, above, below, up_two, down_two)
     near_2, distant_2 = send(near, other_core), send(distant, other_core)
     w_part = w_products(p_all, near, distant)
     w_part = w_products(p_all, near_2, distant_2, w_part)
-    w_part, *pairs = both(w_part, pair, pair_1, pair_2, pair_3)
+    w_part, *pairs = both(w_part, pair, pair_1, paired(*beyond), pair_3)
     pairs += [send(p, other_core) for p in pairs]
     w_parts = lax.all_to_all(w_part, AXES, 0, 0, axis_index_groups=W_GROUPS, tiled=True)
     c_part = c_products(w_parts, pairs).astype(jnp.float16)

time: 118 us -> 118 us (level)
  waiting for transfers between devices: 42.8 us -> 37.1 us
  starting transfers between devices: 33.2 us -> 36.4 us
  local copies, waits for them, and re-layouts: 5.19 us -> 7.02 us
  blocking collectives: 25.1 us -> 26.4 us
    ppermute x18 -> x19, waiting for transfers between devices: 28.3 us -> 23.3 us  [send(): return lax.ppermute(value, AXES, pairs)]
    ppermute x18 -> x19, starting transfers between devices: 29 us -> 31.4 us  [send(): return lax.ppermute(value, AXES, pairs)]
    unnamed x14 -> x22, local copies, waits for them, and re-layouts: 4.44 us -> 6.24 us
    all_to_all x1, blocking collectives: 25.1 us -> 26.4 us  [local(): lax.all_to_all(c_part, AXES, 0, 0, axis_index_groups=C_GROUPS, tiled=True)]
  transfers between devices with their start and end apart: 19 -> 20, of which waited for: 12 -> 10; matrix products, arithmetic and copies ran while one was open for 0% -> 0% of each run, Pallas kernels for 4% -> 2%
where the time goes in v5:
time: 118 us
  waiting for transfers between devices  37.1 us (31%)
  starting transfers between devices  36.4 us (31%)
  blocking collectives  26.4 us (22%)
  Pallas kernels  9.83 us (8%)
  local copies, waits for them, and re-layouts  7.02 us (6%)
    ppermute x19, starting transfers between devices, send(): return lax.ppermute(value, AXES, pairs)  31.4 us
    all_to_all x1, blocking collectives, local(): lax.all_to_all(c_part, AXES, 0, 0, axis_index_groups=C_GROUPS, tiled=True)  26.4 us
    ppermute x19, waiting for transfers between devices, send(): return lax.ppermute(value, AXES, pairs)  23.3 us
    all_to_all x1, waiting for transfers between devices, local(): lax.all_to_all(w_part, AXES, 0, 0, axis_index_groups=W_GROUPS, tiled=True)  13.8 us
    unnamed x22, local copies, waits for them, and re-layouts  6.24 us
    all_to_all x1, starting transfers between devices, local(): lax.all_to_all(w_part, AXES, 0, 0, axis_index_groups=W_GROUPS, tiled=True)  5.07 us
    pallas_call x2, Pallas kernels, w_products(): on_device(functools.partial(w_kernel, LANES * len(before)), (LANES * (1 +...  3.95 us
    pallas_call x1, Pallas kernels, masked(): pl.pallas_call(mask_kernel, out_shape=[jax.ShapeDtypeStruct(v.shape, v.dt...  2.8 us
  transfers between devices with their start and end apart: 20, of which 10 were waited for; matrix products, arithmetic and copies ran while one was open for 0% of the time, Pallas kernels for 2%

profile of v5, /device:TPU:2, one launch (start us, length us, event | category | flops | bytes accessed | tf_op | source)
XLA Modules:
  0.0 117.6 jit_solution(13014426137331602845)
XLA Ops:
  0.0 2.8 %shard_map.46 = (bf16[768,128]{1,0:T(8,128)(2,1)}, bf16[768,768]{1,0:T(8,128)(2,1)}) custom-call(bf16[768,128]{1,0:T(8,128)(2,1)} %p_any.1, bf16[768,768]{1,0:T(8,128)(2,1)} %a_any.1, s32[1,6]{1,0:T(1,128)} %bitcast.14, s32[6,6]{1,0:T(8,128)} %a_pattern.1), custom_call_target="tpu_custom_call" | custom-call | flops 589824 | bytes 4194304 | tf_op jit(solution)/shard_map/pallas_call | solution.py:141
  2.8 2.2 %collective-permute-start.2 = (bf16[768,128]{1,0:T(8,128)(2,1)}, bf16[768,128]{1,0:T(8,128)(2,1)S(1)}, u32[]{:S(2)}, u32[]{:S(2)}) collective-permute-start(bf16[768,128]{1,0:T(8,128)(2,1)} %get-tuple-element.25.one), channel_id=1, source_target_pairs={{0,2},{1,3},{2,0},{3,1},{4,6},{5,7},{6,4},{7,5},{8,10},{9,11},{10,... | collective-permute-start | bytes 589832 | tf_op jit(solution)/shard_map/ppermute | solution.py:31
  5.0 7.2 %collective-permute-start.1 = (bf16[768,128]{1,0:T(8,128)(2,1)}, bf16[768,128]{1,0:T(8,128)(2,1)S(1)}, u32[]{:S(2)}, u32[]{:S(2)}) collective-permute-start(bf16[768,128]{1,0:T(8,128)(2,1)} %get-tuple-element.25.one), channel_id=1, source_target_pairs={{0,128},{1,129},{2,130},{3,131},{4,96},{5,97},{6,98},{7,99},{8,64}... | collective-permute-start | bytes 589832 | tf_op jit(solution)/shard_map/ppermute | solution.py:31
  12.2 1.6 %collective-permute-start = (bf16[768,128]{1,0:T(8,128)(2,1)}, bf16[768,128]{1,0:T(8,128)(2,1)S(1)}, u32[]{:S(2)}, u32[]{:S(2)}) collective-permute-start(bf16[768,128]{1,0:T(8,128)(2,1)} %get-tuple-element.25.one), channel_id=1, source_target_pairs={{0,0},{1,1},{2,2},{3,3},{4,224},{5,225},{6,226},{7,227},{8,192},{9... | collective-permute-start | bytes 589832 | tf_op jit(solution)/shard_map/ppermute | solution.py:31
  13.8 4.2 %collective-permute-start.8 = (bf16[768,768]{1,0:T(8,128)(2,1)}, bf16[768,768]{1,0:T(8,128)(2,1)S(1)}, u32[]{:S(2)}, u32[]{:S(2)}) collective-permute-start(bf16[768,768]{1,0:T(8,128)(2,1)} %get-tuple-element.32), channel_id=1, source_target_pairs={{0,0},{1,16},{2,2},{3,18},{4,4},{5,20},{6,6},{7,22},{8,8},{9,24},{... | collective-permute-start | bytes 3538952 | tf_op jit(solution)/shard_map/ppermute | solution.py:31
  18.1 0.9 copy-done.10
  19.1 1.6 %collective-permute-done.1.two = bf16[768,128]{1,0:T(8,128)(2,1)S(1)} collective-permute-done((bf16[768,128]{1,0:T(8,128)(2,1)}, bf16[768,128]{1,0:T(8,128)(2,1)S(1)}, u32[]{:S(2)}, u32[]{:S(2)}) %collective-permute-start.1) | collective-permute-done | bytes 196640 | tf_op jit(solution)/shard_map/ppermute | solution.py:31
  20.7 8.8 %collective-permute-start.4 = (bf16[2,768,128]{2,1,0:T(8,128)(2,1)S(1)}, bf16[2,768,128]{2,1,0:T(8,128)(2,1)S(1)}, u32[]{:S(2)}, u32[]{:S(2)}) collective-permute-start(bf16[2,768,128]{2,1,0:T(8,128)(2,1)S(1)} %shard_map.48.own), channel_id=1, source_target_pairs={{0,224},{1,225},{2,226},{3,227},{4,228},{5,229},{6,230},{7,231},{8... | collective-permute-start | bytes 1179656 | tf_op jit(solution)/shard_map/ppermute | solution.py:31
  29.4 8.5 %collective-permute-done.4.above = bf16[2,768,128]{2,1,0:T(8,128)(2,1)S(1)} collective-permute-done((bf16[2,768,128]{2,1,0:T(8,128)(2,1)S(1)}, bf16[2,768,128]{2,1,0:T(8,128)(2,1)S(1)}, u32[]{:S(2)}, u32[]{:S(2)}) %collective-permute-start.4) | collective-permute-done | bytes 393248 | tf_op jit(solution)/shard_map/ppermute | solution.py:31
  38.4 3.0 %collective-permute-done.3.below = bf16[2,768,128]{2,1,0:T(8,128)(2,1)S(1)} collective-permute-done((bf16[2,768,128]{2,1,0:T(8,128)(2,1)S(1)}, bf16[2,768,128]{2,1,0:T(8,128)(2,1)S(1)}, u32[]{:S(2)}, u32[]{:S(2)}) %collective-permute-start.3) | collective-permute-done | bytes 393248 | tf_op jit(solution)/shard_map/ppermute | solution.py:31
  41.5 3.2 %collective-permute-start.7 = (bf16[768,128]{1,0:T(8,128)(2,1)S(1)}, bf16[768,128]{1,0:T(8,128)(2,1)S(1)}, u32[]{:S(2)}, u32[]{:S(2)}) collective-permute-start(bf16[768,128]{1,0:T(8,128)(2,1)S(1)} %slice_bitcast_fusion.2), channel_id=1, source_target_pairs={{0,224},{1,225},{2,226},{3,227},{4,228},{5,229},{6,230},{7,231},{8... | collective-permute-start | bytes 589832 | tf_op jit(solution)/shard_map/ppermute | solution.py:31
  44.8 3.4 %collective-permute-done.10.refs_3_ = bf16[2,768,128]{2,1,0:T(8,128)(2,1)S(1)} collective-permute-done((bf16[2,768,128]{2,1,0:T(8,128)(2,1)S(1)}, bf16[2,768,128]{2,1,0:T(8,128)(2,1)S(1)}, u32[]{:S(2)}, u32[]{:S(2)}) %collective-permute-start.10) | collective-permute-done | bytes 393248 | tf_op jit(solution)/shard_map/ppermute | solution.py:31
  49.1 1.8 %collective-permute-start.14 = (bf16[768,128]{1,0:T(8,128)(2,1)S(1)}, bf16[768,128]{1,0:T(8,128)(2,1)S(1)}, u32[]{:S(2)}, u32[]{:S(2)}) collective-permute-start(bf16[768,128]{1,0:T(8,128)(2,1)S(1)} %slice_bitcast_fusion), channel_id=1, source_target_pairs={{0,12},{1,13},{2,14},{3,15},{4,0},{5,1},{6,2},{7,3},{8,4},{9,5},{1... | collective-permute-start | bytes 589832 | tf_op jit(solution)/shard_map/ppermute | solution.py:31
  52.0 1.4 %shard_map.50.rest_0_ = bf16[4,768,128]{2,1,0:T(8,128)(2,1)S(1)} custom-call(bf16[2,768,512]{2,1,0:T(8,128)(2,1)S(1)} %shard_map.49.p_ref, bf16[768,768]{1,0:T(8,128)(2,1)S(1)} %collective-permute-done.8.one, bf16[768,768]{1,0:T(8,128)(2,1)S(1)} %collective-permute-done.9.two), custom_call_target="tpu_custom_call" | custom-call | flops 1207959552 | bytes 6291456 | tf_op jit(solution)/shard_map/pallas_call | solution.py:204
  53.4 2.7 %collective-permute-done.14.two = bf16[768,128]{1,0:T(8,128)(2,1)S(1)} collective-permute-done((bf16[768,128]{1,0:T(8,128)(2,1)S(1)}, bf16[768,128]{1,0:T(8,128)(2,1)S(1)}, u32[]{:S(2)}, u32[]{:S(2)}) %collective-permute-start.14) | collective-permute-done | bytes 196640 | tf_op jit(solution)/shard_map/ppermute | solution.py:31
  56.1 2.6 %collective-permute-done.13.one = bf16[768,128]{1,0:T(8,128)(2,1)S(1)} collective-permute-done((bf16[768,128]{1,0:T(8,128)(2,1)S(1)}, bf16[768,128]{1,0:T(8,128)(2,1)S(1)}, u32[]{:S(2)}, u32[]{:S(2)}) %collective-permute-start.13) | collective-permute-done | bytes 196640 | tf_op jit(solution)/shard_map/ppermute | solution.py:31
  58.7 2.6 %shard_map.51 = bf16[8,768,128]{2,1,0:T(8,128)(2,1)} custom-call(bf16[2,768,512]{2,1,0:T(8,128)(2,1)S(1)} %shard_map.49.p_ref, bf16[768,768]{1,0:T(8,128)(2,1)S(1)} %collective-permute-done.11.one, bf16[768,768]{1,0:T(8,128)(2,1)S(1)} %collective-permute-done.12.two, bf16[4,768,128]{2,1,0:T(8,128)(2,1)S(1)} %shard_map.50.rest_0_), custom_call_target="tpu_custom_call" | custom-call | flops 1207959552 | bytes 6291456 | tf_op jit(solution)/shard_map/pallas_call | solution.py:204
  61.3 5.1 %all-to-all-start = ((bf16[8,768,128]{2,1,0:T(8,128)(2,1)}), bf16[8,768,128]{2,1,0:T(8,128)(2,1)S(1)}, u32[]{:S(2)}, u32[]{:S(2)}) async-start(bf16[8,768,128]{2,1,0:T(8,128)(2,1)} %shard_map.51), calls=%async_computation | async-start | bytes 3145728 | tf_op jit(solution)/shard_map/all_to_all | solution.py:283
  71.0 13.8 %all-to-all-done.parts_ref = bf16[8,768,128]{2,1,0:T(8,128)(2,1)S(1)} async-done(((bf16[8,768,128]{2,1,0:T(8,128)(2,1)}), bf16[8,768,128]{2,1,0:T(8,128)(2,1)S(1)}, u32[]{:S(2)}, u32[]{:S(2)}) %all-to-all-start) | async-done | bytes 1572896 | tf_op jit(solution)/shard_map/all_to_all | solution.py:283
  84.8 1.0 copy-done.5
  85.8 1.0 copy-done.7
  86.8 1.0 copy-done.9
  87.8 2.2 %shard_map.53 = f32[16,136,128]{2,1,0:T(8,128)S(1)} custom-call(bf16[8,768,128]{2,1,0:T(8,128)(2,1)S(1)} %all-to-all-done.parts_ref, bf16[2,768,128]{2,1,0:T(8,128)(2,1)S(1)} %shard_map.47.refs_0_, bf16[2,768,128]{2,1,0:T(8,128)(2,1)S(1)} %copy-done.1, bf16[2,768,128]{2,1,0:T(8,128)(2,1)S(1)} %shard_map.52.refs_2_, bf16[2,768,128]{2,1,0:T(8,128)(2,1)S(1)} %copy-done.3, ...), custom_call_target="tpu_custom_call" | custom-call | flops 805306368 | bytes 6291456 | tf_op jit(solution)/shard_map/pallas_call | solution.py:242
  90.0 26.4 %all_to_all.10 = f16[16,136,128]{2,1,0:T(8,128)(2,1)S(1)} all-to-all(f16[16,136,128]{2,1,0:T(8,128)(2,1)S(1)} %convert_element_type.6), channel_id=1, replica_groups={{0,32,192,224,128,160,64,96,16,48,208,240,144,176,80,112},{17,49,209,24..., dimensions={0} | all-to-all | bytes 1114112 | tf_op jit(solution)/shard_map/all_to_all | solution.py:285
  (57 shorter events, 8.5 us)
Async XLA Ops:
  2.8 15.3 %collective-permute-start.2 = (bf16[768,128]{1,0:T(8,128)(2,1)}, bf16[768,128]{1,0:T(8,128)(2,1)S(1)}, u32[]{:S(2)}, u32[]{:S(2)}) collective-permute-start(bf16[768,128]{1,0:T(8,128)(2,1)} %get-tuple-element.25.one), channel_id=1, source_target_pairs={{0,2},{1,3},{2,0},{3,1},{4,6},{5,7},{6,4},{7,5},{8,10},{9,11},{10,... | collective-permute-start | bytes 589832 | tf_op jit(solution)/shard_map/ppermute | solution.py:31
  5.0 15.6 %collective-permute-start.1 = (bf16[768,128]{1,0:T(8,128)(2,1)}, bf16[768,128]{1,0:T(8,128)(2,1)S(1)}, u32[]{:S(2)}, u32[]{:S(2)}) collective-permute-start(bf16[768,128]{1,0:T(8,128)(2,1)} %get-tuple-element.25.one), channel_id=1, source_target_pairs={{0,128},{1,129},{2,130},{3,131},{4,96},{5,97},{6,98},{7,99},{8,64}... | collective-permute-start | bytes 589832 | tf_op jit(solution)/shard_map/ppermute | solution.py:31
  12.2 8.4 %collective-permute-start = (bf16[768,128]{1,0:T(8,128)(2,1)}, bf16[768,128]{1,0:T(8,128)(2,1)S(1)}, u32[]{:S(2)}, u32[]{:S(2)}) collective-permute-start(bf16[768,128]{1,0:T(8,128)(2,1)} %get-tuple-element.25.one), channel_id=1, source_target_pairs={{0,0},{1,1},{2,2},{3,3},{4,224},{5,225},{6,226},{7,227},{8,192},{9... | collective-permute-start | bytes 589832 | tf_op jit(solution)/shard_map/ppermute | solution.py:31
  13.8 34.6 %collective-permute-start.9 = (bf16[768,768]{1,0:T(8,128)(2,1)}, bf16[768,768]{1,0:T(8,128)(2,1)S(1)}, u32[]{:S(2)}, u32[]{:S(2)}) collective-permute-start(bf16[768,768]{1,0:T(8,128)(2,1)} %get-tuple-element.32), channel_id=1, source_target_pairs={{0,2},{1,18},{2,0},{3,16},{4,6},{5,22},{6,4},{7,20},{8,10},{9,26},... | collective-permute-start | bytes 3538952 | tf_op jit(solution)/shard_map/ppermute | solution.py:31
  13.8 34.6 %collective-permute-start.8 = (bf16[768,768]{1,0:T(8,128)(2,1)}, bf16[768,768]{1,0:T(8,128)(2,1)S(1)}, u32[]{:S(2)}, u32[]{:S(2)}) collective-permute-start(bf16[768,768]{1,0:T(8,128)(2,1)} %get-tuple-element.32), channel_id=1, source_target_pairs={{0,0},{1,16},{2,2},{3,18},{4,4},{5,20},{6,6},{7,22},{8,8},{9,24},{... | collective-permute-start | bytes 3538952 | tf_op jit(solution)/shard_map/ppermute | solution.py:31
  20.7 17.3 %collective-permute-start.4 = (bf16[2,768,128]{2,1,0:T(8,128)(2,1)S(1)}, bf16[2,768,128]{2,1,0:T(8,128)(2,1)S(1)}, u32[]{:S(2)}, u32[]{:S(2)}) collective-permute-start(bf16[2,768,128]{2,1,0:T(8,128)(2,1)S(1)} %shard_map.48.own), channel_id=1, source_target_pairs={{0,224},{1,225},{2,226},{3,227},{4,228},{5,229},{6,230},{7,231},{8... | collective-permute-start | bytes 1179656 | tf_op jit(solution)/shard_map/ppermute | solution.py:31
  29.4 12.0 %collective-permute-start.3 = (bf16[2,768,128]{2,1,0:T(8,128)(2,1)S(1)}, bf16[2,768,128]{2,1,0:T(8,128)(2,1)S(1)}, u32[]{:S(2)}, u32[]{:S(2)}) collective-permute-start(bf16[2,768,128]{2,1,0:T(8,128)(2,1)S(1)} %shard_map.48.own), channel_id=1, source_target_pairs={{0,32},{1,33},{2,34},{3,35},{4,36},{5,37},{6,38},{7,39},{8,40},{9,... | collective-permute-start | bytes 1179656 | tf_op jit(solution)/shard_map/ppermute | solution.py:31
  29.4 12.0 %collective-permute-start.5 = (bf16[2,768,128]{2,1,0:T(8,128)(2,1)S(1)}, bf16[2,768,128]{2,1,0:T(8,128)(2,1)S(1)}, u32[]{:S(2)}, u32[]{:S(2)}) collective-permute-start(bf16[2,768,128]{2,1,0:T(8,128)(2,1)S(1)} %shard_map.47.refs_0_), channel_id=1, source_target_pairs={{0,4},{1,5},{2,6},{3,7},{4,8},{5,9},{6,10},{7,11},{8,12},{9,13},{1... | collective-permute-start | bytes 1179656 | tf_op jit(solution)/shard_map/ppermute | solution.py:31
  38.0 10.2 %collective-permute-start.10 = (bf16[2,768,128]{2,1,0:T(8,128)(2,1)S(1)}, bf16[2,768,128]{2,1,0:T(8,128)(2,1)S(1)}, u32[]{:S(2)}, u32[]{:S(2)}) collective-permute-start(bf16[2,768,128]{2,1,0:T(8,128)(2,1)S(1)} %shard_map.47.refs_0_), channel_id=1, source_target_pairs={{0,12},{1,13},{2,14},{3,15},{4,0},{5,1},{6,2},{7,3},{8,4},{9,5},{1... | collective-permute-start | bytes 1179656 | tf_op jit(solution)/shard_map/ppermute | solution.py:31
  41.4 10.6 %copy-start = (bf16[2,768,128]{2,1,0:T(8,128)(2,1)}, bf16[2,768,128]{2,1,0:T(8,128)(2,1)S(1)}, u32[]{:S(2)}) copy-start(bf16[2,768,128]{2,1,0:T(8,128)(2,1)S(1)} %collective-permute-done.5.refs_1_) | copy-start | bytes 1179652
  41.4 7.0 %collective-permute-start.6 = (bf16[768,128]{1,0:T(8,128)(2,1)S(1)}, bf16[768,128]{1,0:T(8,128)(2,1)S(1)}, u32[]{:S(2)}, u32[]{:S(2)}) collective-permute-start(bf16[768,128]{1,0:T(8,128)(2,1)S(1)} %slice_bitcast_fusion.3), channel_id=1, source_target_pairs={{0,32},{1,33},{2,34},{3,35},{4,36},{5,37},{6,38},{7,39},{8,40},{9,... | collective-permute-start | bytes 589832 | tf_op jit(solution)/shard_map/ppermute | solution.py:31
  41.5 6.9 %collective-permute-start.7 = (bf16[768,128]{1,0:T(8,128)(2,1)S(1)}, bf16[768,128]{1,0:T(8,128)(2,1)S(1)}, u32[]{:S(2)}, u32[]{:S(2)}) collective-permute-start(bf16[768,128]{1,0:T(8,128)(2,1)S(1)} %slice_bitcast_fusion.2), channel_id=1, source_target_pairs={{0,224},{1,225},{2,226},{3,227},{4,228},{5,229},{6,230},{7,231},{8... | collective-permute-start | bytes 589832 | tf_op jit(solution)/shard_map/ppermute | solution.py:31
  48.2 3.8 %copy-start.2 = (bf16[2,768,128]{2,1,0:T(8,128)(2,1)}, bf16[2,768,128]{2,1,0:T(8,128)(2,1)S(1)}, u32[]{:S(2)}) copy-start(bf16[2,768,128]{2,1,0:T(8,128)(2,1)S(1)} %collective-permute-done.10.refs_3_) | copy-start | bytes 1179652
  48.4 10.3 %collective-permute-start.11 = (bf16[768,768]{1,0:T(8,128)(2,1)S(1)}, bf16[768,768]{1,0:T(8,128)(2,1)S(1)}, u32[]{:S(2)}, u32[]{:S(2)}) collective-permute-start(bf16[768,768]{1,0:T(8,128)(2,1)S(1)} %collective-permute-done.8.one), channel_id=1, source_target_pairs={{0,1},{1,0},{2,3},{3,2},{4,5},{5,4},{6,7},{7,6},{8,9},{9,8},{10,11... | collective-permute-start | bytes 3538952 | tf_op jit(solution)/shard_map/ppermute | solution.py:31
  48.5 10.2 %collective-permute-start.12 = (bf16[768,768]{1,0:T(8,128)(2,1)S(1)}, bf16[768,768]{1,0:T(8,128)(2,1)S(1)}, u32[]{:S(2)}, u32[]{:S(2)}) collective-permute-start(bf16[768,768]{1,0:T(8,128)(2,1)S(1)} %collective-permute-done.9.two), channel_id=1, source_target_pairs={{0,1},{1,0},{2,3},{3,2},{4,5},{5,4},{6,7},{7,6},{8,9},{9,8},{10,11... | collective-permute-start | bytes 3538952 | tf_op jit(solution)/shard_map/ppermute | solution.py:31
  49.1 7.0 %collective-permute-start.14 = (bf16[768,128]{1,0:T(8,128)(2,1)S(1)}, bf16[768,128]{1,0:T(8,128)(2,1)S(1)}, u32[]{:S(2)}, u32[]{:S(2)}) collective-permute-start(bf16[768,128]{1,0:T(8,128)(2,1)S(1)} %slice_bitcast_fusion), channel_id=1, source_target_pairs={{0,12},{1,13},{2,14},{3,15},{4,0},{5,1},{6,2},{7,3},{8,4},{9,5},{1... | collective-permute-start | bytes 589832 | tf_op jit(solution)/shard_map/ppermute | solution.py:31
  50.9 7.8 %collective-permute-start.13 = (bf16[768,128]{1,0:T(8,128)(2,1)S(1)}, bf16[768,128]{1,0:T(8,128)(2,1)S(1)}, u32[]{:S(2)}, u32[]{:S(2)}) collective-permute-start(bf16[768,128]{1,0:T(8,128)(2,1)S(1)} %slice_bitcast_fusion.1), channel_id=1, source_target_pairs={{0,4},{1,5},{2,6},{3,7},{4,8},{5,9},{6,10},{7,11},{8,12},{9,13},{1... | collective-permute-start | bytes 589832 | tf_op jit(solution)/shard_map/ppermute | solution.py:31
  61.3 5.1 %copy-start.1 = (bf16[2,768,128]{2,1,0:T(8,128)(2,1)S(1)}, bf16[2,768,128]{2,1,0:T(8,128)(2,1)}, u32[]{:S(2)}) copy-start(bf16[2,768,128]{2,1,0:T(8,128)(2,1)} %copy-done) | copy-start | bytes 1179652
  61.3 5.7 %copy-start.3 = (bf16[2,768,128]{2,1,0:T(8,128)(2,1)S(1)}, bf16[2,768,128]{2,1,0:T(8,128)(2,1)}, u32[]{:S(2)}) copy-start(bf16[2,768,128]{2,1,0:T(8,128)(2,1)} %copy-done.2) | copy-start | bytes 1179652
  61.3 23.5 %all-to-all-start = ((bf16[8,768,128]{2,1,0:T(8,128)(2,1)}), bf16[8,768,128]{2,1,0:T(8,128)(2,1)S(1)}, u32[]{:S(2)}, u32[]{:S(2)}) async-start(bf16[8,768,128]{2,1,0:T(8,128)(2,1)} %shard_map.51), calls=%async_computation | async-start | bytes 3145728 | tf_op jit(solution)/shard_map/all_to_all | solution.py:283
  66.4 1.7 %collective-permute-start.15 = (bf16[2,768,128]{2,1,0:T(8,128)(2,1)S(1)}, bf16[2,768,128]{2,1,0:T(8,128)(2,1)S(1)}, u32[]{:S(2)}, u32[]{:S(2)}) collective-permute-start(bf16[2,768,128]{2,1,0:T(8,128)(2,1)S(1)} %shard_map.47.refs_0_), channel_id=1, source_target_pairs={{0,1},{1,0},{2,3},{3,2},{4,5},{5,4},{6,7},{7,6},{8,9},{9,8},{10,11... | collective-permute-start | bytes 1179656 | tf_op jit(solution)/shard_map/ppermute | solution.py:31
  66.4 2.3 %collective-permute-start.16 = (bf16[2,768,128]{2,1,0:T(8,128)(2,1)S(1)}, bf16[2,768,128]{2,1,0:T(8,128)(2,1)S(1)}, u32[]{:S(2)}, u32[]{:S(2)}) collective-permute-start(bf16[2,768,128]{2,1,0:T(8,128)(2,1)S(1)} %copy-done.1), channel_id=1, source_target_pairs={{0,1},{1,0},{2,3},{3,2},{4,5},{5,4},{6,7},{7,6},{8,9},{9,8},{10,11... | collective-permute-start | bytes 1179656 | tf_op jit(solution)/shard_map/ppermute | solution.py:31
  66.9 2.6 %collective-permute-start.17 = (bf16[2,768,128]{2,1,0:T(8,128)(2,1)S(1)}, bf16[2,768,128]{2,1,0:T(8,128)(2,1)S(1)}, u32[]{:S(2)}, u32[]{:S(2)}) collective-permute-start(bf16[2,768,128]{2,1,0:T(8,128)(2,1)S(1)} %shard_map.52.refs_2_), channel_id=1, source_target_pairs={{0,1},{1,0},{2,3},{3,2},{4,5},{5,4},{6,7},{7,6},{8,9},{9,8},{10,11... | collective-permute-start | bytes 1179656 | tf_op jit(solution)/shard_map/ppermute | solution.py:31
  67.0 3.2 %collective-permute-start.18 = (bf16[2,768,128]{2,1,0:T(8,128)(2,1)S(1)}, bf16[2,768,128]{2,1,0:T(8,128)(2,1)S(1)}, u32[]{:S(2)}, u32[]{:S(2)}) collective-permute-start(bf16[2,768,128]{2,1,0:T(8,128)(2,1)S(1)} %copy-done.3), channel_id=1, source_target_pairs={{0,1},{1,0},{2,3},{3,2},{4,5},{5,4},{6,7},{7,6},{8,9},{9,8},{10,11... | collective-permute-start | bytes 1179656 | tf_op jit(solution)/shard_map/ppermute | solution.py:31
  (7 other events, 6.2 us)

commit v6 on v5

--- a/solution.py
+++ b/solution.py
@@ -267,7 +267,7 @@
     across = send(p_eff, far_x)
     near, distant = send(a_eff, swap), send(a_eff, swap_far)
     pair = paired(p_eff, across)
-    first, second, spot, pair = both(first, second, spot, pair)
+    first, second, spot = both(first, second, spot)
     own = paired(first, second)
     below, above, pair_1 = both(send(own, z_up), send(own, z_down), send(pair, y_up))
     pair_3 = send(pair, y_down)
@@ -278,7 +278,8 @@
     near_2, distant_2 = send(near, other_core), send(distant, other_core)
     w_part = w_products(p_all, near, distant)
     w_part = w_products(p_all, near_2, distant_2, w_part)
-    w_part, *pairs = both(w_part, pair, pair_1, paired(*beyond), pair_3)
+    w_part, pair, pair_1, pair_3, *beyond = both(w_part, pair, pair_1, pair_3, *beyond)
+    pairs = [pair, pair_1, paired(*beyond), pair_3]
     pairs += [send(p, other_core) for p in pairs]
     w_parts = lax.all_to_all(w_part, AXES, 0, 0, axis_index_groups=W_GROUPS, tiled=True)
     c_part = c_products(w_parts, pairs).astype(jnp.float16)

time: 118 us -> 115 us (0.975)
  waiting for transfers between devices: 37.1 us -> 30.9 us
  starting transfers between devices: 36.4 us -> 39 us
  local copies, waits for them, and re-layouts: 7.02 us -> 9.28 us
  blocking collectives: 26.4 us -> 24.5 us
    ppermute x19, waiting for transfers between devices: 23.3 us -> 17.3 us  [send(): return lax.ppermute(value, AXES, pairs)]
    unnamed x22 -> x26, local copies, waits for them, and re-layouts: 6.24 us -> 8.5 us
    all_to_all x1, blocking collectives: 26.4 us -> 24.5 us  [local(): lax.all_to_all(c_part, AXES, 0, 0, axis_index_groups=C_GROUPS, tiled=True)]
    all_to_all x1, starting transfers between devices: 5.07 us -> 6.48 us  [local(): lax.all_to_all(w_part, AXES, 0, 0, axis_index_groups=W_GROUPS, tiled=True)]
  transfers between devices with their start and end apart: 20 -> 20, of which waited for: 10 -> 11; matrix products, arithmetic and copies ran while one was open for 0% -> 0% of each run, Pallas kernels for 2% -> 4%
where the time goes in v6:
time: 115 us; the launch traced here: 114 us
  starting transfers between devices  39 us (34%)
  waiting for transfers between devices  30.9 us (27%)
  blocking collectives  24.5 us (21%)
  Pallas kernels  9.81 us (9%)
  local copies, waits for them, and re-layouts  9.28 us (8%)
    ppermute x19, starting transfers between devices, send(): return lax.ppermute(value, AXES, pairs)  32.6 us
    all_to_all x1, blocking collectives, local(): lax.all_to_all(c_part, AXES, 0, 0, axis_index_groups=C_GROUPS, tiled=True)  24.5 us
    ppermute x19, waiting for transfers between devices, send(): return lax.ppermute(value, AXES, pairs)  17.3 us
    all_to_all x1, waiting for transfers between devices, local(): lax.all_to_all(w_part, AXES, 0, 0, axis_index_groups=W_GROUPS, tiled=True)  13.6 us
    unnamed x26, local copies, waits for them, and re-layouts  8.5 us
    all_to_all x1, starting transfers between devices, local(): lax.all_to_all(w_part, AXES, 0, 0, axis_index_groups=W_GROUPS, tiled=True)  6.48 us
    pallas_call x2, Pallas kernels, w_products(): on_device(functools.partial(w_kernel, LANES * len(before)), (LANES * (1 +...  3.95 us
    pallas_call x1, Pallas kernels, masked(): pl.pallas_call(mask_kernel, out_shape=[jax.ShapeDtypeStruct(v.shape, v.dt...  2.78 us
  transfers between devices with their start and end apart: 20, of which 11 were waited for; matrix products, arithmetic and copies ran while one was open for 0% of the time, Pallas kernels for 4%

profile of v6, /device:TPU:2, one launch (start us, length us, event | category | flops | bytes accessed | tf_op | source)
XLA Modules:
  0.0 114.3 jit_solution(8883476358797055630)
XLA Ops:
  0.0 2.8 %shard_map.46 = (bf16[768,128]{1,0:T(8,128)(2,1)}, bf16[768,768]{1,0:T(8,128)(2,1)}) custom-call(bf16[768,128]{1,0:T(8,128)(2,1)} %p_any.1, bf16[768,768]{1,0:T(8,128)(2,1)} %a_any.1, s32[1,6]{1,0:T(1,128)} %bitcast.14, s32[6,6]{1,0:T(8,128)} %a_pattern.1), custom_call_target="tpu_custom_call" | custom-call | flops 589824 | bytes 4194304 | tf_op jit(solution)/shard_map/pallas_call | solution.py:141
  2.8 1.6 %collective-permute-start = (bf16[768,128]{1,0:T(8,128)(2,1)}, bf16[768,128]{1,0:T(8,128)(2,1)S(1)}, u32[]{:S(2)}, u32[]{:S(2)}) collective-permute-start(bf16[768,128]{1,0:T(8,128)(2,1)} %get-tuple-element.25.one), channel_id=1, source_target_pairs={{0,0},{1,1},{2,2},{3,3},{4,224},{5,225},{6,226},{7,227},{8,192},{9... | collective-permute-start | bytes 589832 | tf_op jit(solution)/shard_map/ppermute | solution.py:31
  4.4 9.9 %collective-permute-start.1 = (bf16[768,128]{1,0:T(8,128)(2,1)}, bf16[768,128]{1,0:T(8,128)(2,1)S(1)}, u32[]{:S(2)}, u32[]{:S(2)}) collective-permute-start(bf16[768,128]{1,0:T(8,128)(2,1)} %get-tuple-element.25.one), channel_id=1, source_target_pairs={{0,128},{1,129},{2,130},{3,131},{4,96},{5,97},{6,98},{7,99},{8,64}... | collective-permute-start | bytes 589832 | tf_op jit(solution)/shard_map/ppermute | solution.py:31
  14.3 2.1 %collective-permute-start.4 = (bf16[768,128]{1,0:T(8,128)(2,1)}, bf16[768,128]{1,0:T(8,128)(2,1)S(1)}, u32[]{:S(2)}, u32[]{:S(2)}) collective-permute-start(bf16[768,128]{1,0:T(8,128)(2,1)} %get-tuple-element.25.one), channel_id=1, source_target_pairs={{0,2},{1,3},{2,0},{3,1},{4,6},{5,7},{6,4},{7,5},{8,10},{9,11},{10,... | collective-permute-start | bytes 589832 | tf_op jit(solution)/shard_map/ppermute | solution.py:31
  16.4 1.9 %collective-permute-start.8 = (bf16[768,768]{1,0:T(8,128)(2,1)}, bf16[768,768]{1,0:T(8,128)(2,1)S(1)}, u32[]{:S(2)}, u32[]{:S(2)}) collective-permute-start(bf16[768,768]{1,0:T(8,128)(2,1)} %get-tuple-element.31), channel_id=1, source_target_pairs={{0,0},{1,16},{2,2},{3,18},{4,4},{5,20},{6,6},{7,22},{8,8},{9,24},{... | collective-permute-start | bytes 3538952 | tf_op jit(solution)/shard_map/ppermute | solution.py:31
  18.3 1.7 %collective-permute-start.9 = (bf16[768,768]{1,0:T(8,128)(2,1)}, bf16[768,768]{1,0:T(8,128)(2,1)S(1)}, u32[]{:S(2)}, u32[]{:S(2)}) collective-permute-start(bf16[768,768]{1,0:T(8,128)(2,1)} %get-tuple-element.31), channel_id=1, source_target_pairs={{0,2},{1,18},{2,0},{3,16},{4,6},{5,22},{6,4},{7,20},{8,10},{9,26},... | collective-permute-start | bytes 3538952 | tf_op jit(solution)/shard_map/ppermute | solution.py:31
  20.1 2.5 %collective-permute-done.1.two = bf16[768,128]{1,0:T(8,128)(2,1)S(1)} collective-permute-done((bf16[768,128]{1,0:T(8,128)(2,1)}, bf16[768,128]{1,0:T(8,128)(2,1)S(1)}, u32[]{:S(2)}, u32[]{:S(2)}) %collective-permute-start.1) | collective-permute-done | bytes 196640 | tf_op jit(solution)/shard_map/ppermute | solution.py:31
  22.7 1.2 %collective-permute-start.2 = (bf16[2,768,128]{2,1,0:T(8,128)(2,1)S(1)}, bf16[2,768,128]{2,1,0:T(8,128)(2,1)S(1)}, u32[]{:S(2)}, u32[]{:S(2)}) collective-permute-start(bf16[2,768,128]{2,1,0:T(8,128)(2,1)S(1)} %shard_map.47.own), channel_id=1, source_target_pairs={{0,32},{1,33},{2,34},{3,35},{4,36},{5,37},{6,38},{7,39},{8,40},{9,... | collective-permute-start | bytes 1179656 | tf_op jit(solution)/shard_map/ppermute | solution.py:31
  23.9 2.5 %collective-permute-start.3 = (bf16[2,768,128]{2,1,0:T(8,128)(2,1)S(1)}, bf16[2,768,128]{2,1,0:T(8,128)(2,1)S(1)}, u32[]{:S(2)}, u32[]{:S(2)}) collective-permute-start(bf16[2,768,128]{2,1,0:T(8,128)(2,1)S(1)} %shard_map.47.own), channel_id=1, source_target_pairs={{0,224},{1,225},{2,226},{3,227},{4,228},{5,229},{6,230},{7,231},{8... | collective-permute-start | bytes 1179656 | tf_op jit(solution)/shard_map/ppermute | solution.py:31
  27.7 7.0 %collective-permute-done.2.below = bf16[2,768,128]{2,1,0:T(8,128)(2,1)S(1)} collective-permute-done((bf16[2,768,128]{2,1,0:T(8,128)(2,1)S(1)}, bf16[2,768,128]{2,1,0:T(8,128)(2,1)S(1)}, u32[]{:S(2)}, u32[]{:S(2)}) %collective-permute-start.2) | collective-permute-done | bytes 393248 | tf_op jit(solution)/shard_map/ppermute | solution.py:31
  34.7 2.7 %collective-permute-start.10 = (bf16[2,768,128]{2,1,0:T(8,128)(2,1)S(1)}, bf16[2,768,128]{2,1,0:T(8,128)(2,1)S(1)}, u32[]{:S(2)}, u32[]{:S(2)}) collective-permute-start(bf16[2,768,128]{2,1,0:T(8,128)(2,1)S(1)} %shard_map.48.refs_0_), channel_id=1, source_target_pairs={{0,12},{1,13},{2,14},{3,15},{4,0},{5,1},{6,2},{7,3},{8,4},{9,5},{1... | collective-permute-start | bytes 1179656 | tf_op jit(solution)/shard_map/ppermute | solution.py:31
  37.3 1.5 %collective-permute-done.5.refs_1_ = bf16[2,768,128]{2,1,0:T(8,128)(2,1)S(1)} collective-permute-done((bf16[2,768,128]{2,1,0:T(8,128)(2,1)S(1)}, bf16[2,768,128]{2,1,0:T(8,128)(2,1)S(1)}, u32[]{:S(2)}, u32[]{:S(2)}) %collective-permute-start.5) | collective-permute-done | bytes 393248 | tf_op jit(solution)/shard_map/ppermute | solution.py:31
  38.9 1.8 %collective-permute-start.6 = (bf16[768,128]{1,0:T(8,128)(2,1)S(1)}, bf16[768,128]{1,0:T(8,128)(2,1)S(1)}, u32[]{:S(2)}, u32[]{:S(2)}) collective-permute-start(bf16[768,128]{1,0:T(8,128)(2,1)S(1)} %slice_bitcast_fusion.3), channel_id=1, source_target_pairs={{0,32},{1,33},{2,34},{3,35},{4,36},{5,37},{6,38},{7,39},{8,40},{9,... | collective-permute-start | bytes 589832 | tf_op jit(solution)/shard_map/ppermute | solution.py:31
  40.7 1.6 %collective-permute-start.7 = (bf16[768,128]{1,0:T(8,128)(2,1)S(1)}, bf16[768,128]{1,0:T(8,128)(2,1)S(1)}, u32[]{:S(2)}, u32[]{:S(2)}) collective-permute-start(bf16[768,128]{1,0:T(8,128)(2,1)S(1)} %slice_bitcast_fusion.2), channel_id=1, source_target_pairs={{0,224},{1,225},{2,226},{3,227},{4,228},{5,229},{6,230},{7,231},{8... | collective-permute-start | bytes 589832 | tf_op jit(solution)/shard_map/ppermute | solution.py:31
  42.3 1.8 %collective-permute-done.10.refs_3_ = bf16[2,768,128]{2,1,0:T(8,128)(2,1)S(1)} collective-permute-done((bf16[2,768,128]{2,1,0:T(8,128)(2,1)S(1)}, bf16[2,768,128]{2,1,0:T(8,128)(2,1)S(1)}, u32[]{:S(2)}, u32[]{:S(2)}) %collective-permute-start.10) | collective-permute-done | bytes 393248 | tf_op jit(solution)/shard_map/ppermute | solution.py:31
  44.1 1.8 %collective-permute-done.6.up_two = bf16[768,128]{1,0:T(8,128)(2,1)S(1)} collective-permute-done((bf16[768,128]{1,0:T(8,128)(2,1)S(1)}, bf16[768,128]{1,0:T(8,128)(2,1)S(1)}, u32[]{:S(2)}, u32[]{:S(2)}) %collective-permute-start.6) | collective-permute-done | bytes 196640 | tf_op jit(solution)/shard_map/ppermute | solution.py:31
  47.9 1.7 %collective-permute-start.13 = (bf16[768,128]{1,0:T(8,128)(2,1)S(1)}, bf16[768,128]{1,0:T(8,128)(2,1)S(1)}, u32[]{:S(2)}, u32[]{:S(2)}) collective-permute-start(bf16[768,128]{1,0:T(8,128)(2,1)S(1)} %slice_bitcast_fusion.1), channel_id=1, source_target_pairs={{0,4},{1,5},{2,6},{3,7},{4,8},{5,9},{6,10},{7,11},{8,12},{9,13},{1... | collective-permute-start | bytes 589832 | tf_op jit(solution)/shard_map/ppermute | solution.py:31
  49.6 1.6 %collective-permute-start.14 = (bf16[768,128]{1,0:T(8,128)(2,1)S(1)}, bf16[768,128]{1,0:T(8,128)(2,1)S(1)}, u32[]{:S(2)}, u32[]{:S(2)}) collective-permute-start(bf16[768,128]{1,0:T(8,128)(2,1)S(1)} %slice_bitcast_fusion), channel_id=1, source_target_pairs={{0,12},{1,13},{2,14},{3,15},{4,0},{5,1},{6,2},{7,3},{8,4},{9,5},{1... | collective-permute-start | bytes 589832 | tf_op jit(solution)/shard_map/ppermute | solution.py:31
  52.1 1.4 %shard_map.50.rest_0_ = bf16[4,768,128]{2,1,0:T(8,128)(2,1)S(1)} custom-call(bf16[2,768,512]{2,1,0:T(8,128)(2,1)S(1)} %shard_map.49.p_ref, bf16[768,768]{1,0:T(8,128)(2,1)S(1)} %collective-permute-done.8.one, bf16[768,768]{1,0:T(8,128)(2,1)S(1)} %collective-permute-done.9.two), custom_call_target="tpu_custom_call" | custom-call | flops 1207959552 | bytes 6291456 | tf_op jit(solution)/shard_map/pallas_call | solution.py:204
  53.5 2.6 %shard_map.51 = bf16[8,768,128]{2,1,0:T(8,128)(2,1)} custom-call(bf16[2,768,512]{2,1,0:T(8,128)(2,1)S(1)} %shard_map.49.p_ref, bf16[768,768]{1,0:T(8,128)(2,1)S(1)} %collective-permute-done.11.one, bf16[768,768]{1,0:T(8,128)(2,1)S(1)} %collective-permute-done.12.two, bf16[4,768,128]{2,1,0:T(8,128)(2,1)S(1)} %shard_map.50.rest_0_), custom_call_target="tpu_custom_call" | custom-call | flops 1207959552 | bytes 6291456 | tf_op jit(solution)/shard_map/pallas_call | solution.py:204
  57.5 6.5 %all-to-all-start = ((bf16[8,768,128]{2,1,0:T(8,128)(2,1)}), bf16[8,768,128]{2,1,0:T(8,128)(2,1)S(1)}, u32[]{:S(2)}, u32[]{:S(2)}) async-start(bf16[8,768,128]{2,1,0:T(8,128)(2,1)} %shard_map.51), calls=%async_computation | async-start | bytes 3145728 | tf_op jit(solution)/shard_map/all_to_all | solution.py:284
  69.8 13.6 %all-to-all-done.parts_ref = bf16[8,768,128]{2,1,0:T(8,128)(2,1)S(1)} async-done(((bf16[8,768,128]{2,1,0:T(8,128)(2,1)}), bf16[8,768,128]{2,1,0:T(8,128)(2,1)S(1)}, u32[]{:S(2)}, u32[]{:S(2)}) %all-to-all-start) | async-done | bytes 1572896 | tf_op jit(solution)/shard_map/all_to_all | solution.py:284
  86.4 2.2 %shard_map.53 = f32[16,136,128]{2,1,0:T(8,128)S(1)} custom-call(bf16[8,768,128]{2,1,0:T(8,128)(2,1)S(1)} %all-to-all-done.parts_ref, bf16[2,768,128]{2,1,0:T(8,128)(2,1)S(1)} %shard_map.48.refs_0_, bf16[2,768,128]{2,1,0:T(8,128)(2,1)S(1)} %collective-permute-done.5.refs_1_, bf16[2,768,128]{2,1,0:T(8,128)(2,1)S(1)} %shard_map.52.refs_2_, ...), custom_call_target="tpu_custom_call" | custom-call | flops 805306368 | bytes 6291456 | tf_op jit(solution)/shard_map/pallas_call | solution.py:242
  88.6 24.5 %all_to_all.10 = f16[16,136,128]{2,1,0:T(8,128)(2,1)S(1)} all-to-all(f16[16,136,128]{2,1,0:T(8,128)(2,1)S(1)} %convert_element_type.6), channel_id=1, replica_groups={{0,32,192,224,128,160,64,96,16,48,208,240,144,176,80,112},{17,49,209,24..., dimensions={0} | all-to-all | bytes 1114112 | tf_op jit(solution)/shard_map/all_to_all | solution.py:286
  (61 shorter events, 15.6 us)
Async XLA Ops:
  2.8 17.4 %collective-permute-start = (bf16[768,128]{1,0:T(8,128)(2,1)}, bf16[768,128]{1,0:T(8,128)(2,1)S(1)}, u32[]{:S(2)}, u32[]{:S(2)}) collective-permute-start(bf16[768,128]{1,0:T(8,128)(2,1)} %get-tuple-element.25.one), channel_id=1, source_target_pairs={{0,0},{1,1},{2,2},{3,3},{4,224},{5,225},{6,226},{7,227},{8,192},{9... | collective-permute-start | bytes 589832 | tf_op jit(solution)/shard_map/ppermute | solution.py:31
  4.4 18.3 %collective-permute-start.1 = (bf16[768,128]{1,0:T(8,128)(2,1)}, bf16[768,128]{1,0:T(8,128)(2,1)S(1)}, u32[]{:S(2)}, u32[]{:S(2)}) collective-permute-start(bf16[768,128]{1,0:T(8,128)(2,1)} %get-tuple-element.25.one), channel_id=1, source_target_pairs={{0,128},{1,129},{2,130},{3,131},{4,96},{5,97},{6,98},{7,99},{8,64}... | collective-permute-start | bytes 589832 | tf_op jit(solution)/shard_map/ppermute | solution.py:31
  14.3 12.2 %collective-permute-start.4 = (bf16[768,128]{1,0:T(8,128)(2,1)}, bf16[768,128]{1,0:T(8,128)(2,1)S(1)}, u32[]{:S(2)}, u32[]{:S(2)}) collective-permute-start(bf16[768,128]{1,0:T(8,128)(2,1)} %get-tuple-element.25.one), channel_id=1, source_target_pairs={{0,2},{1,3},{2,0},{3,1},{4,6},{5,7},{6,4},{7,5},{8,10},{9,11},{10,... | collective-permute-start | bytes 589832 | tf_op jit(solution)/shard_map/ppermute | solution.py:31
  16.4 30.4 %collective-permute-start.8 = (bf16[768,768]{1,0:T(8,128)(2,1)}, bf16[768,768]{1,0:T(8,128)(2,1)S(1)}, u32[]{:S(2)}, u32[]{:S(2)}) collective-permute-start(bf16[768,768]{1,0:T(8,128)(2,1)} %get-tuple-element.31), channel_id=1, source_target_pairs={{0,0},{1,16},{2,2},{3,18},{4,4},{5,20},{6,6},{7,22},{8,8},{9,24},{... | collective-permute-start | bytes 3538952 | tf_op jit(solution)/shard_map/ppermute | solution.py:31
  18.3 29.0 %collective-permute-start.9 = (bf16[768,768]{1,0:T(8,128)(2,1)}, bf16[768,768]{1,0:T(8,128)(2,1)S(1)}, u32[]{:S(2)}, u32[]{:S(2)}) collective-permute-start(bf16[768,768]{1,0:T(8,128)(2,1)} %get-tuple-element.31), channel_id=1, source_target_pairs={{0,2},{1,18},{2,0},{3,16},{4,6},{5,22},{6,4},{7,20},{8,10},{9,26},... | collective-permute-start | bytes 3538952 | tf_op jit(solution)/shard_map/ppermute | solution.py:31
  22.7 12.0 %collective-permute-start.2 = (bf16[2,768,128]{2,1,0:T(8,128)(2,1)S(1)}, bf16[2,768,128]{2,1,0:T(8,128)(2,1)S(1)}, u32[]{:S(2)}, u32[]{:S(2)}) collective-permute-start(bf16[2,768,128]{2,1,0:T(8,128)(2,1)S(1)} %shard_map.47.own), channel_id=1, source_target_pairs={{0,32},{1,33},{2,34},{3,35},{4,36},{5,37},{6,38},{7,39},{8,40},{9,... | collective-permute-start | bytes 1179656 | tf_op jit(solution)/shard_map/ppermute | solution.py:31
  23.9 13.4 %collective-permute-start.3 = (bf16[2,768,128]{2,1,0:T(8,128)(2,1)S(1)}, bf16[2,768,128]{2,1,0:T(8,128)(2,1)S(1)}, u32[]{:S(2)}, u32[]{:S(2)}) collective-permute-start(bf16[2,768,128]{2,1,0:T(8,128)(2,1)S(1)} %shard_map.47.own), channel_id=1, source_target_pairs={{0,224},{1,225},{2,226},{3,227},{4,228},{5,229},{6,230},{7,231},{8... | collective-permute-start | bytes 1179656 | tf_op jit(solution)/shard_map/ppermute | solution.py:31
  27.4 11.4 %collective-permute-start.5 = (bf16[2,768,128]{2,1,0:T(8,128)(2,1)S(1)}, bf16[2,768,128]{2,1,0:T(8,128)(2,1)S(1)}, u32[]{:S(2)}, u32[]{:S(2)}) collective-permute-start(bf16[2,768,128]{2,1,0:T(8,128)(2,1)S(1)} %shard_map.48.refs_0_), channel_id=1, source_target_pairs={{0,4},{1,5},{2,6},{3,7},{4,8},{5,9},{6,10},{7,11},{8,12},{9,13},{1... | collective-permute-start | bytes 1179656 | tf_op jit(solution)/shard_map/ppermute | solution.py:31
  34.7 9.4 %collective-permute-start.10 = (bf16[2,768,128]{2,1,0:T(8,128)(2,1)S(1)}, bf16[2,768,128]{2,1,0:T(8,128)(2,1)S(1)}, u32[]{:S(2)}, u32[]{:S(2)}) collective-permute-start(bf16[2,768,128]{2,1,0:T(8,128)(2,1)S(1)} %shard_map.48.refs_0_), channel_id=1, source_target_pairs={{0,12},{1,13},{2,14},{3,15},{4,0},{5,1},{6,2},{7,3},{8,4},{9,5},{1... | collective-permute-start | bytes 1179656 | tf_op jit(solution)/shard_map/ppermute | solution.py:31
  38.9 7.0 %collective-permute-start.6 = (bf16[768,128]{1,0:T(8,128)(2,1)S(1)}, bf16[768,128]{1,0:T(8,128)(2,1)S(1)}, u32[]{:S(2)}, u32[]{:S(2)}) collective-permute-start(bf16[768,128]{1,0:T(8,128)(2,1)S(1)} %slice_bitcast_fusion.3), channel_id=1, source_target_pairs={{0,32},{1,33},{2,34},{3,35},{4,36},{5,37},{6,38},{7,39},{8,40},{9,... | collective-permute-start | bytes 589832 | tf_op jit(solution)/shard_map/ppermute | solution.py:31
  40.7 5.7 %collective-permute-start.7 = (bf16[768,128]{1,0:T(8,128)(2,1)S(1)}, bf16[768,128]{1,0:T(8,128)(2,1)S(1)}, u32[]{:S(2)}, u32[]{:S(2)}) collective-permute-start(bf16[768,128]{1,0:T(8,128)(2,1)S(1)} %slice_bitcast_fusion.2), channel_id=1, source_target_pairs={{0,224},{1,225},{2,226},{3,227},{4,228},{5,229},{6,230},{7,231},{8... | collective-permute-start | bytes 589832 | tf_op jit(solution)/shard_map/ppermute | solution.py:31
  44.1 8.1 %copy-start = (bf16[2,768,128]{2,1,0:T(8,128)(2,1)}, bf16[2,768,128]{2,1,0:T(8,128)(2,1)S(1)}, u32[]{:S(2)}) copy-start(bf16[2,768,128]{2,1,0:T(8,128)(2,1)S(1)} %collective-permute-done.10.refs_3_) | copy-start | bytes 1179652
  47.3 6.2 %collective-permute-start.11 = (bf16[768,768]{1,0:T(8,128)(2,1)S(1)}, bf16[768,768]{1,0:T(8,128)(2,1)S(1)}, u32[]{:S(2)}, u32[]{:S(2)}) collective-permute-start(bf16[768,768]{1,0:T(8,128)(2,1)S(1)} %collective-permute-done.8.one), channel_id=1, source_target_pairs={{0,1},{1,0},{2,3},{3,2},{4,5},{5,4},{6,7},{7,6},{8,9},{9,8},{10,11... | collective-permute-start | bytes 3538952 | tf_op jit(solution)/shard_map/ppermute | solution.py:31
  47.3 6.2 %collective-permute-start.12 = (bf16[768,768]{1,0:T(8,128)(2,1)S(1)}, bf16[768,768]{1,0:T(8,128)(2,1)S(1)}, u32[]{:S(2)}, u32[]{:S(2)}) collective-permute-start(bf16[768,768]{1,0:T(8,128)(2,1)S(1)} %collective-permute-done.9.two), channel_id=1, source_target_pairs={{0,1},{1,0},{2,3},{3,2},{4,5},{5,4},{6,7},{7,6},{8,9},{9,8},{10,11... | collective-permute-start | bytes 3538952 | tf_op jit(solution)/shard_map/ppermute | solution.py:31
  47.9 8.2 %collective-permute-start.13 = (bf16[768,128]{1,0:T(8,128)(2,1)S(1)}, bf16[768,128]{1,0:T(8,128)(2,1)S(1)}, u32[]{:S(2)}, u32[]{:S(2)}) collective-permute-start(bf16[768,128]{1,0:T(8,128)(2,1)S(1)} %slice_bitcast_fusion.1), channel_id=1, source_target_pairs={{0,4},{1,5},{2,6},{3,7},{4,8},{5,9},{6,10},{7,11},{8,12},{9,13},{1... | collective-permute-start | bytes 589832 | tf_op jit(solution)/shard_map/ppermute | solution.py:31
  49.6 7.2 %collective-permute-start.14 = (bf16[768,128]{1,0:T(8,128)(2,1)S(1)}, bf16[768,128]{1,0:T(8,128)(2,1)S(1)}, u32[]{:S(2)}, u32[]{:S(2)}) collective-permute-start(bf16[768,128]{1,0:T(8,128)(2,1)S(1)} %slice_bitcast_fusion), channel_id=1, source_target_pairs={{0,12},{1,13},{2,14},{3,15},{4,0},{5,1},{6,2},{7,3},{8,4},{9,5},{1... | collective-permute-start | bytes 589832 | tf_op jit(solution)/shard_map/ppermute | solution.py:31
  56.1 9.7 %copy-start.1 = (bf16[2,768,128]{2,1,0:T(8,128)(2,1)S(1)}, bf16[2,768,128]{2,1,0:T(8,128)(2,1)}, u32[]{:S(2)}) copy-start(bf16[2,768,128]{2,1,0:T(8,128)(2,1)} %copy-done) | copy-start | bytes 1179652
  57.5 6.5 %copy-start.10 = (bf16[768,128]{1,0:T(8,128)(2,1)S(1)}, bf16[768,128]{1,0:T(8,128)(2,1)}, u32[]{:S(2)}) copy-start(bf16[768,128]{1,0:T(8,128)(2,1)} %copy-done.9) | copy-start | bytes 589828
  57.5 25.9 %all-to-all-start = ((bf16[8,768,128]{2,1,0:T(8,128)(2,1)}), bf16[8,768,128]{2,1,0:T(8,128)(2,1)S(1)}, u32[]{:S(2)}, u32[]{:S(2)}) async-start(bf16[8,768,128]{2,1,0:T(8,128)(2,1)} %shard_map.51), calls=%async_computation | async-start | bytes 3145728 | tf_op jit(solution)/shard_map/all_to_all | solution.py:284
  64.9 2.0 %collective-permute-start.17 = (bf16[2,768,128]{2,1,0:T(8,128)(2,1)S(1)}, bf16[2,768,128]{2,1,0:T(8,128)(2,1)S(1)}, u32[]{:S(2)}, u32[]{:S(2)}) collective-permute-start(bf16[2,768,128]{2,1,0:T(8,128)(2,1)S(1)} %shard_map.52.refs_2_), channel_id=1, source_target_pairs={{0,1},{1,0},{2,3},{3,2},{4,5},{5,4},{6,7},{7,6},{8,9},{9,8},{10,11... | collective-permute-start | bytes 1179656 | tf_op jit(solution)/shard_map/ppermute | solution.py:31
  65.2 2.3 %collective-permute-start.15 = (bf16[2,768,128]{2,1,0:T(8,128)(2,1)S(1)}, bf16[2,768,128]{2,1,0:T(8,128)(2,1)S(1)}, u32[]{:S(2)}, u32[]{:S(2)}) collective-permute-start(bf16[2,768,128]{2,1,0:T(8,128)(2,1)S(1)} %shard_map.48.refs_0_), channel_id=1, source_target_pairs={{0,1},{1,0},{2,3},{3,2},{4,5},{5,4},{6,7},{7,6},{8,9},{9,8},{10,11... | collective-permute-start | bytes 1179656 | tf_op jit(solution)/shard_map/ppermute | solution.py:31
  65.7 2.6 %collective-permute-start.16 = (bf16[2,768,128]{2,1,0:T(8,128)(2,1)S(1)}, bf16[2,768,128]{2,1,0:T(8,128)(2,1)S(1)}, u32[]{:S(2)}, u32[]{:S(2)}) collective-permute-start(bf16[2,768,128]{2,1,0:T(8,128)(2,1)S(1)} %collective-permute-done.5.refs_1_), channel_id=1, source_target_pairs={{0,1},{1,0},{2,3},{3,2},{4,5},{5,4},{6,7},{7,6},{8,9},{9,8},{10,11... | collective-permute-start | bytes 1179656 | tf_op jit(solution)/shard_map/ppermute | solution.py:31
  65.8 3.2 %collective-permute-start.18 = (bf16[2,768,128]{2,1,0:T(8,128)(2,1)S(1)}, bf16[2,768,128]{2,1,0:T(8,128)(2,1)S(1)}, u32[]{:S(2)}, u32[]{:S(2)}) collective-permute-start(bf16[2,768,128]{2,1,0:T(8,128)(2,1)S(1)} %copy-done.1), channel_id=1, source_target_pairs={{0,1},{1,0},{2,3},{3,2},{4,5},{5,4},{6,7},{7,6},{8,9},{9,8},{10,11... | collective-permute-start | bytes 1179656 | tf_op jit(solution)/shard_map/ppermute | solution.py:31
  83.4 1.0 copy-start.3
  (9 other events, 7.5 us)

commit v7 on v6

--- a/solution.py
+++ b/solution.py
@@ -104,14 +104,14 @@
 ANY = pl.BlockSpec(memory_space=pl.ANY)
 
 
-def on_device(kernel, shape, dtype, specs, scratch=(), cost=None, grant=1):
+def on_device(kernel, shape, dtype, specs, scratch=(), cost=None, grant=0.25):
     return pl.pallas_call(
         kernel,
         out_shape=jax.ShapeDtypeStruct(shape, dtype),
         in_specs=specs,
         out_specs=VMEM,
         scratch_shapes=scratch,
-        compiler_params=pltpu.CompilerParams(vmem_limit_bytes=grant << 20),
+        compiler_params=pltpu.CompilerParams(vmem_limit_bytes=int(grant * 2**20)),
         cost_estimate=cost,
     )
 
@@ -207,21 +207,11 @@
         jnp.bfloat16,
         [VMEM] * (3 + len(before)),
         cost=pl.CostEstimate(flops=4 * size * size * LANES * BLOCK, bytes_accessed=6 << 20, transcendentals=0),
-        grant=3,
+        grant=2,
     )(p_all, one, two, *before)
 
 
-def c_kernel(parts_ref, *refs):
-    pairs, (out_ref, w_ref) = refs[: 2 * LANES], refs[2 * LANES :]
-    for start in range(0, parts_ref.shape[1], BLOCK):
-        rows = slice(start, start + BLOCK)
-        w = parts_ref[0, rows].astype(jnp.float32)
-        for i in range(1, parts_ref.shape[0]):
-            w += parts_ref[i, rows].astype(jnp.float32)
-        turned = w.T
-        high = turned.astype(jnp.bfloat16)
-        w_ref[:BLOCK, rows] = high
-        w_ref[BLOCK:, rows] = (turned - high.astype(jnp.float32)).astype(jnp.bfloat16)
+def coarse_chunks(w_ref, pairs, out_ref):
     units = [pair.at[i] for pair in pairs for i in range(2)]
     top = jnp.zeros((BLOCK, BLOCK), jnp.float32)
     for i, unit in enumerate(units):
@@ -237,17 +227,40 @@
         out_ref[i, BLOCK:] = jnp.broadcast_to(power, (8, BLOCK))
 
 
+def own_kernel(parts_ref, *refs):
+    pairs, (out_ref, w_ref) = refs[:LANES], refs[LANES:]
+    for start in range(0, parts_ref.shape[1], BLOCK):
+        rows = slice(start, start + BLOCK)
+        w = parts_ref[0, rows].astype(jnp.float32)
+        for i in range(1, parts_ref.shape[0]):
+            w += parts_ref[i, rows].astype(jnp.float32)
+        turned = w.T
+        high = turned.astype(jnp.bfloat16)
+        w_ref[:BLOCK, rows] = high
+        w_ref[BLOCK:, rows] = (turned - high.astype(jnp.float32)).astype(jnp.bfloat16)
+    coarse_chunks(w_ref, pairs, out_ref)
+
+
+def other_kernel(w_ref, *refs):
+    coarse_chunks(w_ref, refs[:LANES], refs[LANES])
+
+
 def c_products(parts, pairs):
     size = parts.shape[1]
-    return on_device(
-        c_kernel,
-        (4 * LANES, BLOCK + 8, BLOCK),
-        jnp.float32,
-        [VMEM] * (2 * LANES + 1),
-        [pltpu.VMEM((2 * BLOCK, size), jnp.bfloat16)],
-        pl.CostEstimate(flops=16 * LANES * size * BLOCK * BLOCK, bytes_accessed=6 << 20, transcendentals=0),
-        grant=2,
-    )(parts, *pairs)
+    cost = pl.CostEstimate(flops=8 * LANES * size * BLOCK * BLOCK, bytes_accessed=4 << 20, transcendentals=0)
+    chunks = jax.ShapeDtypeStruct((2 * LANES, BLOCK + 8, BLOCK), jnp.float32)
+    own, w_both = pl.pallas_call(
+        own_kernel,
+        out_shape=[chunks, jax.ShapeDtypeStruct((2 * BLOCK, size), jnp.bfloat16)],
+        in_specs=[VMEM] * (LANES + 1),
+        out_specs=[VMEM] * 2,
+        compiler_params=pltpu.CompilerParams(vmem_limit_bytes=2 << 20),
+        cost_estimate=cost,
+    )(parts, *pairs[:LANES])
+    other = on_device(
+        other_kernel, chunks.shape, chunks.dtype, [VMEM] * (LANES + 1), cost=cost, grant=2
+    )(w_both, *pairs[LANES:])
+    return jnp.concatenate([own, other])
 
 
 def unpack(parts):

time: 115 us -> 113 us (0.983)
  local copies, waits for them, and re-layouts: 9.28 us -> 3.98 us
  waiting for transfers between devices: 30.9 us -> 33.2 us
  Pallas kernels: 9.81 us -> 11.3 us
    unnamed x26 -> x14, local copies, waits for them, and re-layouts: 8.5 us -> 3.2 us
    all_to_all x1, waiting for transfers between devices: 13.6 us -> 17.2 us  [local(): lax.all_to_all(w_part, AXES, 0, 0, axis_index_groups=W_GROUPS, tiled=True)]
    pallas_call x1 -> x2, Pallas kernels: 2.17 us -> 3.65 us  [the longest x1 2.33 us: c_products(): on_device(other_kernel, chunks.shape, chunks.dtype, [VMEM] * (LANES + 1),...]
    ppermute x19, waiting for transfers between devices: 17.3 us -> 16.1 us  [send(): return lax.ppermute(value, AXES, pairs)]
  transfers between devices with their start and end apart: 20 -> 20, of which waited for: 11 -> 9; matrix products, arithmetic and copies ran while one was open for 0% -> 0% of each run, Pallas kernels for 4% -> 5%
where the time goes in v7:
time: 113 us
  starting transfers between devices  39.1 us (35%)
  waiting for transfers between devices  33.2 us (29%)
  blocking collectives  24.5 us (22%)
  Pallas kernels  11.3 us (10%)
  local copies, waits for them, and re-layouts  3.98 us (4%)
    ppermute x19, starting transfers between devices, send(): return lax.ppermute(value, AXES, pairs)  32.6 us
    all_to_all x1, blocking collectives, local(): lax.all_to_all(c_part, AXES, 0, 0, axis_index_groups=C_GROUPS, tiled=True)  24.5 us
    all_to_all x1, waiting for transfers between devices, local(): lax.all_to_all(w_part, AXES, 0, 0, axis_index_groups=W_GROUPS, tiled=True)  17.2 us
    ppermute x19, waiting for transfers between devices, send(): return lax.ppermute(value, AXES, pairs)  16.1 us
    all_to_all x1, starting transfers between devices, local(): lax.all_to_all(w_part, AXES, 0, 0, axis_index_groups=W_GROUPS, tiled=True)  6.53 us
    pallas_call x2, Pallas kernels, w_products(): on_device(functools.partial(w_kernel, LANES * len(before)), (LANES * (1 +...  3.92 us
    unnamed x14, local copies, waits for them, and re-layouts  3.2 us
    pallas_call x1, Pallas kernels, masked(): pl.pallas_call(mask_kernel, out_shape=[jax.ShapeDtypeStruct(v.shape, v.dt...  2.78 us
  transfers between devices with their start and end apart: 20, of which 9 were waited for; matrix products, arithmetic and copies ran while one was open for 0% of the time, Pallas kernels for 5%

profile of v7, /device:TPU:2, one launch (start us, length us, event | category | flops | bytes accessed | tf_op | source)
XLA Modules:
  0.0 113.0 jit_solution(2660386831168971821)
XLA Ops:
  0.0 2.8 %shard_map.46 = (bf16[768,128]{1,0:T(8,128)(2,1)}, bf16[768,768]{1,0:T(8,128)(2,1)}) custom-call(bf16[768,128]{1,0:T(8,128)(2,1)} %p_any.1, bf16[768,768]{1,0:T(8,128)(2,1)} %a_any.1, s32[1,6]{1,0:T(1,128)} %bitcast.14, s32[6,6]{1,0:T(8,128)} %a_pattern.1), custom_call_target="tpu_custom_call" | custom-call | flops 589824 | bytes 4194304 | tf_op jit(solution)/shard_map/pallas_call | solution.py:141
  2.8 1.6 %collective-permute-start = (bf16[768,128]{1,0:T(8,128)(2,1)}, bf16[768,128]{1,0:T(8,128)(2,1)S(1)}, u32[]{:S(2)}, u32[]{:S(2)}) collective-permute-start(bf16[768,128]{1,0:T(8,128)(2,1)} %get-tuple-element.27.one), channel_id=1, source_target_pairs={{0,0},{1,1},{2,2},{3,3},{4,224},{5,225},{6,226},{7,227},{8,192},{9... | collective-permute-start | bytes 589832 | tf_op jit(solution)/shard_map/ppermute | solution.py:31
  4.4 9.9 %collective-permute-start.1 = (bf16[768,128]{1,0:T(8,128)(2,1)}, bf16[768,128]{1,0:T(8,128)(2,1)S(1)}, u32[]{:S(2)}, u32[]{:S(2)}) collective-permute-start(bf16[768,128]{1,0:T(8,128)(2,1)} %get-tuple-element.27.one), channel_id=1, source_target_pairs={{0,128},{1,129},{2,130},{3,131},{4,96},{5,97},{6,98},{7,99},{8,64}... | collective-permute-start | bytes 589832 | tf_op jit(solution)/shard_map/ppermute | solution.py:31
  14.3 2.1 %collective-permute-start.4 = (bf16[768,128]{1,0:T(8,128)(2,1)}, bf16[768,128]{1,0:T(8,128)(2,1)S(1)}, u32[]{:S(2)}, u32[]{:S(2)}) collective-permute-start(bf16[768,128]{1,0:T(8,128)(2,1)} %get-tuple-element.27.one), channel_id=1, source_target_pairs={{0,2},{1,3},{2,0},{3,1},{4,6},{5,7},{6,4},{7,5},{8,10},{9,11},{10,... | collective-permute-start | bytes 589832 | tf_op jit(solution)/shard_map/ppermute | solution.py:31
  16.4 1.9 %collective-permute-start.8 = (bf16[768,768]{1,0:T(8,128)(2,1)}, bf16[768,768]{1,0:T(8,128)(2,1)S(1)}, u32[]{:S(2)}, u32[]{:S(2)}) collective-permute-start(bf16[768,768]{1,0:T(8,128)(2,1)} %get-tuple-element.33), channel_id=1, source_target_pairs={{0,0},{1,16},{2,2},{3,18},{4,4},{5,20},{6,6},{7,22},{8,8},{9,24},{... | collective-permute-start | bytes 3538952 | tf_op jit(solution)/shard_map/ppermute | solution.py:31
  18.3 1.7 %collective-permute-start.9 = (bf16[768,768]{1,0:T(8,128)(2,1)}, bf16[768,768]{1,0:T(8,128)(2,1)S(1)}, u32[]{:S(2)}, u32[]{:S(2)}) collective-permute-start(bf16[768,768]{1,0:T(8,128)(2,1)} %get-tuple-element.33), channel_id=1, source_target_pairs={{0,2},{1,18},{2,0},{3,16},{4,6},{5,22},{6,4},{7,20},{8,10},{9,26},... | collective-permute-start | bytes 3538952 | tf_op jit(solution)/shard_map/ppermute | solution.py:31
  20.1 2.5 %collective-permute-done.1.two = bf16[768,128]{1,0:T(8,128)(2,1)S(1)} collective-permute-done((bf16[768,128]{1,0:T(8,128)(2,1)}, bf16[768,128]{1,0:T(8,128)(2,1)S(1)}, u32[]{:S(2)}, u32[]{:S(2)}) %collective-permute-start.1) | collective-permute-done | bytes 196640 | tf_op jit(solution)/shard_map/ppermute | solution.py:31
  23.9 2.5 %collective-permute-start.3 = (bf16[2,768,128]{2,1,0:T(8,128)(2,1)S(1)}, bf16[2,768,128]{2,1,0:T(8,128)(2,1)S(1)}, u32[]{:S(2)}, u32[]{:S(2)}) collective-permute-start(bf16[2,768,128]{2,1,0:T(8,128)(2,1)S(1)} %shard_map.47.own), channel_id=1, source_target_pairs={{0,224},{1,225},{2,226},{3,227},{4,228},{5,229},{6,230},{7,231},{8... | collective-permute-start | bytes 1179656 | tf_op jit(solution)/shard_map/ppermute | solution.py:31
  27.7 7.0 %collective-permute-done.2.below = bf16[2,768,128]{2,1,0:T(8,128)(2,1)S(1)} collective-permute-done((bf16[2,768,128]{2,1,0:T(8,128)(2,1)S(1)}, bf16[2,768,128]{2,1,0:T(8,128)(2,1)S(1)}, u32[]{:S(2)}, u32[]{:S(2)}) %collective-permute-start.2) | collective-permute-done | bytes 393248 | tf_op jit(solution)/shard_map/ppermute | solution.py:31
  34.7 2.7 %collective-permute-start.10 = (bf16[2,768,128]{2,1,0:T(8,128)(2,1)S(1)}, bf16[2,768,128]{2,1,0:T(8,128)(2,1)S(1)}, u32[]{:S(2)}, u32[]{:S(2)}) collective-permute-start(bf16[2,768,128]{2,1,0:T(8,128)(2,1)S(1)} %shard_map.48.refs_0_), channel_id=1, source_target_pairs={{0,12},{1,13},{2,14},{3,15},{4,0},{5,1},{6,2},{7,3},{8,4},{9,5},{1... | collective-permute-start | bytes 1179656 | tf_op jit(solution)/shard_map/ppermute | solution.py:31
  37.3 1.5 %collective-permute-done.5.refs_1_ = bf16[2,768,128]{2,1,0:T(8,128)(2,1)S(1)} collective-permute-done((bf16[2,768,128]{2,1,0:T(8,128)(2,1)S(1)}, bf16[2,768,128]{2,1,0:T(8,128)(2,1)S(1)}, u32[]{:S(2)}, u32[]{:S(2)}) %collective-permute-start.5) | collective-permute-done | bytes 393248 | tf_op jit(solution)/shard_map/ppermute | solution.py:31
  38.9 1.8 %collective-permute-start.6 = (bf16[768,128]{1,0:T(8,128)(2,1)S(1)}, bf16[768,128]{1,0:T(8,128)(2,1)S(1)}, u32[]{:S(2)}, u32[]{:S(2)}) collective-permute-start(bf16[768,128]{1,0:T(8,128)(2,1)S(1)} %slice_bitcast_fusion.3), channel_id=1, source_target_pairs={{0,32},{1,33},{2,34},{3,35},{4,36},{5,37},{6,38},{7,39},{8,40},{9,... | collective-permute-start | bytes 589832 | tf_op jit(solution)/shard_map/ppermute | solution.py:31
  40.7 1.6 %collective-permute-start.7 = (bf16[768,128]{1,0:T(8,128)(2,1)S(1)}, bf16[768,128]{1,0:T(8,128)(2,1)S(1)}, u32[]{:S(2)}, u32[]{:S(2)}) collective-permute-start(bf16[768,128]{1,0:T(8,128)(2,1)S(1)} %slice_bitcast_fusion.2), channel_id=1, source_target_pairs={{0,224},{1,225},{2,226},{3,227},{4,228},{5,229},{6,230},{7,231},{8... | collective-permute-start | bytes 589832 | tf_op jit(solution)/shard_map/ppermute | solution.py:31
  42.3 1.8 %collective-permute-done.10.refs_3_ = bf16[2,768,128]{2,1,0:T(8,128)(2,1)S(1)} collective-permute-done((bf16[2,768,128]{2,1,0:T(8,128)(2,1)S(1)}, bf16[2,768,128]{2,1,0:T(8,128)(2,1)S(1)}, u32[]{:S(2)}, u32[]{:S(2)}) %collective-permute-start.10) | collective-permute-done | bytes 393248 | tf_op jit(solution)/shard_map/ppermute | solution.py:31
  44.1 1.8 %collective-permute-done.6.up_two = bf16[768,128]{1,0:T(8,128)(2,1)S(1)} collective-permute-done((bf16[768,128]{1,0:T(8,128)(2,1)S(1)}, bf16[768,128]{1,0:T(8,128)(2,1)S(1)}, u32[]{:S(2)}, u32[]{:S(2)}) %collective-permute-start.6) | collective-permute-done | bytes 196640 | tf_op jit(solution)/shard_map/ppermute | solution.py:31
  47.9 1.7 %collective-permute-start.13 = (bf16[768,128]{1,0:T(8,128)(2,1)S(1)}, bf16[768,128]{1,0:T(8,128)(2,1)S(1)}, u32[]{:S(2)}, u32[]{:S(2)}) collective-permute-start(bf16[768,128]{1,0:T(8,128)(2,1)S(1)} %slice_bitcast_fusion.1), channel_id=1, source_target_pairs={{0,4},{1,5},{2,6},{3,7},{4,8},{5,9},{6,10},{7,11},{8,12},{9,13},{1... | collective-permute-start | bytes 589832 | tf_op jit(solution)/shard_map/ppermute | solution.py:31
  49.6 1.6 %collective-permute-start.14 = (bf16[768,128]{1,0:T(8,128)(2,1)S(1)}, bf16[768,128]{1,0:T(8,128)(2,1)S(1)}, u32[]{:S(2)}, u32[]{:S(2)}) collective-permute-start(bf16[768,128]{1,0:T(8,128)(2,1)S(1)} %slice_bitcast_fusion), channel_id=1, source_target_pairs={{0,12},{1,13},{2,14},{3,15},{4,0},{5,1},{6,2},{7,3},{8,4},{9,5},{1... | collective-permute-start | bytes 589832 | tf_op jit(solution)/shard_map/ppermute | solution.py:31
  52.1 1.4 %shard_map.50.rest_0_ = bf16[4,768,128]{2,1,0:T(8,128)(2,1)S(1)} custom-call(bf16[2,768,512]{2,1,0:T(8,128)(2,1)S(1)} %shard_map.49.p_ref, bf16[768,768]{1,0:T(8,128)(2,1)S(1)} %collective-permute-done.8.one, bf16[768,768]{1,0:T(8,128)(2,1)S(1)} %collective-permute-done.9.two), custom_call_target="tpu_custom_call" | custom-call | flops 1207959552 | bytes 6291456 | tf_op jit(solution)/shard_map/pallas_call | solution.py:204
  53.5 2.5 %shard_map.51 = bf16[8,768,128]{2,1,0:T(8,128)(2,1)} custom-call(bf16[2,768,512]{2,1,0:T(8,128)(2,1)S(1)} %shard_map.49.p_ref, bf16[768,768]{1,0:T(8,128)(2,1)S(1)} %collective-permute-done.11.one, bf16[768,768]{1,0:T(8,128)(2,1)S(1)} %collective-permute-done.12.two, bf16[4,768,128]{2,1,0:T(8,128)(2,1)S(1)} %shard_map.50.rest_0_), custom_call_target="tpu_custom_call" | custom-call | flops 1207959552 | bytes 6291456 | tf_op jit(solution)/shard_map/pallas_call | solution.py:204
  57.4 6.5 %all-to-all-start = ((bf16[8,768,128]{2,1,0:T(8,128)(2,1)}), bf16[8,768,128]{2,1,0:T(8,128)(2,1)S(1)}, u32[]{:S(2)}, u32[]{:S(2)}) async-start(bf16[8,768,128]{2,1,0:T(8,128)(2,1)} %shard_map.51), calls=%async_computation | async-start | bytes 3145728 | tf_op jit(solution)/shard_map/all_to_all | solution.py:297
  66.2 17.2 %all-to-all-done.parts_ref = bf16[8,768,128]{2,1,0:T(8,128)(2,1)S(1)} async-done(((bf16[8,768,128]{2,1,0:T(8,128)(2,1)}), bf16[8,768,128]{2,1,0:T(8,128)(2,1)S(1)}, u32[]{:S(2)}, u32[]{:S(2)}) %all-to-all-start) | async-done | bytes 1572896 | tf_op jit(solution)/shard_map/all_to_all | solution.py:297
  83.4 1.3 %shard_map.53 = (f32[8,136,128]{2,1,0:T(8,128)S(1)}, bf16[256,768]{1,0:T(8,128)(2,1)S(1)}) custom-call(bf16[8,768,128]{2,1,0:T(8,128)(2,1)S(1)} %all-to-all-done.parts_ref, bf16[2,768,128]{2,1,0:T(8,128)(2,1)S(1)} %shard_map.48.refs_0_, bf16[2,768,128]{2,1,0:T(8,128)(2,1)S(1)} %collective-permute-done.5.refs_1_, bf16[2,768,128]{2,1,0:T(8,128)(2,1)S(1)} %shard_map.52.refs_2_, ...), custom_call_target="tpu_custom_call" | custom-call | flops 402653184 | bytes 4194304 | tf_op jit(solution)/shard_map/pallas_call | solution.py:252
  84.7 2.3 %shard_map.54 = f32[8,136,128]{2,1,0:T(8,128)S(1)} custom-call(bf16[256,768]{1,0:T(8,128)(2,1)S(1)} %get-tuple-element.48.w_ref, bf16[2,768,128]{2,1,0:T(8,128)(2,1)} %collective-permute-done.15.refs_0_, bf16[2,768,128]{2,1,0:T(8,128)(2,1)} %collective-permute-done.16.refs_1_, bf16[2,768,128]{2,1,0:T(8,128)(2,1)S(1)} %collective-permute-done.17.refs_2_, ...), custom_call_target="tpu_custom_call" | custom-call | flops 402653184 | bytes 4194304 | tf_op jit(solution)/shard_map/pallas_call | solution.py:260
  87.3 24.5 %all_to_all.10 = f16[16,136,128]{2,1,0:T(8,128)(2,1)S(1)} all-to-all(f16[16,136,128]{2,1,0:T(8,128)(2,1)S(1)} %pad_maximum_fusion), channel_id=1, replica_groups={{0,32,192,224,128,160,64,96,16,48,208,240,144,176,80,112},{17,49,209,24..., dimensions={0} | all-to-all | bytes 1114112 | tf_op jit(solution)/shard_map/all_to_all | solution.py:299
  (52 shorter events, 10.5 us)
Async XLA Ops:
  2.8 17.4 %collective-permute-start = (bf16[768,128]{1,0:T(8,128)(2,1)}, bf16[768,128]{1,0:T(8,128)(2,1)S(1)}, u32[]{:S(2)}, u32[]{:S(2)}) collective-permute-start(bf16[768,128]{1,0:T(8,128)(2,1)} %get-tuple-element.27.one), channel_id=1, source_target_pairs={{0,0},{1,1},{2,2},{3,3},{4,224},{5,225},{6,226},{7,227},{8,192},{9... | collective-permute-start | bytes 589832 | tf_op jit(solution)/shard_map/ppermute | solution.py:31
  4.4 18.3 %collective-permute-start.1 = (bf16[768,128]{1,0:T(8,128)(2,1)}, bf16[768,128]{1,0:T(8,128)(2,1)S(1)}, u32[]{:S(2)}, u32[]{:S(2)}) collective-permute-start(bf16[768,128]{1,0:T(8,128)(2,1)} %get-tuple-element.27.one), channel_id=1, source_target_pairs={{0,128},{1,129},{2,130},{3,131},{4,96},{5,97},{6,98},{7,99},{8,64}... | collective-permute-start | bytes 589832 | tf_op jit(solution)/shard_map/ppermute | solution.py:31
  14.3 12.2 %collective-permute-start.4 = (bf16[768,128]{1,0:T(8,128)(2,1)}, bf16[768,128]{1,0:T(8,128)(2,1)S(1)}, u32[]{:S(2)}, u32[]{:S(2)}) collective-permute-start(bf16[768,128]{1,0:T(8,128)(2,1)} %get-tuple-element.27.one), channel_id=1, source_target_pairs={{0,2},{1,3},{2,0},{3,1},{4,6},{5,7},{6,4},{7,5},{8,10},{9,11},{10,... | collective-permute-start | bytes 589832 | tf_op jit(solution)/shard_map/ppermute | solution.py:31
  16.4 30.4 %collective-permute-start.8 = (bf16[768,768]{1,0:T(8,128)(2,1)}, bf16[768,768]{1,0:T(8,128)(2,1)S(1)}, u32[]{:S(2)}, u32[]{:S(2)}) collective-permute-start(bf16[768,768]{1,0:T(8,128)(2,1)} %get-tuple-element.33), channel_id=1, source_target_pairs={{0,0},{1,16},{2,2},{3,18},{4,4},{5,20},{6,6},{7,22},{8,8},{9,24},{... | collective-permute-start | bytes 3538952 | tf_op jit(solution)/shard_map/ppermute | solution.py:31
  18.3 29.0 %collective-permute-start.9 = (bf16[768,768]{1,0:T(8,128)(2,1)}, bf16[768,768]{1,0:T(8,128)(2,1)S(1)}, u32[]{:S(2)}, u32[]{:S(2)}) collective-permute-start(bf16[768,768]{1,0:T(8,128)(2,1)} %get-tuple-element.33), channel_id=1, source_target_pairs={{0,2},{1,18},{2,0},{3,16},{4,6},{5,22},{6,4},{7,20},{8,10},{9,26},... | collective-permute-start | bytes 3538952 | tf_op jit(solution)/shard_map/ppermute | solution.py:31
  22.7 12.0 %collective-permute-start.2 = (bf16[2,768,128]{2,1,0:T(8,128)(2,1)S(1)}, bf16[2,768,128]{2,1,0:T(8,128)(2,1)S(1)}, u32[]{:S(2)}, u32[]{:S(2)}) collective-permute-start(bf16[2,768,128]{2,1,0:T(8,128)(2,1)S(1)} %shard_map.47.own), channel_id=1, source_target_pairs={{0,32},{1,33},{2,34},{3,35},{4,36},{5,37},{6,38},{7,39},{8,40},{9,... | collective-permute-start | bytes 1179656 | tf_op jit(solution)/shard_map/ppermute | solution.py:31
  23.9 13.4 %collective-permute-start.3 = (bf16[2,768,128]{2,1,0:T(8,128)(2,1)S(1)}, bf16[2,768,128]{2,1,0:T(8,128)(2,1)S(1)}, u32[]{:S(2)}, u32[]{:S(2)}) collective-permute-start(bf16[2,768,128]{2,1,0:T(8,128)(2,1)S(1)} %shard_map.47.own), channel_id=1, source_target_pairs={{0,224},{1,225},{2,226},{3,227},{4,228},{5,229},{6,230},{7,231},{8... | collective-permute-start | bytes 1179656 | tf_op jit(solution)/shard_map/ppermute | solution.py:31
  26.5 0.9 copy-start.2
  27.4 11.4 %collective-permute-start.5 = (bf16[2,768,128]{2,1,0:T(8,128)(2,1)S(1)}, bf16[2,768,128]{2,1,0:T(8,128)(2,1)S(1)}, u32[]{:S(2)}, u32[]{:S(2)}) collective-permute-start(bf16[2,768,128]{2,1,0:T(8,128)(2,1)S(1)} %shard_map.48.refs_0_), channel_id=1, source_target_pairs={{0,4},{1,5},{2,6},{3,7},{4,8},{5,9},{6,10},{7,11},{8,12},{9,13},{1... | collective-permute-start | bytes 1179656 | tf_op jit(solution)/shard_map/ppermute | solution.py:31
  34.7 9.4 %collective-permute-start.10 = (bf16[2,768,128]{2,1,0:T(8,128)(2,1)S(1)}, bf16[2,768,128]{2,1,0:T(8,128)(2,1)S(1)}, u32[]{:S(2)}, u32[]{:S(2)}) collective-permute-start(bf16[2,768,128]{2,1,0:T(8,128)(2,1)S(1)} %shard_map.48.refs_0_), channel_id=1, source_target_pairs={{0,12},{1,13},{2,14},{3,15},{4,0},{5,1},{6,2},{7,3},{8,4},{9,5},{1... | collective-permute-start | bytes 1179656 | tf_op jit(solution)/shard_map/ppermute | solution.py:31
  38.9 7.0 %collective-permute-start.6 = (bf16[768,128]{1,0:T(8,128)(2,1)S(1)}, bf16[768,128]{1,0:T(8,128)(2,1)S(1)}, u32[]{:S(2)}, u32[]{:S(2)}) collective-permute-start(bf16[768,128]{1,0:T(8,128)(2,1)S(1)} %slice_bitcast_fusion.3), channel_id=1, source_target_pairs={{0,32},{1,33},{2,34},{3,35},{4,36},{5,37},{6,38},{7,39},{8,40},{9,... | collective-permute-start | bytes 589832 | tf_op jit(solution)/shard_map/ppermute | solution.py:31
  40.7 5.7 %collective-permute-start.7 = (bf16[768,128]{1,0:T(8,128)(2,1)S(1)}, bf16[768,128]{1,0:T(8,128)(2,1)S(1)}, u32[]{:S(2)}, u32[]{:S(2)}) collective-permute-start(bf16[768,128]{1,0:T(8,128)(2,1)S(1)} %slice_bitcast_fusion.2), channel_id=1, source_target_pairs={{0,224},{1,225},{2,226},{3,227},{4,228},{5,229},{6,230},{7,231},{8... | collective-permute-start | bytes 589832 | tf_op jit(solution)/shard_map/ppermute | solution.py:31
  44.1 8.1 %copy-start = (bf16[2,768,128]{2,1,0:T(8,128)(2,1)}, bf16[2,768,128]{2,1,0:T(8,128)(2,1)S(1)}, u32[]{:S(2)}) copy-start(bf16[2,768,128]{2,1,0:T(8,128)(2,1)S(1)} %collective-permute-done.10.refs_3_) | copy-start | bytes 1179652
  47.3 6.2 %collective-permute-start.11 = (bf16[768,768]{1,0:T(8,128)(2,1)S(1)}, bf16[768,768]{1,0:T(8,128)(2,1)S(1)}, u32[]{:S(2)}, u32[]{:S(2)}) collective-permute-start(bf16[768,768]{1,0:T(8,128)(2,1)S(1)} %collective-permute-done.8.one), channel_id=1, source_target_pairs={{0,1},{1,0},{2,3},{3,2},{4,5},{5,4},{6,7},{7,6},{8,9},{9,8},{10,11... | collective-permute-start | bytes 3538952 | tf_op jit(solution)/shard_map/ppermute | solution.py:31
  47.3 6.2 %collective-permute-start.12 = (bf16[768,768]{1,0:T(8,128)(2,1)S(1)}, bf16[768,768]{1,0:T(8,128)(2,1)S(1)}, u32[]{:S(2)}, u32[]{:S(2)}) collective-permute-start(bf16[768,768]{1,0:T(8,128)(2,1)S(1)} %collective-permute-done.9.two), channel_id=1, source_target_pairs={{0,1},{1,0},{2,3},{3,2},{4,5},{5,4},{6,7},{7,6},{8,9},{9,8},{10,11... | collective-permute-start | bytes 3538952 | tf_op jit(solution)/shard_map/ppermute | solution.py:31
  47.9 8.2 %collective-permute-start.13 = (bf16[768,128]{1,0:T(8,128)(2,1)S(1)}, bf16[768,128]{1,0:T(8,128)(2,1)S(1)}, u32[]{:S(2)}, u32[]{:S(2)}) collective-permute-start(bf16[768,128]{1,0:T(8,128)(2,1)S(1)} %slice_bitcast_fusion.1), channel_id=1, source_target_pairs={{0,4},{1,5},{2,6},{3,7},{4,8},{5,9},{6,10},{7,11},{8,12},{9,13},{1... | collective-permute-start | bytes 589832 | tf_op jit(solution)/shard_map/ppermute | solution.py:31
  49.6 7.1 %collective-permute-start.14 = (bf16[768,128]{1,0:T(8,128)(2,1)S(1)}, bf16[768,128]{1,0:T(8,128)(2,1)S(1)}, u32[]{:S(2)}, u32[]{:S(2)}) collective-permute-start(bf16[768,128]{1,0:T(8,128)(2,1)S(1)} %slice_bitcast_fusion), channel_id=1, source_target_pairs={{0,12},{1,13},{2,14},{3,15},{4,0},{5,1},{6,2},{7,3},{8,4},{9,5},{1... | collective-permute-start | bytes 589832 | tf_op jit(solution)/shard_map/ppermute | solution.py:31
  56.1 9.7 %copy-start.1 = (bf16[2,768,128]{2,1,0:T(8,128)(2,1)S(1)}, bf16[2,768,128]{2,1,0:T(8,128)(2,1)}, u32[]{:S(2)}) copy-start(bf16[2,768,128]{2,1,0:T(8,128)(2,1)} %copy-done) | copy-start | bytes 1179652
  57.4 6.5 %copy-start.4 = (bf16[768,128]{1,0:T(8,128)(2,1)S(1)}, bf16[768,128]{1,0:T(8,128)(2,1)}, u32[]{:S(2)}) copy-start(bf16[768,128]{1,0:T(8,128)(2,1)} %copy-done.3) | copy-start | bytes 589828
  57.4 26.0 %all-to-all-start = ((bf16[8,768,128]{2,1,0:T(8,128)(2,1)}), bf16[8,768,128]{2,1,0:T(8,128)(2,1)S(1)}, u32[]{:S(2)}, u32[]{:S(2)}) async-start(bf16[8,768,128]{2,1,0:T(8,128)(2,1)} %shard_map.51), calls=%async_computation | async-start | bytes 3145728 | tf_op jit(solution)/shard_map/all_to_all | solution.py:297
  64.9 19.8 %collective-permute-start.17 = (bf16[2,768,128]{2,1,0:T(8,128)(2,1)S(1)}, bf16[2,768,128]{2,1,0:T(8,128)(2,1)S(1)}, u32[]{:S(2)}, u32[]{:S(2)}) collective-permute-start(bf16[2,768,128]{2,1,0:T(8,128)(2,1)S(1)} %shard_map.52.refs_2_), channel_id=1, source_target_pairs={{0,1},{1,0},{2,3},{3,2},{4,5},{5,4},{6,7},{7,6},{8,9},{9,8},{10,11... | collective-permute-start | bytes 1179656 | tf_op jit(solution)/shard_map/ppermute | solution.py:31
  65.2 19.5 %collective-permute-start.15 = (bf16[2,768,128]{2,1,0:T(8,128)(2,1)S(1)}, bf16[2,768,128]{2,1,0:T(8,128)(2,1)}, u32[]{:S(2)}, u32[]{:S(2)}) collective-permute-start(bf16[2,768,128]{2,1,0:T(8,128)(2,1)S(1)} %shard_map.48.refs_0_), channel_id=1, source_target_pairs={{0,1},{1,0},{2,3},{3,2},{4,5},{5,4},{6,7},{7,6},{8,9},{9,8},{10,11... | collective-permute-start | bytes 1179656 | tf_op jit(solution)/shard_map/ppermute | solution.py:31
  65.7 19.0 %collective-permute-start.16 = (bf16[2,768,128]{2,1,0:T(8,128)(2,1)S(1)}, bf16[2,768,128]{2,1,0:T(8,128)(2,1)}, u32[]{:S(2)}, u32[]{:S(2)}) collective-permute-start(bf16[2,768,128]{2,1,0:T(8,128)(2,1)S(1)} %collective-permute-done.5.refs_1_), channel_id=1, source_target_pairs={{0,1},{1,0},{2,3},{3,2},{4,5},{5,4},{6,7},{7,6},{8,9},{9,8},{10,11... | collective-permute-start | bytes 1179656 | tf_op jit(solution)/shard_map/ppermute | solution.py:31
  65.8 19.0 %collective-permute-start.18 = (bf16[2,768,128]{2,1,0:T(8,128)(2,1)S(1)}, bf16[2,768,128]{2,1,0:T(8,128)(2,1)}, u32[]{:S(2)}, u32[]{:S(2)}) collective-permute-start(bf16[2,768,128]{2,1,0:T(8,128)(2,1)S(1)} %copy-done.1), channel_id=1, source_target_pairs={{0,1},{1,0},{2,3},{3,2},{4,5},{5,4},{6,7},{7,6},{8,9},{9,8},{10,11... | collective-permute-start | bytes 1179656 | tf_op jit(solution)/shard_map/ppermute | solution.py:31
  (3 other events, 2.3 us)

commit v8 on v7

--- a/solution.py
+++ b/solution.py
@@ -212,7 +212,9 @@
 
 
 def coarse_chunks(w_ref, pairs, out_ref):
-    units = [pair.at[i] for pair in pairs for i in range(2)]
+    units = []
+    for pair in pairs:
+        units += [pair.at[0], pair.at[1]] if len(pair.shape) == 3 else [pair]
     top = jnp.zeros((BLOCK, BLOCK), jnp.float32)
     for i, unit in enumerate(units):
         both = dot32(w_ref[...], unit[...])
@@ -228,7 +230,7 @@
 
 
 def own_kernel(parts_ref, *refs):
-    pairs, (out_ref, w_ref) = refs[:LANES], refs[LANES:]
+    pairs, (out_ref, w_ref) = refs[:-2], refs[-2:]
     for start in range(0, parts_ref.shape[1], BLOCK):
         rows = slice(start, start + BLOCK)
         w = parts_ref[0, rows].astype(jnp.float32)
@@ -242,24 +244,24 @@
 
 
 def other_kernel(w_ref, *refs):
-    coarse_chunks(w_ref, refs[:LANES], refs[LANES])
-
-
-def c_products(parts, pairs):
+    coarse_chunks(w_ref, refs[:-1], refs[-1])
+
+
+def c_products(parts, pairs, passed):
     size = parts.shape[1]
     cost = pl.CostEstimate(flops=8 * LANES * size * BLOCK * BLOCK, bytes_accessed=4 << 20, transcendentals=0)
     chunks = jax.ShapeDtypeStruct((2 * LANES, BLOCK + 8, BLOCK), jnp.float32)
     own, w_both = pl.pallas_call(
         own_kernel,
         out_shape=[chunks, jax.ShapeDtypeStruct((2 * BLOCK, size), jnp.bfloat16)],
-        in_specs=[VMEM] * (LANES + 1),
+        in_specs=[VMEM] * (len(pairs) + 1),
         out_specs=[VMEM] * 2,
         compiler_params=pltpu.CompilerParams(vmem_limit_bytes=2 << 20),
         cost_estimate=cost,
-    )(parts, *pairs[:LANES])
+    )(parts, *pairs)
     other = on_device(
-        other_kernel, chunks.shape, chunks.dtype, [VMEM] * (LANES + 1), cost=cost, grant=2
-    )(w_both, *pairs[LANES:])
+        other_kernel, chunks.shape, chunks.dtype, [VMEM] * (len(passed) + 1), cost=cost, grant=2
+    )(w_both, *passed)
     return jnp.concatenate([own, other])
 
 
@@ -292,10 +294,10 @@
     w_part = w_products(p_all, near, distant)
     w_part = w_products(p_all, near_2, distant_2, w_part)
     w_part, pair, pair_1, pair_3, *beyond = both(w_part, pair, pair_1, pair_3, *beyond)
-    pairs = [pair, pair_1, paired(*beyond), pair_3]
-    pairs += [send(p, other_core) for p in pairs]
+    pairs = [pair, pair_1, *beyond, pair_3]
+    passed = [send(p, other_core) for p in pairs]
     w_parts = lax.all_to_all(w_part, AXES, 0, 0, axis_index_groups=W_GROUPS, tiled=True)
-    c_part = c_products(w_parts, pairs).astype(jnp.float16)
+    c_part = c_products(w_parts, pairs, passed).astype(jnp.float16)
     return unpack(lax.all_to_all(c_part, AXES, 0, 0, axis_index_groups=C_GROUPS, tiled=True))
 
 

time: 113 us -> 114 us (level)
  local copies, waits for them, and re-layouts: 3.98 us -> 1.72 us
  waiting for transfers between devices: 33.2 us -> 34.7 us
    unnamed x14 -> x6, local copies, waits for them, and re-layouts: 3.2 us -> 0.93 us
    all_to_all x1, waiting for transfers between devices: 17.2 us -> 18.4 us  [local(): lax.all_to_all(w_part, AXES, 0, 0, axis_index_groups=W_GROUPS, tiled=True)]
    ppermute x19 -> x20, starting transfers between devices: 32.6 us -> 32.3 us  [send(): return lax.ppermute(value, AXES, pairs)]
    ppermute x19 -> x20, waiting for transfers between devices: 16.1 us -> 16.3 us  [send(): return lax.ppermute(value, AXES, pairs)]
  transfers between devices with their start and end apart: 20 -> 21, of which waited for: 9 -> 10; matrix products, arithmetic and copies ran while one was open for 0% -> 0% of each run, Pallas kernels for 5% -> 6%
where the time goes in v8:
time: 114 us; the launch traced here: 113 us
  starting transfers between devices  39.2 us (34%)
  waiting for transfers between devices  34.7 us (30%)
  blocking collectives  24.5 us (21%)
  Pallas kernels  12.3 us (11%)
  local copies, waits for them, and re-layouts  1.72 us (2%)
    ppermute x20, starting transfers between devices, send(): return lax.ppermute(value, AXES, pairs)  32.3 us
    all_to_all x1, blocking collectives, local(): lax.all_to_all(c_part, AXES, 0, 0, axis_index_groups=C_GROUPS, tiled=True)  24.5 us
    all_to_all x1, waiting for transfers between devices, local(): lax.all_to_all(w_part, AXES, 0, 0, axis_index_groups=W_GROUPS, tiled=True)  18.4 us
    ppermute x20, waiting for transfers between devices, send(): return lax.ppermute(value, AXES, pairs)  16.3 us
    all_to_all x1, starting transfers between devices, local(): lax.all_to_all(w_part, AXES, 0, 0, axis_index_groups=W_GROUPS, tiled=True)  6.91 us
    pallas_call x2, Pallas kernels, w_products(): on_device(functools.partial(w_kernel, LANES * len(before)), (LANES * (1 +...  3.93 us
    pallas_call x1, Pallas kernels, masked(): pl.pallas_call(mask_kernel, out_shape=[jax.ShapeDtypeStruct(v.shape, v.dt...  2.79 us
    pallas_call x1, Pallas kernels, c_products(): on_device(other_kernel, chunks.shape, chunks.dtype, [VMEM] * (len(passed)...  2.39 us
  transfers between devices with their start and end apart: 21, of which 10 were waited for; matrix products, arithmetic and copies ran while one was open for 0% of the time, Pallas kernels for 6%

profile of v8, /device:TPU:2, one launch (start us, length us, event | category | flops | bytes accessed | tf_op | source)
XLA Modules:
  0.0 113.4 jit_solution(17340085321807826443)
XLA Ops:
  0.0 2.8 %shard_map.46 = (bf16[768,128]{1,0:T(8,128)(2,1)}, bf16[768,768]{1,0:T(8,128)(2,1)}) custom-call(bf16[768,128]{1,0:T(8,128)(2,1)} %p_any.1, bf16[768,768]{1,0:T(8,128)(2,1)} %a_any.1, s32[1,6]{1,0:T(1,128)} %bitcast.14, s32[6,6]{1,0:T(8,128)} %a_pattern.1), custom_call_target="tpu_custom_call" | custom-call | flops 589824 | bytes 4194304 | tf_op jit(solution)/shard_map/pallas_call | solution.py:141
  2.8 1.6 %collective-permute-start = (bf16[768,128]{1,0:T(8,128)(2,1)}, bf16[768,128]{1,0:T(8,128)(2,1)S(1)}, u32[]{:S(2)}, u32[]{:S(2)}) collective-permute-start(bf16[768,128]{1,0:T(8,128)(2,1)} %get-tuple-element.27.one), channel_id=1, source_target_pairs={{0,0},{1,1},{2,2},{3,3},{4,224},{5,225},{6,226},{7,227},{8,192},{9... | collective-permute-start | bytes 589832 | tf_op jit(solution)/shard_map/ppermute | solution.py:31
  4.4 9.9 %collective-permute-start.1 = (bf16[768,128]{1,0:T(8,128)(2,1)}, bf16[768,128]{1,0:T(8,128)(2,1)S(1)}, u32[]{:S(2)}, u32[]{:S(2)}) collective-permute-start(bf16[768,128]{1,0:T(8,128)(2,1)} %get-tuple-element.27.one), channel_id=1, source_target_pairs={{0,128},{1,129},{2,130},{3,131},{4,96},{5,97},{6,98},{7,99},{8,64}... | collective-permute-start | bytes 589832 | tf_op jit(solution)/shard_map/ppermute | solution.py:31
  14.3 2.1 %collective-permute-start.4 = (bf16[768,128]{1,0:T(8,128)(2,1)}, bf16[768,128]{1,0:T(8,128)(2,1)S(1)}, u32[]{:S(2)}, u32[]{:S(2)}) collective-permute-start(bf16[768,128]{1,0:T(8,128)(2,1)} %get-tuple-element.27.one), channel_id=1, source_target_pairs={{0,2},{1,3},{2,0},{3,1},{4,6},{5,7},{6,4},{7,5},{8,10},{9,11},{10,... | collective-permute-start | bytes 589832 | tf_op jit(solution)/shard_map/ppermute | solution.py:31
  16.4 1.9 %collective-permute-start.8 = (bf16[768,768]{1,0:T(8,128)(2,1)}, bf16[768,768]{1,0:T(8,128)(2,1)S(1)}, u32[]{:S(2)}, u32[]{:S(2)}) collective-permute-start(bf16[768,768]{1,0:T(8,128)(2,1)} %get-tuple-element.33), channel_id=1, source_target_pairs={{0,0},{1,16},{2,2},{3,18},{4,4},{5,20},{6,6},{7,22},{8,8},{9,24},{... | collective-permute-start | bytes 3538952 | tf_op jit(solution)/shard_map/ppermute | solution.py:31
  18.3 1.7 %collective-permute-start.9 = (bf16[768,768]{1,0:T(8,128)(2,1)}, bf16[768,768]{1,0:T(8,128)(2,1)S(1)}, u32[]{:S(2)}, u32[]{:S(2)}) collective-permute-start(bf16[768,768]{1,0:T(8,128)(2,1)} %get-tuple-element.33), channel_id=1, source_target_pairs={{0,2},{1,18},{2,0},{3,16},{4,6},{5,22},{6,4},{7,20},{8,10},{9,26},... | collective-permute-start | bytes 3538952 | tf_op jit(solution)/shard_map/ppermute | solution.py:31
  20.2 2.5 %collective-permute-done.1.two = bf16[768,128]{1,0:T(8,128)(2,1)S(1)} collective-permute-done((bf16[768,128]{1,0:T(8,128)(2,1)}, bf16[768,128]{1,0:T(8,128)(2,1)S(1)}, u32[]{:S(2)}, u32[]{:S(2)}) %collective-permute-start.1) | collective-permute-done | bytes 196640 | tf_op jit(solution)/shard_map/ppermute | solution.py:31
  23.9 2.5 %collective-permute-start.3 = (bf16[2,768,128]{2,1,0:T(8,128)(2,1)S(1)}, bf16[2,768,128]{2,1,0:T(8,128)(2,1)S(1)}, u32[]{:S(2)}, u32[]{:S(2)}) collective-permute-start(bf16[2,768,128]{2,1,0:T(8,128)(2,1)S(1)} %shard_map.47.own), channel_id=1, source_target_pairs={{0,224},{1,225},{2,226},{3,227},{4,228},{5,229},{6,230},{7,231},{8... | collective-permute-start | bytes 1179656 | tf_op jit(solution)/shard_map/ppermute | solution.py:31
  27.7 7.0 %collective-permute-done.2.below = bf16[2,768,128]{2,1,0:T(8,128)(2,1)S(1)} collective-permute-done((bf16[2,768,128]{2,1,0:T(8,128)(2,1)S(1)}, bf16[2,768,128]{2,1,0:T(8,128)(2,1)S(1)}, u32[]{:S(2)}, u32[]{:S(2)}) %collective-permute-start.2) | collective-permute-done | bytes 393248 | tf_op jit(solution)/shard_map/ppermute | solution.py:31
  34.7 2.7 %collective-permute-start.10 = (bf16[2,768,128]{2,1,0:T(8,128)(2,1)S(1)}, bf16[2,768,128]{2,1,0:T(8,128)(2,1)S(1)}, u32[]{:S(2)}, u32[]{:S(2)}) collective-permute-start(bf16[2,768,128]{2,1,0:T(8,128)(2,1)S(1)} %shard_map.48.refs_0_), channel_id=1, source_target_pairs={{0,12},{1,13},{2,14},{3,15},{4,0},{5,1},{6,2},{7,3},{8,4},{9,5},{1... | collective-permute-start | bytes 1179656 | tf_op jit(solution)/shard_map/ppermute | solution.py:31
  37.4 1.5 %collective-permute-done.5.refs_1_ = bf16[2,768,128]{2,1,0:T(8,128)(2,1)S(1)} collective-permute-done((bf16[2,768,128]{2,1,0:T(8,128)(2,1)S(1)}, bf16[2,768,128]{2,1,0:T(8,128)(2,1)S(1)}, u32[]{:S(2)}, u32[]{:S(2)}) %collective-permute-start.5) | collective-permute-done | bytes 393248 | tf_op jit(solution)/shard_map/ppermute | solution.py:31
  38.9 1.8 %collective-permute-start.6 = (bf16[768,128]{1,0:T(8,128)(2,1)S(1)}, bf16[768,128]{1,0:T(8,128)(2,1)S(1)}, u32[]{:S(2)}, u32[]{:S(2)}) collective-permute-start(bf16[768,128]{1,0:T(8,128)(2,1)S(1)} %slice_bitcast_fusion.3), channel_id=1, source_target_pairs={{0,32},{1,33},{2,34},{3,35},{4,36},{5,37},{6,38},{7,39},{8,40},{9,... | collective-permute-start | bytes 589832 | tf_op jit(solution)/shard_map/ppermute | solution.py:31
  40.7 1.6 %collective-permute-start.7 = (bf16[768,128]{1,0:T(8,128)(2,1)S(1)}, bf16[768,128]{1,0:T(8,128)(2,1)S(1)}, u32[]{:S(2)}, u32[]{:S(2)}) collective-permute-start(bf16[768,128]{1,0:T(8,128)(2,1)S(1)} %slice_bitcast_fusion.2), channel_id=1, source_target_pairs={{0,224},{1,225},{2,226},{3,227},{4,228},{5,229},{6,230},{7,231},{8... | collective-permute-start | bytes 589832 | tf_op jit(solution)/shard_map/ppermute | solution.py:31
  42.3 1.8 %collective-permute-done.10.refs_4_ = bf16[2,768,128]{2,1,0:T(8,128)(2,1)S(1)} collective-permute-done((bf16[2,768,128]{2,1,0:T(8,128)(2,1)S(1)}, bf16[2,768,128]{2,1,0:T(8,128)(2,1)S(1)}, u32[]{:S(2)}, u32[]{:S(2)}) %collective-permute-start.10) | collective-permute-done | bytes 393248 | tf_op jit(solution)/shard_map/ppermute | solution.py:31
  44.1 1.8 %collective-permute-done.6.up_two = bf16[768,128]{1,0:T(8,128)(2,1)S(1)} collective-permute-done((bf16[768,128]{1,0:T(8,128)(2,1)S(1)}, bf16[768,128]{1,0:T(8,128)(2,1)S(1)}, u32[]{:S(2)}, u32[]{:S(2)}) %collective-permute-start.6) | collective-permute-done | bytes 196640 | tf_op jit(solution)/shard_map/ppermute | solution.py:31
  47.9 1.7 %collective-permute-start.13 = (bf16[768,128]{1,0:T(8,128)(2,1)S(1)}, bf16[768,128]{1,0:T(8,128)(2,1)}, u32[]{:S(2)}, u32[]{:S(2)}) collective-permute-start(bf16[768,128]{1,0:T(8,128)(2,1)S(1)} %slice_bitcast_fusion.1), channel_id=1, source_target_pairs={{0,4},{1,5},{2,6},{3,7},{4,8},{5,9},{6,10},{7,11},{8,12},{9,13},{1... | collective-permute-start | bytes 589832 | tf_op jit(solution)/shard_map/ppermute | solution.py:31
  49.6 1.6 %collective-permute-start.14 = (bf16[768,128]{1,0:T(8,128)(2,1)S(1)}, bf16[768,128]{1,0:T(8,128)(2,1)}, u32[]{:S(2)}, u32[]{:S(2)}) collective-permute-start(bf16[768,128]{1,0:T(8,128)(2,1)S(1)} %slice_bitcast_fusion), channel_id=1, source_target_pairs={{0,12},{1,13},{2,14},{3,15},{4,0},{5,1},{6,2},{7,3},{8,4},{9,5},{1... | collective-permute-start | bytes 589832 | tf_op jit(solution)/shard_map/ppermute | solution.py:31
  52.1 1.4 %shard_map.50.rest_0_ = bf16[4,768,128]{2,1,0:T(8,128)(2,1)S(1)} custom-call(bf16[2,768,512]{2,1,0:T(8,128)(2,1)S(1)} %shard_map.49.p_ref, bf16[768,768]{1,0:T(8,128)(2,1)S(1)} %collective-permute-done.8.one, bf16[768,768]{1,0:T(8,128)(2,1)S(1)} %collective-permute-done.9.two), custom_call_target="tpu_custom_call" | custom-call | flops 1207959552 | bytes 6291456 | tf_op jit(solution)/shard_map/pallas_call | solution.py:204
  53.5 2.6 %shard_map.51 = bf16[8,768,128]{2,1,0:T(8,128)(2,1)} custom-call(bf16[2,768,512]{2,1,0:T(8,128)(2,1)S(1)} %shard_map.49.p_ref, bf16[768,768]{1,0:T(8,128)(2,1)S(1)} %collective-permute-done.11.one, bf16[768,768]{1,0:T(8,128)(2,1)S(1)} %collective-permute-done.12.two, bf16[4,768,128]{2,1,0:T(8,128)(2,1)S(1)} %shard_map.50.rest_0_), custom_call_target="tpu_custom_call" | custom-call | flops 1207959552 | bytes 6291456 | tf_op jit(solution)/shard_map/pallas_call | solution.py:204
  56.3 6.9 %all-to-all-start = ((bf16[8,768,128]{2,1,0:T(8,128)(2,1)}), bf16[8,768,128]{2,1,0:T(8,128)(2,1)S(1)}, u32[]{:S(2)}, u32[]{:S(2)}) async-start(bf16[8,768,128]{2,1,0:T(8,128)(2,1)} %shard_map.51), calls=%async_computation | async-start | bytes 3145728 | tf_op jit(solution)/shard_map/all_to_all | solution.py:299
  64.3 18.4 %all-to-all-done.parts_ref = bf16[8,768,128]{2,1,0:T(8,128)(2,1)S(1)} async-done(((bf16[8,768,128]{2,1,0:T(8,128)(2,1)}), bf16[8,768,128]{2,1,0:T(8,128)(2,1)S(1)}, u32[]{:S(2)}, u32[]{:S(2)}) %all-to-all-start) | async-done | bytes 1572896 | tf_op jit(solution)/shard_map/all_to_all | solution.py:299
  82.7 2.3 %shard_map.52 = (f32[8,136,128]{2,1,0:T(8,128)S(1)}, bf16[256,768]{1,0:T(8,128)(2,1)S(1)}) custom-call(bf16[8,768,128]{2,1,0:T(8,128)(2,1)S(1)} %all-to-all-done.parts_ref, bf16[2,768,128]{2,1,0:T(8,128)(2,1)S(1)} %shard_map.48.refs_0_, bf16[2,768,128]{2,1,0:T(8,128)(2,1)S(1)} %collective-permute-done.5.refs_1_, ...), custom_call_target="tpu_custom_call" | custom-call | flops 402653184 | bytes 4194304 | tf_op jit(solution)/shard_map/pallas_call | solution.py:254
  85.1 2.4 %shard_map.53 = f32[8,136,128]{2,1,0:T(8,128)S(1)} custom-call(bf16[256,768]{1,0:T(8,128)(2,1)S(1)} %get-tuple-element.48.w_ref, bf16[2,768,128]{2,1,0:T(8,128)(2,1)} %collective-permute-done.15.refs_0_, bf16[2,768,128]{2,1,0:T(8,128)(2,1)} %collective-permute-done.16.refs_1_, bf16[768,128]{1,0:T(8,128)(2,1)S(1)} %collective-permute-done.17.refs_2_, ...), custom_call_target="tpu_custom_call" | custom-call | flops 402653184 | bytes 4194304 | tf_op jit(solution)/shard_map/pallas_call | solution.py:262
  87.7 24.5 %all_to_all.10 = f16[16,136,128]{2,1,0:T(8,128)(2,1)S(1)} all-to-all(f16[16,136,128]{2,1,0:T(8,128)(2,1)S(1)} %pad_maximum_fusion), channel_id=1, replica_groups={{0,32,192,224,128,160,64,96,16,48,208,240,144,176,80,112},{17,49,209,24..., dimensions={0} | all-to-all | bytes 1114112 | tf_op jit(solution)/shard_map/all_to_all | solution.py:301
  (45 shorter events, 8.2 us)
Async XLA Ops:
  2.8 17.4 %collective-permute-start = (bf16[768,128]{1,0:T(8,128)(2,1)}, bf16[768,128]{1,0:T(8,128)(2,1)S(1)}, u32[]{:S(2)}, u32[]{:S(2)}) collective-permute-start(bf16[768,128]{1,0:T(8,128)(2,1)} %get-tuple-element.27.one), channel_id=1, source_target_pairs={{0,0},{1,1},{2,2},{3,3},{4,224},{5,225},{6,226},{7,227},{8,192},{9... | collective-permute-start | bytes 589832 | tf_op jit(solution)/shard_map/ppermute | solution.py:31
  4.4 18.3 %collective-permute-start.1 = (bf16[768,128]{1,0:T(8,128)(2,1)}, bf16[768,128]{1,0:T(8,128)(2,1)S(1)}, u32[]{:S(2)}, u32[]{:S(2)}) collective-permute-start(bf16[768,128]{1,0:T(8,128)(2,1)} %get-tuple-element.27.one), channel_id=1, source_target_pairs={{0,128},{1,129},{2,130},{3,131},{4,96},{5,97},{6,98},{7,99},{8,64}... | collective-permute-start | bytes 589832 | tf_op jit(solution)/shard_map/ppermute | solution.py:31
  14.3 12.2 %collective-permute-start.4 = (bf16[768,128]{1,0:T(8,128)(2,1)}, bf16[768,128]{1,0:T(8,128)(2,1)S(1)}, u32[]{:S(2)}, u32[]{:S(2)}) collective-permute-start(bf16[768,128]{1,0:T(8,128)(2,1)} %get-tuple-element.27.one), channel_id=1, source_target_pairs={{0,2},{1,3},{2,0},{3,1},{4,6},{5,7},{6,4},{7,5},{8,10},{9,11},{10,... | collective-permute-start | bytes 589832 | tf_op jit(solution)/shard_map/ppermute | solution.py:31
  16.4 30.4 %collective-permute-start.8 = (bf16[768,768]{1,0:T(8,128)(2,1)}, bf16[768,768]{1,0:T(8,128)(2,1)S(1)}, u32[]{:S(2)}, u32[]{:S(2)}) collective-permute-start(bf16[768,768]{1,0:T(8,128)(2,1)} %get-tuple-element.33), channel_id=1, source_target_pairs={{0,0},{1,16},{2,2},{3,18},{4,4},{5,20},{6,6},{7,22},{8,8},{9,24},{... | collective-permute-start | bytes 3538952 | tf_op jit(solution)/shard_map/ppermute | solution.py:31
  18.3 29.0 %collective-permute-start.9 = (bf16[768,768]{1,0:T(8,128)(2,1)}, bf16[768,768]{1,0:T(8,128)(2,1)S(1)}, u32[]{:S(2)}, u32[]{:S(2)}) collective-permute-start(bf16[768,768]{1,0:T(8,128)(2,1)} %get-tuple-element.33), channel_id=1, source_target_pairs={{0,2},{1,18},{2,0},{3,16},{4,6},{5,22},{6,4},{7,20},{8,10},{9,26},... | collective-permute-start | bytes 3538952 | tf_op jit(solution)/shard_map/ppermute | solution.py:31
  22.7 12.0 %collective-permute-start.2 = (bf16[2,768,128]{2,1,0:T(8,128)(2,1)S(1)}, bf16[2,768,128]{2,1,0:T(8,128)(2,1)S(1)}, u32[]{:S(2)}, u32[]{:S(2)}) collective-permute-start(bf16[2,768,128]{2,1,0:T(8,128)(2,1)S(1)} %shard_map.47.own), channel_id=1, source_target_pairs={{0,32},{1,33},{2,34},{3,35},{4,36},{5,37},{6,38},{7,39},{8,40},{9,... | collective-permute-start | bytes 1179656 | tf_op jit(solution)/shard_map/ppermute | solution.py:31
  23.9 13.4 %collective-permute-start.3 = (bf16[2,768,128]{2,1,0:T(8,128)(2,1)S(1)}, bf16[2,768,128]{2,1,0:T(8,128)(2,1)S(1)}, u32[]{:S(2)}, u32[]{:S(2)}) collective-permute-start(bf16[2,768,128]{2,1,0:T(8,128)(2,1)S(1)} %shard_map.47.own), channel_id=1, source_target_pairs={{0,224},{1,225},{2,226},{3,227},{4,228},{5,229},{6,230},{7,231},{8... | collective-permute-start | bytes 1179656 | tf_op jit(solution)/shard_map/ppermute | solution.py:31
  26.5 0.9 copy-start.2
  27.4 11.4 %collective-permute-start.5 = (bf16[2,768,128]{2,1,0:T(8,128)(2,1)S(1)}, bf16[2,768,128]{2,1,0:T(8,128)(2,1)S(1)}, u32[]{:S(2)}, u32[]{:S(2)}) collective-permute-start(bf16[2,768,128]{2,1,0:T(8,128)(2,1)S(1)} %shard_map.48.refs_0_), channel_id=1, source_target_pairs={{0,4},{1,5},{2,6},{3,7},{4,8},{5,9},{6,10},{7,11},{8,12},{9,13},{1... | collective-permute-start | bytes 1179656 | tf_op jit(solution)/shard_map/ppermute | solution.py:31
  34.7 9.4 %collective-permute-start.10 = (bf16[2,768,128]{2,1,0:T(8,128)(2,1)S(1)}, bf16[2,768,128]{2,1,0:T(8,128)(2,1)S(1)}, u32[]{:S(2)}, u32[]{:S(2)}) collective-permute-start(bf16[2,768,128]{2,1,0:T(8,128)(2,1)S(1)} %shard_map.48.refs_0_), channel_id=1, source_target_pairs={{0,12},{1,13},{2,14},{3,15},{4,0},{5,1},{6,2},{7,3},{8,4},{9,5},{1... | collective-permute-start | bytes 1179656 | tf_op jit(solution)/shard_map/ppermute | solution.py:31
  38.9 7.0 %collective-permute-start.6 = (bf16[768,128]{1,0:T(8,128)(2,1)S(1)}, bf16[768,128]{1,0:T(8,128)(2,1)S(1)}, u32[]{:S(2)}, u32[]{:S(2)}) collective-permute-start(bf16[768,128]{1,0:T(8,128)(2,1)S(1)} %slice_bitcast_fusion.3), channel_id=1, source_target_pairs={{0,32},{1,33},{2,34},{3,35},{4,36},{5,37},{6,38},{7,39},{8,40},{9,... | collective-permute-start | bytes 589832 | tf_op jit(solution)/shard_map/ppermute | solution.py:31
  40.7 5.7 %collective-permute-start.7 = (bf16[768,128]{1,0:T(8,128)(2,1)S(1)}, bf16[768,128]{1,0:T(8,128)(2,1)S(1)}, u32[]{:S(2)}, u32[]{:S(2)}) collective-permute-start(bf16[768,128]{1,0:T(8,128)(2,1)S(1)} %slice_bitcast_fusion.2), channel_id=1, source_target_pairs={{0,224},{1,225},{2,226},{3,227},{4,228},{5,229},{6,230},{7,231},{8... | collective-permute-start | bytes 589832 | tf_op jit(solution)/shard_map/ppermute | solution.py:31
  44.1 8.1 %copy-start = (bf16[2,768,128]{2,1,0:T(8,128)(2,1)}, bf16[2,768,128]{2,1,0:T(8,128)(2,1)S(1)}, u32[]{:S(2)}) copy-start(bf16[2,768,128]{2,1,0:T(8,128)(2,1)S(1)} %collective-permute-done.10.refs_4_) | copy-start | bytes 1179652
  47.3 6.2 %collective-permute-start.11 = (bf16[768,768]{1,0:T(8,128)(2,1)S(1)}, bf16[768,768]{1,0:T(8,128)(2,1)S(1)}, u32[]{:S(2)}, u32[]{:S(2)}) collective-permute-start(bf16[768,768]{1,0:T(8,128)(2,1)S(1)} %collective-permute-done.8.one), channel_id=1, source_target_pairs={{0,1},{1,0},{2,3},{3,2},{4,5},{5,4},{6,7},{7,6},{8,9},{9,8},{10,11... | collective-permute-start | bytes 3538952 | tf_op jit(solution)/shard_map/ppermute | solution.py:31
  47.3 6.2 %collective-permute-start.12 = (bf16[768,768]{1,0:T(8,128)(2,1)S(1)}, bf16[768,768]{1,0:T(8,128)(2,1)S(1)}, u32[]{:S(2)}, u32[]{:S(2)}) collective-permute-start(bf16[768,768]{1,0:T(8,128)(2,1)S(1)} %collective-permute-done.9.two), channel_id=1, source_target_pairs={{0,1},{1,0},{2,3},{3,2},{4,5},{5,4},{6,7},{7,6},{8,9},{9,8},{10,11... | collective-permute-start | bytes 3538952 | tf_op jit(solution)/shard_map/ppermute | solution.py:31
  47.9 8.2 %collective-permute-start.13 = (bf16[768,128]{1,0:T(8,128)(2,1)S(1)}, bf16[768,128]{1,0:T(8,128)(2,1)}, u32[]{:S(2)}, u32[]{:S(2)}) collective-permute-start(bf16[768,128]{1,0:T(8,128)(2,1)S(1)} %slice_bitcast_fusion.1), channel_id=1, source_target_pairs={{0,4},{1,5},{2,6},{3,7},{4,8},{5,9},{6,10},{7,11},{8,12},{9,13},{1... | collective-permute-start | bytes 589832 | tf_op jit(solution)/shard_map/ppermute | solution.py:31
  49.6 6.7 %collective-permute-start.14 = (bf16[768,128]{1,0:T(8,128)(2,1)S(1)}, bf16[768,128]{1,0:T(8,128)(2,1)}, u32[]{:S(2)}, u32[]{:S(2)}) collective-permute-start(bf16[768,128]{1,0:T(8,128)(2,1)S(1)} %slice_bitcast_fusion), channel_id=1, source_target_pairs={{0,12},{1,13},{2,14},{3,15},{4,0},{5,1},{6,2},{7,3},{8,4},{9,5},{1... | collective-permute-start | bytes 589832 | tf_op jit(solution)/shard_map/ppermute | solution.py:31
  56.1 7.7 %copy-start.1 = (bf16[2,768,128]{2,1,0:T(8,128)(2,1)S(1)}, bf16[2,768,128]{2,1,0:T(8,128)(2,1)}, u32[]{:S(2)}) copy-start(bf16[2,768,128]{2,1,0:T(8,128)(2,1)} %copy-done) | copy-start | bytes 1179652
  56.3 26.3 %all-to-all-start = ((bf16[8,768,128]{2,1,0:T(8,128)(2,1)}), bf16[8,768,128]{2,1,0:T(8,128)(2,1)S(1)}, u32[]{:S(2)}, u32[]{:S(2)}) async-start(bf16[8,768,128]{2,1,0:T(8,128)(2,1)} %shard_map.51), calls=%async_computation | async-start | bytes 3145728 | tf_op jit(solution)/shard_map/all_to_all | solution.py:299
  63.3 21.8 %collective-permute-start.15 = (bf16[2,768,128]{2,1,0:T(8,128)(2,1)S(1)}, bf16[2,768,128]{2,1,0:T(8,128)(2,1)}, u32[]{:S(2)}, u32[]{:S(2)}) collective-permute-start(bf16[2,768,128]{2,1,0:T(8,128)(2,1)S(1)} %shard_map.48.refs_0_), channel_id=1, source_target_pairs={{0,1},{1,0},{2,3},{3,2},{4,5},{5,4},{6,7},{7,6},{8,9},{9,8},{10,11... | collective-permute-start | bytes 1179656 | tf_op jit(solution)/shard_map/ppermute | solution.py:31
  63.3 21.8 %collective-permute-start.16 = (bf16[2,768,128]{2,1,0:T(8,128)(2,1)S(1)}, bf16[2,768,128]{2,1,0:T(8,128)(2,1)}, u32[]{:S(2)}, u32[]{:S(2)}) collective-permute-start(bf16[2,768,128]{2,1,0:T(8,128)(2,1)S(1)} %collective-permute-done.5.refs_1_), channel_id=1, source_target_pairs={{0,1},{1,0},{2,3},{3,2},{4,5},{5,4},{6,7},{7,6},{8,9},{9,8},{10,11... | collective-permute-start | bytes 1179656 | tf_op jit(solution)/shard_map/ppermute | solution.py:31
  63.8 21.3 %collective-permute-start.19 = (bf16[2,768,128]{2,1,0:T(8,128)(2,1)S(1)}, bf16[2,768,128]{2,1,0:T(8,128)(2,1)}, u32[]{:S(2)}, u32[]{:S(2)}) collective-permute-start(bf16[2,768,128]{2,1,0:T(8,128)(2,1)S(1)} %copy-done.1), channel_id=1, source_target_pairs={{0,1},{1,0},{2,3},{3,2},{4,5},{5,4},{6,7},{7,6},{8,9},{9,8},{10,11... | collective-permute-start | bytes 1179656 | tf_op jit(solution)/shard_map/ppermute | solution.py:31
  63.8 21.3 %collective-permute-start.17 = (bf16[768,128]{1,0:T(8,128)(2,1)}, bf16[768,128]{1,0:T(8,128)(2,1)S(1)}, u32[]{:S(2)}, u32[]{:S(2)}) collective-permute-start(bf16[768,128]{1,0:T(8,128)(2,1)} %collective-permute-done.13.refs_2_), channel_id=1, source_target_pairs={{0,1},{1,0},{2,3},{3,2},{4,5},{5,4},{6,7},{7,6},{8,9},{9,8},{10,11... | collective-permute-start | bytes 589832 | tf_op jit(solution)/shard_map/ppermute | solution.py:31
  64.3 20.8 %collective-permute-start.18 = (bf16[768,128]{1,0:T(8,128)(2,1)}, bf16[768,128]{1,0:T(8,128)(2,1)}, u32[]{:S(2)}, u32[]{:S(2)}) collective-permute-start(bf16[768,128]{1,0:T(8,128)(2,1)} %collective-permute-done.14.refs_3_), channel_id=1, source_target_pairs={{0,1},{1,0},{2,3},{3,2},{4,5},{5,4},{6,7},{7,6},{8,9},{9,8},{10,11... | collective-permute-start | bytes 589832 | tf_op jit(solution)/shard_map/ppermute | solution.py:31

commit v9 on v8

--- a/solution.py
+++ b/solution.py
@@ -280,17 +280,17 @@
     p_eff, a_eff = masked(prolong, a_matrix, p_pattern, a_pattern)
     first, second = send(p_eff, turn), send(p_eff, turn_far)
     across = send(p_eff, far_x)
-    near, distant = send(a_eff, swap), send(a_eff, swap_far)
+    distant, near = send(a_eff, swap_far), send(a_eff, swap)
     pair = paired(p_eff, across)
     first, second, spot = both(first, second, spot)
     own = paired(first, second)
     below, above, pair_1 = both(send(own, z_up), send(own, z_down), send(pair, y_up))
     pair_3 = send(pair, y_down)
     up_two, down_two = send(below[0], z_up), send(above[0], z_down)
-    up_two, down_two, near, distant, pair_3, pair_1 = both(up_two, down_two, near, distant, pair_3, pair_1)
+    up_two, down_two, distant, near, pair_3, pair_1 = both(up_two, down_two, distant, near, pair_3, pair_1)
     beyond = send(pair_1[0], y_up), send(pair_3[1], y_down)
     p_all = line_up(spot, own, above, below, up_two, down_two)
-    near_2, distant_2 = send(near, other_core), send(distant, other_core)
+    distant_2, near_2 = send(distant, other_core), send(near, other_core)
     w_part = w_products(p_all, near, distant)
     w_part = w_products(p_all, near_2, distant_2, w_part)
     w_part, pair, pair_1, pair_3, *beyond = both(w_part, pair, pair_1, pair_3, *beyond)

time: 114 us -> 112 us (0.982)
  waiting for transfers between devices: 34.7 us -> 33.2 us
    all_to_all x1, starting transfers between devices: 6.91 us -> 5.52 us  [local(): lax.all_to_all(w_part, AXES, 0, 0, axis_index_groups=W_GROUPS, tiled=True)]
  transfers between devices with their start and end apart: 21 -> 21, of which waited for: 10 -> 9; matrix products, arithmetic and copies ran while one was open for 0% -> 0% of each run, Pallas kernels for 6% -> 6%
where the time goes in v9:
time: 112 us; the launch traced here: 111 us
  starting transfers between devices  38.3 us (34%)
  waiting for transfers between devices  33.2 us (30%)
  blocking collectives  24.7 us (22%)
  Pallas kernels  12.3 us (11%)
  local copies, waits for them, and re-layouts  1.72 us (2%)
    ppermute x20, starting transfers between devices, send(): return lax.ppermute(value, AXES, pairs)  32.8 us
    all_to_all x1, blocking collectives, local(): lax.all_to_all(c_part, AXES, 0, 0, axis_index_groups=C_GROUPS, tiled=True)  24.7 us
    all_to_all x1, waiting for transfers between devices, local(): lax.all_to_all(w_part, AXES, 0, 0, axis_index_groups=W_GROUPS, tiled=True)  17.4 us
    ppermute x20, waiting for transfers between devices, send(): return lax.ppermute(value, AXES, pairs)  15.8 us
    all_to_all x1, starting transfers between devices, local(): lax.all_to_all(w_part, AXES, 0, 0, axis_index_groups=W_GROUPS, tiled=True)  5.52 us
    pallas_call x2, Pallas kernels, w_products(): on_device(functools.partial(w_kernel, LANES * len(before)), (LANES * (1 +...  3.93 us
    pallas_call x1, Pallas kernels, masked(): pl.pallas_call(mask_kernel, out_shape=[jax.ShapeDtypeStruct(v.shape, v.dt...  2.79 us
    pallas_call x1, Pallas kernels, c_products(): on_device(other_kernel, chunks.shape, chunks.dtype, [VMEM] * (len(passed)...  2.39 us
  transfers between devices with their start and end apart: 21, of which 9 were waited for; matrix products, arithmetic and copies ran while one was open for 0% of the time, Pallas kernels for 6%

profile of v9, /device:TPU:2, one launch (start us, length us, event | category | flops | bytes accessed | tf_op | source)
XLA Modules:
  0.0 111.3 jit_solution(5782150041475089846)
XLA Ops:
  0.0 2.8 %shard_map.46 = (bf16[768,128]{1,0:T(8,128)(2,1)}, bf16[768,768]{1,0:T(8,128)(2,1)}) custom-call(bf16[768,128]{1,0:T(8,128)(2,1)} %p_any.1, bf16[768,768]{1,0:T(8,128)(2,1)} %a_any.1, s32[1,6]{1,0:T(1,128)} %bitcast.14, s32[6,6]{1,0:T(8,128)} %a_pattern.1), custom_call_target="tpu_custom_call" | custom-call | flops 589824 | bytes 4194304 | tf_op jit(solution)/shard_map/pallas_call | solution.py:141
  2.8 1.6 %collective-permute-start = (bf16[768,128]{1,0:T(8,128)(2,1)}, bf16[768,128]{1,0:T(8,128)(2,1)S(1)}, u32[]{:S(2)}, u32[]{:S(2)}) collective-permute-start(bf16[768,128]{1,0:T(8,128)(2,1)} %get-tuple-element.27.one), channel_id=1, source_target_pairs={{0,0},{1,1},{2,2},{3,3},{4,224},{5,225},{6,226},{7,227},{8,192},{9... | collective-permute-start | bytes 589832 | tf_op jit(solution)/shard_map/ppermute | solution.py:31
  4.4 9.9 %collective-permute-start.1 = (bf16[768,128]{1,0:T(8,128)(2,1)}, bf16[768,128]{1,0:T(8,128)(2,1)S(1)}, u32[]{:S(2)}, u32[]{:S(2)}) collective-permute-start(bf16[768,128]{1,0:T(8,128)(2,1)} %get-tuple-element.27.one), channel_id=1, source_target_pairs={{0,128},{1,129},{2,130},{3,131},{4,96},{5,97},{6,98},{7,99},{8,64}... | collective-permute-start | bytes 589832 | tf_op jit(solution)/shard_map/ppermute | solution.py:31
  14.3 2.1 %collective-permute-start.4 = (bf16[768,128]{1,0:T(8,128)(2,1)}, bf16[768,128]{1,0:T(8,128)(2,1)S(1)}, u32[]{:S(2)}, u32[]{:S(2)}) collective-permute-start(bf16[768,128]{1,0:T(8,128)(2,1)} %get-tuple-element.27.one), channel_id=1, source_target_pairs={{0,2},{1,3},{2,0},{3,1},{4,6},{5,7},{6,4},{7,5},{8,10},{9,11},{10,... | collective-permute-start | bytes 589832 | tf_op jit(solution)/shard_map/ppermute | solution.py:31
  16.4 4.2 %collective-permute-start.9 = (bf16[768,768]{1,0:T(8,128)(2,1)}, bf16[768,768]{1,0:T(8,128)(2,1)S(1)}, u32[]{:S(2)}, u32[]{:S(2)}) collective-permute-start(bf16[768,768]{1,0:T(8,128)(2,1)} %get-tuple-element.33), channel_id=1, source_target_pairs={{0,0},{1,16},{2,2},{3,18},{4,4},{5,20},{6,6},{7,22},{8,8},{9,24},{... | collective-permute-start | bytes 3538952 | tf_op jit(solution)/shard_map/ppermute | solution.py:31
  20.7 2.0 %collective-permute-done.1.two = bf16[768,128]{1,0:T(8,128)(2,1)S(1)} collective-permute-done((bf16[768,128]{1,0:T(8,128)(2,1)}, bf16[768,128]{1,0:T(8,128)(2,1)S(1)}, u32[]{:S(2)}, u32[]{:S(2)}) %collective-permute-start.1) | collective-permute-done | bytes 196640 | tf_op jit(solution)/shard_map/ppermute | solution.py:31
  22.7 1.2 %collective-permute-start.2 = (bf16[2,768,128]{2,1,0:T(8,128)(2,1)S(1)}, bf16[2,768,128]{2,1,0:T(8,128)(2,1)S(1)}, u32[]{:S(2)}, u32[]{:S(2)}) collective-permute-start(bf16[2,768,128]{2,1,0:T(8,128)(2,1)S(1)} %shard_map.47.own), channel_id=1, source_target_pairs={{0,32},{1,33},{2,34},{3,35},{4,36},{5,37},{6,38},{7,39},{8,40},{9,... | collective-permute-start | bytes 1179656 | tf_op jit(solution)/shard_map/ppermute | solution.py:31
  23.9 2.5 %collective-permute-start.3 = (bf16[2,768,128]{2,1,0:T(8,128)(2,1)S(1)}, bf16[2,768,128]{2,1,0:T(8,128)(2,1)S(1)}, u32[]{:S(2)}, u32[]{:S(2)}) collective-permute-start(bf16[2,768,128]{2,1,0:T(8,128)(2,1)S(1)} %shard_map.47.own), channel_id=1, source_target_pairs={{0,224},{1,225},{2,226},{3,227},{4,228},{5,229},{6,230},{7,231},{8... | collective-permute-start | bytes 1179656 | tf_op jit(solution)/shard_map/ppermute | solution.py:31
  27.7 7.0 %collective-permute-done.2.below = bf16[2,768,128]{2,1,0:T(8,128)(2,1)S(1)} collective-permute-done((bf16[2,768,128]{2,1,0:T(8,128)(2,1)S(1)}, bf16[2,768,128]{2,1,0:T(8,128)(2,1)S(1)}, u32[]{:S(2)}, u32[]{:S(2)}) %collective-permute-start.2) | collective-permute-done | bytes 393248 | tf_op jit(solution)/shard_map/ppermute | solution.py:31
  34.7 2.7 %collective-permute-start.10 = (bf16[2,768,128]{2,1,0:T(8,128)(2,1)S(1)}, bf16[2,768,128]{2,1,0:T(8,128)(2,1)S(1)}, u32[]{:S(2)}, u32[]{:S(2)}) collective-permute-start(bf16[2,768,128]{2,1,0:T(8,128)(2,1)S(1)} %shard_map.48.refs_0_), channel_id=1, source_target_pairs={{0,12},{1,13},{2,14},{3,15},{4,0},{5,1},{6,2},{7,3},{8,4},{9,5},{1... | collective-permute-start | bytes 1179656 | tf_op jit(solution)/shard_map/ppermute | solution.py:31
  37.4 1.5 %collective-permute-done.5.refs_1_ = bf16[2,768,128]{2,1,0:T(8,128)(2,1)S(1)} collective-permute-done((bf16[2,768,128]{2,1,0:T(8,128)(2,1)S(1)}, bf16[2,768,128]{2,1,0:T(8,128)(2,1)S(1)}, u32[]{:S(2)}, u32[]{:S(2)}) %collective-permute-start.5) | collective-permute-done | bytes 393248 | tf_op jit(solution)/shard_map/ppermute | solution.py:31
  38.9 1.8 %collective-permute-start.6 = (bf16[768,128]{1,0:T(8,128)(2,1)S(1)}, bf16[768,128]{1,0:T(8,128)(2,1)S(1)}, u32[]{:S(2)}, u32[]{:S(2)}) collective-permute-start(bf16[768,128]{1,0:T(8,128)(2,1)S(1)} %slice_bitcast_fusion.3), channel_id=1, source_target_pairs={{0,32},{1,33},{2,34},{3,35},{4,36},{5,37},{6,38},{7,39},{8,40},{9,... | collective-permute-start | bytes 589832 | tf_op jit(solution)/shard_map/ppermute | solution.py:31
  40.7 1.6 %collective-permute-start.7 = (bf16[768,128]{1,0:T(8,128)(2,1)S(1)}, bf16[768,128]{1,0:T(8,128)(2,1)S(1)}, u32[]{:S(2)}, u32[]{:S(2)}) collective-permute-start(bf16[768,128]{1,0:T(8,128)(2,1)S(1)} %slice_bitcast_fusion.2), channel_id=1, source_target_pairs={{0,224},{1,225},{2,226},{3,227},{4,228},{5,229},{6,230},{7,231},{8... | collective-permute-start | bytes 589832 | tf_op jit(solution)/shard_map/ppermute | solution.py:31
  42.3 1.8 %collective-permute-done.10.refs_4_ = bf16[2,768,128]{2,1,0:T(8,128)(2,1)S(1)} collective-permute-done((bf16[2,768,128]{2,1,0:T(8,128)(2,1)S(1)}, bf16[2,768,128]{2,1,0:T(8,128)(2,1)S(1)}, u32[]{:S(2)}, u32[]{:S(2)}) %collective-permute-start.10) | collective-permute-done | bytes 393248 | tf_op jit(solution)/shard_map/ppermute | solution.py:31
  44.1 1.8 %collective-permute-done.6.up_two = bf16[768,128]{1,0:T(8,128)(2,1)S(1)} collective-permute-done((bf16[768,128]{1,0:T(8,128)(2,1)S(1)}, bf16[768,128]{1,0:T(8,128)(2,1)S(1)}, u32[]{:S(2)}, u32[]{:S(2)}) %collective-permute-start.6) | collective-permute-done | bytes 196640 | tf_op jit(solution)/shard_map/ppermute | solution.py:31
  47.9 1.7 %collective-permute-start.13 = (bf16[768,128]{1,0:T(8,128)(2,1)S(1)}, bf16[768,128]{1,0:T(8,128)(2,1)}, u32[]{:S(2)}, u32[]{:S(2)}) collective-permute-start(bf16[768,128]{1,0:T(8,128)(2,1)S(1)} %slice_bitcast_fusion.1), channel_id=1, source_target_pairs={{0,4},{1,5},{2,6},{3,7},{4,8},{5,9},{6,10},{7,11},{8,12},{9,13},{1... | collective-permute-start | bytes 589832 | tf_op jit(solution)/shard_map/ppermute | solution.py:31
  49.7 1.6 %collective-permute-start.14 = (bf16[768,128]{1,0:T(8,128)(2,1)S(1)}, bf16[768,128]{1,0:T(8,128)(2,1)}, u32[]{:S(2)}, u32[]{:S(2)}) collective-permute-start(bf16[768,128]{1,0:T(8,128)(2,1)S(1)} %slice_bitcast_fusion), channel_id=1, source_target_pairs={{0,12},{1,13},{2,14},{3,15},{4,0},{5,1},{6,2},{7,3},{8,4},{9,5},{1... | collective-permute-start | bytes 589832 | tf_op jit(solution)/shard_map/ppermute | solution.py:31
  52.2 1.4 %shard_map.50.rest_0_ = bf16[4,768,128]{2,1,0:T(8,128)(2,1)S(1)} custom-call(bf16[2,768,512]{2,1,0:T(8,128)(2,1)S(1)} %shard_map.49.p_ref, bf16[768,768]{1,0:T(8,128)(2,1)S(1)} %collective-permute-done.9.one, bf16[768,768]{1,0:T(8,128)(2,1)S(1)} %collective-permute-done.8.two), custom_call_target="tpu_custom_call" | custom-call | flops 1207959552 | bytes 6291456 | tf_op jit(solution)/shard_map/pallas_call | solution.py:204
  53.6 2.6 %shard_map.51 = bf16[8,768,128]{2,1,0:T(8,128)(2,1)} custom-call(bf16[2,768,512]{2,1,0:T(8,128)(2,1)S(1)} %shard_map.49.p_ref, bf16[768,768]{1,0:T(8,128)(2,1)S(1)} %collective-permute-done.11.one, bf16[768,768]{1,0:T(8,128)(2,1)S(1)} %collective-permute-done.12.two, bf16[4,768,128]{2,1,0:T(8,128)(2,1)S(1)} %shard_map.50.rest_0_), custom_call_target="tpu_custom_call" | custom-call | flops 1207959552 | bytes 6291456 | tf_op jit(solution)/shard_map/pallas_call | solution.py:204
  56.4 5.5 %all-to-all-start = ((bf16[8,768,128]{2,1,0:T(8,128)(2,1)}), bf16[8,768,128]{2,1,0:T(8,128)(2,1)S(1)}, u32[]{:S(2)}, u32[]{:S(2)}) async-start(bf16[8,768,128]{2,1,0:T(8,128)(2,1)} %shard_map.51), calls=%async_computation | async-start | bytes 3145728 | tf_op jit(solution)/shard_map/all_to_all | solution.py:299
  62.9 17.4 %all-to-all-done.parts_ref = bf16[8,768,128]{2,1,0:T(8,128)(2,1)S(1)} async-done(((bf16[8,768,128]{2,1,0:T(8,128)(2,1)}), bf16[8,768,128]{2,1,0:T(8,128)(2,1)S(1)}, u32[]{:S(2)}, u32[]{:S(2)}) %all-to-all-start) | async-done | bytes 1572896 | tf_op jit(solution)/shard_map/all_to_all | solution.py:299
  80.3 2.3 %shard_map.52 = (f32[8,136,128]{2,1,0:T(8,128)S(1)}, bf16[256,768]{1,0:T(8,128)(2,1)S(1)}) custom-call(bf16[8,768,128]{2,1,0:T(8,128)(2,1)S(1)} %all-to-all-done.parts_ref, bf16[2,768,128]{2,1,0:T(8,128)(2,1)S(1)} %shard_map.48.refs_0_, bf16[2,768,128]{2,1,0:T(8,128)(2,1)S(1)} %collective-permute-done.5.refs_1_, ...), custom_call_target="tpu_custom_call" | custom-call | flops 402653184 | bytes 4194304 | tf_op jit(solution)/shard_map/pallas_call | solution.py:254
  82.7 2.4 %shard_map.53 = f32[8,136,128]{2,1,0:T(8,128)S(1)} custom-call(bf16[256,768]{1,0:T(8,128)(2,1)S(1)} %get-tuple-element.48.w_ref, bf16[2,768,128]{2,1,0:T(8,128)(2,1)} %collective-permute-done.15.refs_0_, bf16[2,768,128]{2,1,0:T(8,128)(2,1)} %collective-permute-done.16.refs_1_, bf16[768,128]{1,0:T(8,128)(2,1)S(1)} %collective-permute-done.17.refs_2_, ...), custom_call_target="tpu_custom_call" | custom-call | flops 402653184 | bytes 4194304 | tf_op jit(solution)/shard_map/pallas_call | solution.py:262
  85.4 24.7 %all_to_all.10 = f16[16,136,128]{2,1,0:T(8,128)(2,1)S(1)} all-to-all(f16[16,136,128]{2,1,0:T(8,128)(2,1)S(1)} %pad_maximum_fusion), channel_id=1, replica_groups={{0,32,192,224,128,160,64,96,16,48,208,240,144,176,80,112},{17,49,209,24..., dimensions={0} | all-to-all | bytes 1114112 | tf_op jit(solution)/shard_map/all_to_all | solution.py:301
  (45 shorter events, 7.0 us)
Async XLA Ops:
  2.8 17.9 %collective-permute-start = (bf16[768,128]{1,0:T(8,128)(2,1)}, bf16[768,128]{1,0:T(8,128)(2,1)S(1)}, u32[]{:S(2)}, u32[]{:S(2)}) collective-permute-start(bf16[768,128]{1,0:T(8,128)(2,1)} %get-tuple-element.27.one), channel_id=1, source_target_pairs={{0,0},{1,1},{2,2},{3,3},{4,224},{5,225},{6,226},{7,227},{8,192},{9... | collective-permute-start | bytes 589832 | tf_op jit(solution)/shard_map/ppermute | solution.py:31
  4.4 18.3 %collective-permute-start.1 = (bf16[768,128]{1,0:T(8,128)(2,1)}, bf16[768,128]{1,0:T(8,128)(2,1)S(1)}, u32[]{:S(2)}, u32[]{:S(2)}) collective-permute-start(bf16[768,128]{1,0:T(8,128)(2,1)} %get-tuple-element.27.one), channel_id=1, source_target_pairs={{0,128},{1,129},{2,130},{3,131},{4,96},{5,97},{6,98},{7,99},{8,64}... | collective-permute-start | bytes 589832 | tf_op jit(solution)/shard_map/ppermute | solution.py:31
  14.3 12.2 %collective-permute-start.4 = (bf16[768,128]{1,0:T(8,128)(2,1)}, bf16[768,128]{1,0:T(8,128)(2,1)S(1)}, u32[]{:S(2)}, u32[]{:S(2)}) collective-permute-start(bf16[768,128]{1,0:T(8,128)(2,1)} %get-tuple-element.27.one), channel_id=1, source_target_pairs={{0,2},{1,3},{2,0},{3,1},{4,6},{5,7},{6,4},{7,5},{8,10},{9,11},{10,... | collective-permute-start | bytes 589832 | tf_op jit(solution)/shard_map/ppermute | solution.py:31
  16.4 31.0 %collective-permute-start.8 = (bf16[768,768]{1,0:T(8,128)(2,1)}, bf16[768,768]{1,0:T(8,128)(2,1)S(1)}, u32[]{:S(2)}, u32[]{:S(2)}) collective-permute-start(bf16[768,768]{1,0:T(8,128)(2,1)} %get-tuple-element.33), channel_id=1, source_target_pairs={{0,2},{1,18},{2,0},{3,16},{4,6},{5,22},{6,4},{7,20},{8,10},{9,26},... | collective-permute-start | bytes 3538952 | tf_op jit(solution)/shard_map/ppermute | solution.py:31
  16.4 31.0 %collective-permute-start.9 = (bf16[768,768]{1,0:T(8,128)(2,1)}, bf16[768,768]{1,0:T(8,128)(2,1)S(1)}, u32[]{:S(2)}, u32[]{:S(2)}) collective-permute-start(bf16[768,768]{1,0:T(8,128)(2,1)} %get-tuple-element.33), channel_id=1, source_target_pairs={{0,0},{1,16},{2,2},{3,18},{4,4},{5,20},{6,6},{7,22},{8,8},{9,24},{... | collective-permute-start | bytes 3538952 | tf_op jit(solution)/shard_map/ppermute | solution.py:31
  22.7 12.0 %collective-permute-start.2 = (bf16[2,768,128]{2,1,0:T(8,128)(2,1)S(1)}, bf16[2,768,128]{2,1,0:T(8,128)(2,1)S(1)}, u32[]{:S(2)}, u32[]{:S(2)}) collective-permute-start(bf16[2,768,128]{2,1,0:T(8,128)(2,1)S(1)} %shard_map.47.own), channel_id=1, source_target_pairs={{0,32},{1,33},{2,34},{3,35},{4,36},{5,37},{6,38},{7,39},{8,40},{9,... | collective-permute-start | bytes 1179656 | tf_op jit(solution)/shard_map/ppermute | solution.py:31
  23.9 13.4 %collective-permute-start.3 = (bf16[2,768,128]{2,1,0:T(8,128)(2,1)S(1)}, bf16[2,768,128]{2,1,0:T(8,128)(2,1)S(1)}, u32[]{:S(2)}, u32[]{:S(2)}) collective-permute-start(bf16[2,768,128]{2,1,0:T(8,128)(2,1)S(1)} %shard_map.47.own), channel_id=1, source_target_pairs={{0,224},{1,225},{2,226},{3,227},{4,228},{5,229},{6,230},{7,231},{8... | collective-permute-start | bytes 1179656 | tf_op jit(solution)/shard_map/ppermute | solution.py:31
  26.5 0.9 copy-start.2
  27.4 11.4 %collective-permute-start.5 = (bf16[2,768,128]{2,1,0:T(8,128)(2,1)S(1)}, bf16[2,768,128]{2,1,0:T(8,128)(2,1)S(1)}, u32[]{:S(2)}, u32[]{:S(2)}) collective-permute-start(bf16[2,768,128]{2,1,0:T(8,128)(2,1)S(1)} %shard_map.48.refs_0_), channel_id=1, source_target_pairs={{0,4},{1,5},{2,6},{3,7},{4,8},{5,9},{6,10},{7,11},{8,12},{9,13},{1... | collective-permute-start | bytes 1179656 | tf_op jit(solution)/shard_map/ppermute | solution.py:31
  34.7 9.4 %collective-permute-start.10 = (bf16[2,768,128]{2,1,0:T(8,128)(2,1)S(1)}, bf16[2,768,128]{2,1,0:T(8,128)(2,1)S(1)}, u32[]{:S(2)}, u32[]{:S(2)}) collective-permute-start(bf16[2,768,128]{2,1,0:T(8,128)(2,1)S(1)} %shard_map.48.refs_0_), channel_id=1, source_target_pairs={{0,12},{1,13},{2,14},{3,15},{4,0},{5,1},{6,2},{7,3},{8,4},{9,5},{1... | collective-permute-start | bytes 1179656 | tf_op jit(solution)/shard_map/ppermute | solution.py:31
  38.9 7.0 %collective-permute-start.6 = (bf16[768,128]{1,0:T(8,128)(2,1)S(1)}, bf16[768,128]{1,0:T(8,128)(2,1)S(1)}, u32[]{:S(2)}, u32[]{:S(2)}) collective-permute-start(bf16[768,128]{1,0:T(8,128)(2,1)S(1)} %slice_bitcast_fusion.3), channel_id=1, source_target_pairs={{0,32},{1,33},{2,34},{3,35},{4,36},{5,37},{6,38},{7,39},{8,40},{9,... | collective-permute-start | bytes 589832 | tf_op jit(solution)/shard_map/ppermute | solution.py:31
  40.7 5.7 %collective-permute-start.7 = (bf16[768,128]{1,0:T(8,128)(2,1)S(1)}, bf16[768,128]{1,0:T(8,128)(2,1)S(1)}, u32[]{:S(2)}, u32[]{:S(2)}) collective-permute-start(bf16[768,128]{1,0:T(8,128)(2,1)S(1)} %slice_bitcast_fusion.2), channel_id=1, source_target_pairs={{0,224},{1,225},{2,226},{3,227},{4,228},{5,229},{6,230},{7,231},{8... | collective-permute-start | bytes 589832 | tf_op jit(solution)/shard_map/ppermute | solution.py:31
  44.1 8.1 %copy-start = (bf16[2,768,128]{2,1,0:T(8,128)(2,1)}, bf16[2,768,128]{2,1,0:T(8,128)(2,1)S(1)}, u32[]{:S(2)}) copy-start(bf16[2,768,128]{2,1,0:T(8,128)(2,1)S(1)} %collective-permute-done.10.refs_4_) | copy-start | bytes 1179652
  47.4 6.2 %collective-permute-start.11 = (bf16[768,768]{1,0:T(8,128)(2,1)S(1)}, bf16[768,768]{1,0:T(8,128)(2,1)S(1)}, u32[]{:S(2)}, u32[]{:S(2)}) collective-permute-start(bf16[768,768]{1,0:T(8,128)(2,1)S(1)} %collective-permute-done.9.one), channel_id=1, source_target_pairs={{0,1},{1,0},{2,3},{3,2},{4,5},{5,4},{6,7},{7,6},{8,9},{9,8},{10,11... | collective-permute-start | bytes 3538952 | tf_op jit(solution)/shard_map/ppermute | solution.py:31
  47.4 6.2 %collective-permute-start.12 = (bf16[768,768]{1,0:T(8,128)(2,1)S(1)}, bf16[768,768]{1,0:T(8,128)(2,1)S(1)}, u32[]{:S(2)}, u32[]{:S(2)}) collective-permute-start(bf16[768,768]{1,0:T(8,128)(2,1)S(1)} %collective-permute-done.8.two), channel_id=1, source_target_pairs={{0,1},{1,0},{2,3},{3,2},{4,5},{5,4},{6,7},{7,6},{8,9},{9,8},{10,11... | collective-permute-start | bytes 3538952 | tf_op jit(solution)/shard_map/ppermute | solution.py:31
  47.9 8.2 %collective-permute-start.13 = (bf16[768,128]{1,0:T(8,128)(2,1)S(1)}, bf16[768,128]{1,0:T(8,128)(2,1)}, u32[]{:S(2)}, u32[]{:S(2)}) collective-permute-start(bf16[768,128]{1,0:T(8,128)(2,1)S(1)} %slice_bitcast_fusion.1), channel_id=1, source_target_pairs={{0,4},{1,5},{2,6},{3,7},{4,8},{5,9},{6,10},{7,11},{8,12},{9,13},{1... | collective-permute-start | bytes 589832 | tf_op jit(solution)/shard_map/ppermute | solution.py:31
  49.7 6.7 %collective-permute-start.14 = (bf16[768,128]{1,0:T(8,128)(2,1)S(1)}, bf16[768,128]{1,0:T(8,128)(2,1)}, u32[]{:S(2)}, u32[]{:S(2)}) collective-permute-start(bf16[768,128]{1,0:T(8,128)(2,1)S(1)} %slice_bitcast_fusion), channel_id=1, source_target_pairs={{0,12},{1,13},{2,14},{3,15},{4,0},{5,1},{6,2},{7,3},{8,4},{9,5},{1... | collective-permute-start | bytes 589832 | tf_op jit(solution)/shard_map/ppermute | solution.py:31
  56.1 6.3 %copy-start.1 = (bf16[2,768,128]{2,1,0:T(8,128)(2,1)S(1)}, bf16[2,768,128]{2,1,0:T(8,128)(2,1)}, u32[]{:S(2)}) copy-start(bf16[2,768,128]{2,1,0:T(8,128)(2,1)} %copy-done) | copy-start | bytes 1179652
  56.4 23.9 %all-to-all-start = ((bf16[8,768,128]{2,1,0:T(8,128)(2,1)}), bf16[8,768,128]{2,1,0:T(8,128)(2,1)S(1)}, u32[]{:S(2)}, u32[]{:S(2)}) async-start(bf16[8,768,128]{2,1,0:T(8,128)(2,1)} %shard_map.51), calls=%async_computation | async-start | bytes 3145728 | tf_op jit(solution)/shard_map/all_to_all | solution.py:299
  61.9 20.8 %collective-permute-start.15 = (bf16[2,768,128]{2,1,0:T(8,128)(2,1)S(1)}, bf16[2,768,128]{2,1,0:T(8,128)(2,1)}, u32[]{:S(2)}, u32[]{:S(2)}) collective-permute-start(bf16[2,768,128]{2,1,0:T(8,128)(2,1)S(1)} %shard_map.48.refs_0_), channel_id=1, source_target_pairs={{0,1},{1,0},{2,3},{3,2},{4,5},{5,4},{6,7},{7,6},{8,9},{9,8},{10,11... | collective-permute-start | bytes 1179656 | tf_op jit(solution)/shard_map/ppermute | solution.py:31
  61.9 20.8 %collective-permute-start.16 = (bf16[2,768,128]{2,1,0:T(8,128)(2,1)S(1)}, bf16[2,768,128]{2,1,0:T(8,128)(2,1)}, u32[]{:S(2)}, u32[]{:S(2)}) collective-permute-start(bf16[2,768,128]{2,1,0:T(8,128)(2,1)S(1)} %collective-permute-done.5.refs_1_), channel_id=1, source_target_pairs={{0,1},{1,0},{2,3},{3,2},{4,5},{5,4},{6,7},{7,6},{8,9},{9,8},{10,11... | collective-permute-start | bytes 1179656 | tf_op jit(solution)/shard_map/ppermute | solution.py:31
  62.4 20.3 %collective-permute-start.19 = (bf16[2,768,128]{2,1,0:T(8,128)(2,1)S(1)}, bf16[2,768,128]{2,1,0:T(8,128)(2,1)}, u32[]{:S(2)}, u32[]{:S(2)}) collective-permute-start(bf16[2,768,128]{2,1,0:T(8,128)(2,1)S(1)} %copy-done.1), channel_id=1, source_target_pairs={{0,1},{1,0},{2,3},{3,2},{4,5},{5,4},{6,7},{7,6},{8,9},{9,8},{10,11... | collective-permute-start | bytes 1179656 | tf_op jit(solution)/shard_map/ppermute | solution.py:31
  62.4 20.2 %collective-permute-start.17 = (bf16[768,128]{1,0:T(8,128)(2,1)}, bf16[768,128]{1,0:T(8,128)(2,1)S(1)}, u32[]{:S(2)}, u32[]{:S(2)}) collective-permute-start(bf16[768,128]{1,0:T(8,128)(2,1)} %collective-permute-done.13.refs_2_), channel_id=1, source_target_pairs={{0,1},{1,0},{2,3},{3,2},{4,5},{5,4},{6,7},{7,6},{8,9},{9,8},{10,11... | collective-permute-start | bytes 589832 | tf_op jit(solution)/shard_map/ppermute | solution.py:31
  62.9 19.8 %collective-permute-start.18 = (bf16[768,128]{1,0:T(8,128)(2,1)}, bf16[768,128]{1,0:T(8,128)(2,1)}, u32[]{:S(2)}, u32[]{:S(2)}) collective-permute-start(bf16[768,128]{1,0:T(8,128)(2,1)} %collective-permute-done.14.refs_3_), channel_id=1, source_target_pairs={{0,1},{1,0},{2,3},{3,2},{4,5},{5,4},{6,7},{7,6},{8,9},{9,8},{10,11... | collective-permute-start | bytes 589832 | tf_op jit(solution)/shard_map/ppermute | solution.py:31

commit v10 on v9

--- a/solution.py
+++ b/solution.py
@@ -278,11 +278,11 @@
     row, col = lax.axis_index("row"), lax.axis_index("col")
     spot = jnp.stack([row // 2, col // 4, (col // 2) % 2]).astype(jnp.int32)
     p_eff, a_eff = masked(prolong, a_matrix, p_pattern, a_pattern)
-    first, second = send(p_eff, turn), send(p_eff, turn_far)
+    second, first = send(p_eff, turn_far), send(p_eff, turn)
     across = send(p_eff, far_x)
     distant, near = send(a_eff, swap_far), send(a_eff, swap)
     pair = paired(p_eff, across)
-    first, second, spot = both(first, second, spot)
+    second, first, spot = both(second, first, spot)
     own = paired(first, second)
     below, above, pair_1 = both(send(own, z_up), send(own, z_down), send(pair, y_up))
     pair_3 = send(pair, y_down)

time: 112 us -> 113 us (level)
  transfers between devices with their start and end apart: 21 -> 21, of which waited for: 9 -> 8; matrix products, arithmetic and copies ran while one was open for 0% -> 0% of each run, Pallas kernels for 6% -> 6%
where the time goes in v10:
time: 113 us; the launch traced here: 112 us
  starting transfers between devices  38 us (34%)
  waiting for transfers between devices  33.7 us (30%)
  blocking collectives  25.5 us (23%)
  Pallas kernels  12.3 us (11%)
  local copies, waits for them, and re-layouts  1.72 us (2%)
    ppermute x20, starting transfers between devices, send(): return lax.ppermute(value, AXES, pairs)  32.6 us
    all_to_all x1, blocking collectives, local(): lax.all_to_all(c_part, AXES, 0, 0, axis_index_groups=C_GROUPS, tiled=True)  25.5 us
    all_to_all x1, waiting for transfers between devices, local(): lax.all_to_all(w_part, AXES, 0, 0, axis_index_groups=W_GROUPS, tiled=True)  17.2 us
    ppermute x20, waiting for transfers between devices, send(): return lax.ppermute(value, AXES, pairs)  16.6 us
    all_to_all x1, starting transfers between devices, local(): lax.all_to_all(w_part, AXES, 0, 0, axis_index_groups=W_GROUPS, tiled=True)  5.38 us
    pallas_call x2, Pallas kernels, w_products(): on_device(functools.partial(w_kernel, LANES * len(before)), (LANES * (1 +...  3.93 us
    pallas_call x1, Pallas kernels, masked(): pl.pallas_call(mask_kernel, out_shape=[jax.ShapeDtypeStruct(v.shape, v.dt...  2.79 us
    pallas_call x1, Pallas kernels, c_products(): on_device(other_kernel, chunks.shape, chunks.dtype, [VMEM] * (len(passed)...  2.39 us
  transfers between devices with their start and end apart: 21, of which 8 were waited for; matrix products, arithmetic and copies ran while one was open for 0% of the time, Pallas kernels for 6%

profile of v10, /device:TPU:2, one launch (start us, length us, event | category | flops | bytes accessed | tf_op | source)
XLA Modules:
  0.0 112.2 jit_solution(1382352699559707674)
XLA Ops:
  0.0 2.8 %shard_map.46 = (bf16[768,128]{1,0:T(8,128)(2,1)}, bf16[768,768]{1,0:T(8,128)(2,1)}) custom-call(bf16[768,128]{1,0:T(8,128)(2,1)} %p_any.1, bf16[768,768]{1,0:T(8,128)(2,1)} %a_any.1, s32[1,6]{1,0:T(1,128)} %bitcast.14, s32[6,6]{1,0:T(8,128)} %a_pattern.1), custom_call_target="tpu_custom_call" | custom-call | flops 589824 | bytes 4194304 | tf_op jit(solution)/shard_map/pallas_call | solution.py:141
  2.8 7.3 %collective-permute-start = (bf16[768,128]{1,0:T(8,128)(2,1)}, bf16[768,128]{1,0:T(8,128)(2,1)S(1)}, u32[]{:S(2)}, u32[]{:S(2)}) collective-permute-start(bf16[768,128]{1,0:T(8,128)(2,1)} %get-tuple-element.27.one), channel_id=1, source_target_pairs={{0,128},{1,129},{2,130},{3,131},{4,96},{5,97},{6,98},{7,99},{8,64}... | collective-permute-start | bytes 589832 | tf_op jit(solution)/shard_map/ppermute | solution.py:31
  10.1 1.6 %collective-permute-start.1 = (bf16[768,128]{1,0:T(8,128)(2,1)}, bf16[768,128]{1,0:T(8,128)(2,1)S(1)}, u32[]{:S(2)}, u32[]{:S(2)}) collective-permute-start(bf16[768,128]{1,0:T(8,128)(2,1)} %get-tuple-element.27.one), channel_id=1, source_target_pairs={{0,0},{1,1},{2,2},{3,3},{4,224},{5,225},{6,226},{7,227},{8,192},{9... | collective-permute-start | bytes 589832 | tf_op jit(solution)/shard_map/ppermute | solution.py:31
  11.6 2.1 %collective-permute-start.4 = (bf16[768,128]{1,0:T(8,128)(2,1)}, bf16[768,128]{1,0:T(8,128)(2,1)S(1)}, u32[]{:S(2)}, u32[]{:S(2)}) collective-permute-start(bf16[768,128]{1,0:T(8,128)(2,1)} %get-tuple-element.27.one), channel_id=1, source_target_pairs={{0,2},{1,3},{2,0},{3,1},{4,6},{5,7},{6,4},{7,5},{8,10},{9,11},{10,... | collective-permute-start | bytes 589832 | tf_op jit(solution)/shard_map/ppermute | solution.py:31
  13.8 4.2 %collective-permute-start.9 = (bf16[768,768]{1,0:T(8,128)(2,1)}, bf16[768,768]{1,0:T(8,128)(2,1)S(1)}, u32[]{:S(2)}, u32[]{:S(2)}) collective-permute-start(bf16[768,768]{1,0:T(8,128)(2,1)} %get-tuple-element.33), channel_id=1, source_target_pairs={{0,0},{1,16},{2,2},{3,18},{4,4},{5,20},{6,6},{7,22},{8,8},{9,24},{... | collective-permute-start | bytes 3538952 | tf_op jit(solution)/shard_map/ppermute | solution.py:31
  18.1 0.7 collective-permute-done.two
  19.2 8.4 %collective-permute-start.3 = (bf16[2,768,128]{2,1,0:T(8,128)(2,1)S(1)}, bf16[2,768,128]{2,1,0:T(8,128)(2,1)S(1)}, u32[]{:S(2)}, u32[]{:S(2)}) collective-permute-start(bf16[2,768,128]{2,1,0:T(8,128)(2,1)S(1)} %shard_map.47.own), channel_id=1, source_target_pairs={{0,224},{1,225},{2,226},{3,227},{4,228},{5,229},{6,230},{7,231},{8... | collective-permute-start | bytes 1179656 | tf_op jit(solution)/shard_map/ppermute | solution.py:31
  27.7 0.9 copy-done.2
  28.8 8.0 %collective-permute-done.2.below = bf16[2,768,128]{2,1,0:T(8,128)(2,1)S(1)} collective-permute-done((bf16[2,768,128]{2,1,0:T(8,128)(2,1)S(1)}, bf16[2,768,128]{2,1,0:T(8,128)(2,1)S(1)}, u32[]{:S(2)}, u32[]{:S(2)}) %collective-permute-start.2) | collective-permute-done | bytes 393248 | tf_op jit(solution)/shard_map/ppermute | solution.py:31
  36.9 3.8 %collective-permute-done.5.refs_1_ = bf16[2,768,128]{2,1,0:T(8,128)(2,1)S(1)} collective-permute-done((bf16[2,768,128]{2,1,0:T(8,128)(2,1)S(1)}, bf16[2,768,128]{2,1,0:T(8,128)(2,1)S(1)}, u32[]{:S(2)}, u32[]{:S(2)}) %collective-permute-start.5) | collective-permute-done | bytes 393248 | tf_op jit(solution)/shard_map/ppermute | solution.py:31
  40.8 3.3 %collective-permute-start.7 = (bf16[768,128]{1,0:T(8,128)(2,1)S(1)}, bf16[768,128]{1,0:T(8,128)(2,1)S(1)}, u32[]{:S(2)}, u32[]{:S(2)}) collective-permute-start(bf16[768,128]{1,0:T(8,128)(2,1)S(1)} %slice_bitcast_fusion.2), channel_id=1, source_target_pairs={{0,224},{1,225},{2,226},{3,227},{4,228},{5,229},{6,230},{7,231},{8... | collective-permute-start | bytes 589832 | tf_op jit(solution)/shard_map/ppermute | solution.py:31
  44.1 3.3 %collective-permute-done.10.refs_4_ = bf16[2,768,128]{2,1,0:T(8,128)(2,1)S(1)} collective-permute-done((bf16[2,768,128]{2,1,0:T(8,128)(2,1)S(1)}, bf16[2,768,128]{2,1,0:T(8,128)(2,1)S(1)}, u32[]{:S(2)}, u32[]{:S(2)}) %collective-permute-start.10) | collective-permute-done | bytes 393248 | tf_op jit(solution)/shard_map/ppermute | solution.py:31
  48.3 2.0 %collective-permute-start.13 = (bf16[768,128]{1,0:T(8,128)(2,1)S(1)}, bf16[768,128]{1,0:T(8,128)(2,1)}, u32[]{:S(2)}, u32[]{:S(2)}) collective-permute-start(bf16[768,128]{1,0:T(8,128)(2,1)S(1)} %slice_bitcast_fusion.1), channel_id=1, source_target_pairs={{0,4},{1,5},{2,6},{3,7},{4,8},{5,9},{6,10},{7,11},{8,12},{9,13},{1... | collective-permute-start | bytes 589832 | tf_op jit(solution)/shard_map/ppermute | solution.py:31
  50.3 1.4 %collective-permute-start.14 = (bf16[768,128]{1,0:T(8,128)(2,1)S(1)}, bf16[768,128]{1,0:T(8,128)(2,1)}, u32[]{:S(2)}, u32[]{:S(2)}) collective-permute-start(bf16[768,128]{1,0:T(8,128)(2,1)S(1)} %slice_bitcast_fusion), channel_id=1, source_target_pairs={{0,12},{1,13},{2,14},{3,15},{4,0},{5,1},{6,2},{7,3},{8,4},{9,5},{1... | collective-permute-start | bytes 589832 | tf_op jit(solution)/shard_map/ppermute | solution.py:31
  51.7 0.8 shard_map.49.p_ref
  52.5 1.4 %shard_map.50.rest_0_ = bf16[4,768,128]{2,1,0:T(8,128)(2,1)S(1)} custom-call(bf16[2,768,512]{2,1,0:T(8,128)(2,1)S(1)} %shard_map.49.p_ref, bf16[768,768]{1,0:T(8,128)(2,1)S(1)} %collective-permute-done.9.one, bf16[768,768]{1,0:T(8,128)(2,1)S(1)} %collective-permute-done.8.two), custom_call_target="tpu_custom_call" | custom-call | flops 1207959552 | bytes 6291456 | tf_op jit(solution)/shard_map/pallas_call | solution.py:204
  53.9 2.6 %shard_map.51 = bf16[8,768,128]{2,1,0:T(8,128)(2,1)} custom-call(bf16[2,768,512]{2,1,0:T(8,128)(2,1)S(1)} %shard_map.49.p_ref, bf16[768,768]{1,0:T(8,128)(2,1)S(1)} %collective-permute-done.11.one, bf16[768,768]{1,0:T(8,128)(2,1)S(1)} %collective-permute-done.12.two, bf16[4,768,128]{2,1,0:T(8,128)(2,1)S(1)} %shard_map.50.rest_0_), custom_call_target="tpu_custom_call" | custom-call | flops 1207959552 | bytes 6291456 | tf_op jit(solution)/shard_map/pallas_call | solution.py:204
  57.0 5.4 %all-to-all-start = ((bf16[8,768,128]{2,1,0:T(8,128)(2,1)}), bf16[8,768,128]{2,1,0:T(8,128)(2,1)S(1)}, u32[]{:S(2)}, u32[]{:S(2)}) async-start(bf16[8,768,128]{2,1,0:T(8,128)(2,1)} %shard_map.51), calls=%async_computation | async-start | bytes 3145728 | tf_op jit(solution)/shard_map/all_to_all | solution.py:299
  62.4 0.5 collective-permute-start.16
  63.4 17.2 %all-to-all-done.parts_ref = bf16[8,768,128]{2,1,0:T(8,128)(2,1)S(1)} async-done(((bf16[8,768,128]{2,1,0:T(8,128)(2,1)}), bf16[8,768,128]{2,1,0:T(8,128)(2,1)S(1)}, u32[]{:S(2)}, u32[]{:S(2)}) %all-to-all-start) | async-done | bytes 1572896 | tf_op jit(solution)/shard_map/all_to_all | solution.py:299
  80.5 2.3 %shard_map.52 = (f32[8,136,128]{2,1,0:T(8,128)S(1)}, bf16[256,768]{1,0:T(8,128)(2,1)S(1)}) custom-call(bf16[8,768,128]{2,1,0:T(8,128)(2,1)S(1)} %all-to-all-done.parts_ref, bf16[2,768,128]{2,1,0:T(8,128)(2,1)S(1)} %shard_map.48.refs_0_, bf16[2,768,128]{2,1,0:T(8,128)(2,1)S(1)} %collective-permute-done.5.refs_1_, ...), custom_call_target="tpu_custom_call" | custom-call | flops 402653184 | bytes 4194304 | tf_op jit(solution)/shard_map/pallas_call | solution.py:254
  82.9 2.4 %shard_map.53 = f32[8,136,128]{2,1,0:T(8,128)S(1)} custom-call(bf16[256,768]{1,0:T(8,128)(2,1)S(1)} %get-tuple-element.48.w_ref, bf16[2,768,128]{2,1,0:T(8,128)(2,1)} %collective-permute-done.15.refs_0_, bf16[2,768,128]{2,1,0:T(8,128)(2,1)} %collective-permute-done.16.refs_1_, bf16[768,128]{1,0:T(8,128)(2,1)S(1)} %collective-permute-done.17.refs_2_, ...), custom_call_target="tpu_custom_call" | custom-call | flops 402653184 | bytes 4194304 | tf_op jit(solution)/shard_map/pallas_call | solution.py:262
  85.6 25.5 %all_to_all.10 = f16[16,136,128]{2,1,0:T(8,128)(2,1)S(1)} all-to-all(f16[16,136,128]{2,1,0:T(8,128)(2,1)S(1)} %pad_maximum_fusion), channel_id=1, replica_groups={{0,32,192,224,128,160,64,96,16,48,208,240,144,176,80,112},{17,49,209,24..., dimensions={0} | all-to-all | bytes 1114112 | tf_op jit(solution)/shard_map/all_to_all | solution.py:301
  111.5 0.7 copy.5
  (45 shorter events, 3.4 us)
Async XLA Ops:
  2.8 16.0 %collective-permute-start = (bf16[768,128]{1,0:T(8,128)(2,1)}, bf16[768,128]{1,0:T(8,128)(2,1)S(1)}, u32[]{:S(2)}, u32[]{:S(2)}) collective-permute-start(bf16[768,128]{1,0:T(8,128)(2,1)} %get-tuple-element.27.one), channel_id=1, source_target_pairs={{0,128},{1,129},{2,130},{3,131},{4,96},{5,97},{6,98},{7,99},{8,64}... | collective-permute-start | bytes 589832 | tf_op jit(solution)/shard_map/ppermute | solution.py:31
  10.1 8.7 %collective-permute-start.1 = (bf16[768,128]{1,0:T(8,128)(2,1)}, bf16[768,128]{1,0:T(8,128)(2,1)S(1)}, u32[]{:S(2)}, u32[]{:S(2)}) collective-permute-start(bf16[768,128]{1,0:T(8,128)(2,1)} %get-tuple-element.27.one), channel_id=1, source_target_pairs={{0,0},{1,1},{2,2},{3,3},{4,224},{5,225},{6,226},{7,227},{8,192},{9... | collective-permute-start | bytes 589832 | tf_op jit(solution)/shard_map/ppermute | solution.py:31
  11.6 16.0 %collective-permute-start.4 = (bf16[768,128]{1,0:T(8,128)(2,1)}, bf16[768,128]{1,0:T(8,128)(2,1)S(1)}, u32[]{:S(2)}, u32[]{:S(2)}) collective-permute-start(bf16[768,128]{1,0:T(8,128)(2,1)} %get-tuple-element.27.one), channel_id=1, source_target_pairs={{0,2},{1,3},{2,0},{3,1},{4,6},{5,7},{6,4},{7,5},{8,10},{9,11},{10,... | collective-permute-start | bytes 589832 | tf_op jit(solution)/shard_map/ppermute | solution.py:31
  13.8 33.9 %collective-permute-start.8 = (bf16[768,768]{1,0:T(8,128)(2,1)}, bf16[768,768]{1,0:T(8,128)(2,1)S(1)}, u32[]{:S(2)}, u32[]{:S(2)}) collective-permute-start(bf16[768,768]{1,0:T(8,128)(2,1)} %get-tuple-element.33), channel_id=1, source_target_pairs={{0,2},{1,18},{2,0},{3,16},{4,6},{5,22},{6,4},{7,20},{8,10},{9,26},... | collective-permute-start | bytes 3538952 | tf_op jit(solution)/shard_map/ppermute | solution.py:31
  13.8 33.9 %collective-permute-start.9 = (bf16[768,768]{1,0:T(8,128)(2,1)}, bf16[768,768]{1,0:T(8,128)(2,1)S(1)}, u32[]{:S(2)}, u32[]{:S(2)}) collective-permute-start(bf16[768,768]{1,0:T(8,128)(2,1)} %get-tuple-element.33), channel_id=1, source_target_pairs={{0,0},{1,16},{2,2},{3,18},{4,4},{5,20},{6,6},{7,22},{8,8},{9,24},{... | collective-permute-start | bytes 3538952 | tf_op jit(solution)/shard_map/ppermute | solution.py:31
  18.8 18.1 %collective-permute-start.2 = (bf16[2,768,128]{2,1,0:T(8,128)(2,1)S(1)}, bf16[2,768,128]{2,1,0:T(8,128)(2,1)S(1)}, u32[]{:S(2)}, u32[]{:S(2)}) collective-permute-start(bf16[2,768,128]{2,1,0:T(8,128)(2,1)S(1)} %shard_map.47.own), channel_id=1, source_target_pairs={{0,32},{1,33},{2,34},{3,35},{4,36},{5,37},{6,38},{7,39},{8,40},{9,... | collective-permute-start | bytes 1179656 | tf_op jit(solution)/shard_map/ppermute | solution.py:31
  19.2 17.7 %collective-permute-start.3 = (bf16[2,768,128]{2,1,0:T(8,128)(2,1)S(1)}, bf16[2,768,128]{2,1,0:T(8,128)(2,1)S(1)}, u32[]{:S(2)}, u32[]{:S(2)}) collective-permute-start(bf16[2,768,128]{2,1,0:T(8,128)(2,1)S(1)} %shard_map.47.own), channel_id=1, source_target_pairs={{0,224},{1,225},{2,226},{3,227},{4,228},{5,229},{6,230},{7,231},{8... | collective-permute-start | bytes 1179656 | tf_op jit(solution)/shard_map/ppermute | solution.py:31
  27.7 0.9 copy-start.2
  28.6 12.0 %collective-permute-start.5 = (bf16[2,768,128]{2,1,0:T(8,128)(2,1)S(1)}, bf16[2,768,128]{2,1,0:T(8,128)(2,1)S(1)}, u32[]{:S(2)}, u32[]{:S(2)}) collective-permute-start(bf16[2,768,128]{2,1,0:T(8,128)(2,1)S(1)} %shard_map.48.refs_0_), channel_id=1, source_target_pairs={{0,4},{1,5},{2,6},{3,7},{4,8},{5,9},{6,10},{7,11},{8,12},{9,13},{1... | collective-permute-start | bytes 1179656 | tf_op jit(solution)/shard_map/ppermute | solution.py:31
  36.9 10.5 %collective-permute-start.10 = (bf16[2,768,128]{2,1,0:T(8,128)(2,1)S(1)}, bf16[2,768,128]{2,1,0:T(8,128)(2,1)S(1)}, u32[]{:S(2)}, u32[]{:S(2)}) collective-permute-start(bf16[2,768,128]{2,1,0:T(8,128)(2,1)S(1)} %shard_map.48.refs_0_), channel_id=1, source_target_pairs={{0,12},{1,13},{2,14},{3,15},{4,0},{5,1},{6,2},{7,3},{8,4},{9,5},{1... | collective-permute-start | bytes 1179656 | tf_op jit(solution)/shard_map/ppermute | solution.py:31
  40.7 7.0 %collective-permute-start.6 = (bf16[768,128]{1,0:T(8,128)(2,1)S(1)}, bf16[768,128]{1,0:T(8,128)(2,1)S(1)}, u32[]{:S(2)}, u32[]{:S(2)}) collective-permute-start(bf16[768,128]{1,0:T(8,128)(2,1)S(1)} %slice_bitcast_fusion.3), channel_id=1, source_target_pairs={{0,32},{1,33},{2,34},{3,35},{4,36},{5,37},{6,38},{7,39},{8,40},{9,... | collective-permute-start | bytes 589832 | tf_op jit(solution)/shard_map/ppermute | solution.py:31
  40.8 6.8 %collective-permute-start.7 = (bf16[768,128]{1,0:T(8,128)(2,1)S(1)}, bf16[768,128]{1,0:T(8,128)(2,1)S(1)}, u32[]{:S(2)}, u32[]{:S(2)}) collective-permute-start(bf16[768,128]{1,0:T(8,128)(2,1)S(1)} %slice_bitcast_fusion.2), channel_id=1, source_target_pairs={{0,224},{1,225},{2,226},{3,227},{4,228},{5,229},{6,230},{7,231},{8... | collective-permute-start | bytes 589832 | tf_op jit(solution)/shard_map/ppermute | solution.py:31
  47.4 5.1 %copy-start = (bf16[2,768,128]{2,1,0:T(8,128)(2,1)}, bf16[2,768,128]{2,1,0:T(8,128)(2,1)S(1)}, u32[]{:S(2)}) copy-start(bf16[2,768,128]{2,1,0:T(8,128)(2,1)S(1)} %collective-permute-done.10.refs_4_) | copy-start | bytes 1179652
  47.7 6.3 %collective-permute-start.11 = (bf16[768,768]{1,0:T(8,128)(2,1)S(1)}, bf16[768,768]{1,0:T(8,128)(2,1)S(1)}, u32[]{:S(2)}, u32[]{:S(2)}) collective-permute-start(bf16[768,768]{1,0:T(8,128)(2,1)S(1)} %collective-permute-done.9.one), channel_id=1, source_target_pairs={{0,1},{1,0},{2,3},{3,2},{4,5},{5,4},{6,7},{7,6},{8,9},{9,8},{10,11... | collective-permute-start | bytes 3538952 | tf_op jit(solution)/shard_map/ppermute | solution.py:31
  47.8 6.2 %collective-permute-start.12 = (bf16[768,768]{1,0:T(8,128)(2,1)S(1)}, bf16[768,768]{1,0:T(8,128)(2,1)S(1)}, u32[]{:S(2)}, u32[]{:S(2)}) collective-permute-start(bf16[768,768]{1,0:T(8,128)(2,1)S(1)} %collective-permute-done.8.two), channel_id=1, source_target_pairs={{0,1},{1,0},{2,3},{3,2},{4,5},{5,4},{6,7},{7,6},{8,9},{9,8},{10,11... | collective-permute-start | bytes 3538952 | tf_op jit(solution)/shard_map/ppermute | solution.py:31
  48.3 8.3 %collective-permute-start.13 = (bf16[768,128]{1,0:T(8,128)(2,1)S(1)}, bf16[768,128]{1,0:T(8,128)(2,1)}, u32[]{:S(2)}, u32[]{:S(2)}) collective-permute-start(bf16[768,128]{1,0:T(8,128)(2,1)S(1)} %slice_bitcast_fusion.1), channel_id=1, source_target_pairs={{0,4},{1,5},{2,6},{3,7},{4,8},{5,9},{6,10},{7,11},{8,12},{9,13},{1... | collective-permute-start | bytes 589832 | tf_op jit(solution)/shard_map/ppermute | solution.py:31
  50.3 6.7 %collective-permute-start.14 = (bf16[768,128]{1,0:T(8,128)(2,1)S(1)}, bf16[768,128]{1,0:T(8,128)(2,1)}, u32[]{:S(2)}, u32[]{:S(2)}) collective-permute-start(bf16[768,128]{1,0:T(8,128)(2,1)S(1)} %slice_bitcast_fusion), channel_id=1, source_target_pairs={{0,12},{1,13},{2,14},{3,15},{4,0},{5,1},{6,2},{7,3},{8,4},{9,5},{1... | collective-permute-start | bytes 589832 | tf_op jit(solution)/shard_map/ppermute | solution.py:31
  56.5 6.4 %copy-start.1 = (bf16[2,768,128]{2,1,0:T(8,128)(2,1)S(1)}, bf16[2,768,128]{2,1,0:T(8,128)(2,1)}, u32[]{:S(2)}) copy-start(bf16[2,768,128]{2,1,0:T(8,128)(2,1)} %copy-done) | copy-start | bytes 1179652
  57.0 23.6 %all-to-all-start = ((bf16[8,768,128]{2,1,0:T(8,128)(2,1)}), bf16[8,768,128]{2,1,0:T(8,128)(2,1)S(1)}, u32[]{:S(2)}, u32[]{:S(2)}) async-start(bf16[8,768,128]{2,1,0:T(8,128)(2,1)} %shard_map.51), calls=%async_computation | async-start | bytes 3145728 | tf_op jit(solution)/shard_map/all_to_all | solution.py:299
  62.4 20.6 %collective-permute-start.15 = (bf16[2,768,128]{2,1,0:T(8,128)(2,1)S(1)}, bf16[2,768,128]{2,1,0:T(8,128)(2,1)}, u32[]{:S(2)}, u32[]{:S(2)}) collective-permute-start(bf16[2,768,128]{2,1,0:T(8,128)(2,1)S(1)} %shard_map.48.refs_0_), channel_id=1, source_target_pairs={{0,1},{1,0},{2,3},{3,2},{4,5},{5,4},{6,7},{7,6},{8,9},{9,8},{10,11... | collective-permute-start | bytes 1179656 | tf_op jit(solution)/shard_map/ppermute | solution.py:31
  62.4 20.6 %collective-permute-start.16 = (bf16[2,768,128]{2,1,0:T(8,128)(2,1)S(1)}, bf16[2,768,128]{2,1,0:T(8,128)(2,1)}, u32[]{:S(2)}, u32[]{:S(2)}) collective-permute-start(bf16[2,768,128]{2,1,0:T(8,128)(2,1)S(1)} %collective-permute-done.5.refs_1_), channel_id=1, source_target_pairs={{0,1},{1,0},{2,3},{3,2},{4,5},{5,4},{6,7},{7,6},{8,9},{9,8},{10,11... | collective-permute-start | bytes 1179656 | tf_op jit(solution)/shard_map/ppermute | solution.py:31
  62.9 20.1 %collective-permute-start.19 = (bf16[2,768,128]{2,1,0:T(8,128)(2,1)S(1)}, bf16[2,768,128]{2,1,0:T(8,128)(2,1)}, u32[]{:S(2)}, u32[]{:S(2)}) collective-permute-start(bf16[2,768,128]{2,1,0:T(8,128)(2,1)S(1)} %copy-done.1), channel_id=1, source_target_pairs={{0,1},{1,0},{2,3},{3,2},{4,5},{5,4},{6,7},{7,6},{8,9},{9,8},{10,11... | collective-permute-start | bytes 1179656 | tf_op jit(solution)/shard_map/ppermute | solution.py:31
  62.9 20.0 %collective-permute-start.17 = (bf16[768,128]{1,0:T(8,128)(2,1)}, bf16[768,128]{1,0:T(8,128)(2,1)S(1)}, u32[]{:S(2)}, u32[]{:S(2)}) collective-permute-start(bf16[768,128]{1,0:T(8,128)(2,1)} %collective-permute-done.13.refs_2_), channel_id=1, source_target_pairs={{0,1},{1,0},{2,3},{3,2},{4,5},{5,4},{6,7},{7,6},{8,9},{9,8},{10,11... | collective-permute-start | bytes 589832 | tf_op jit(solution)/shard_map/ppermute | solution.py:31
  63.4 19.5 %collective-permute-start.18 = (bf16[768,128]{1,0:T(8,128)(2,1)}, bf16[768,128]{1,0:T(8,128)(2,1)}, u32[]{:S(2)}, u32[]{:S(2)}) collective-permute-start(bf16[768,128]{1,0:T(8,128)(2,1)} %collective-permute-done.14.refs_3_), channel_id=1, source_target_pairs={{0,1},{1,0},{2,3},{3,2},{4,5},{5,4},{6,7},{7,6},{8,9},{9,8},{10,11... | collective-permute-start | bytes 589832 | tf_op jit(solution)/shard_map/ppermute | solution.py:31

commit v11 on v9

--- a/solution.py
+++ b/solution.py
@@ -123,7 +123,7 @@
 def mask_kernel(p_any, a_any, p_pattern, a_pattern, p_out, a_out, p_stored, a_stored, sems):
     moves = [(p_pattern, p_stored), (p_any, p_out), (a_pattern, a_stored), (a_any, a_out)]
     copies = [pltpu.make_async_copy(*move, sems.at[i]) for i, move in enumerate(moves)]
-    for copy in copies:
+    for copy in reversed(copies):
         copy.start()
     for first, stored, out_ref in ((0, p_stored, p_out), (2, a_stored, a_out)):
         copies[first].wait()

time: 112 us -> 112 us (level)
  no operation moved by 1% of the time
where the time goes in v11:
time: 112 us; the launch traced here: 111 us
  starting transfers between devices  38.3 us (34%)
  waiting for transfers between devices  33.2 us (30%)
  blocking collectives  24.7 us (22%)
  Pallas kernels  12.3 us (11%)
  local copies, waits for them, and re-layouts  1.72 us (2%)
    ppermute x20, starting transfers between devices, send(): return lax.ppermute(value, AXES, pairs)  32.8 us
    all_to_all x1, blocking collectives, local(): lax.all_to_all(c_part, AXES, 0, 0, axis_index_groups=C_GROUPS, tiled=True)  24.7 us
    all_to_all x1, waiting for transfers between devices, local(): lax.all_to_all(w_part, AXES, 0, 0, axis_index_groups=W_GROUPS, tiled=True)  17.4 us
    ppermute x20, waiting for transfers between devices, send(): return lax.ppermute(value, AXES, pairs)  15.8 us
    all_to_all x1, starting transfers between devices, local(): lax.all_to_all(w_part, AXES, 0, 0, axis_index_groups=W_GROUPS, tiled=True)  5.52 us
    pallas_call x2, Pallas kernels, w_products(): on_device(functools.partial(w_kernel, LANES * len(before)), (LANES * (1 +...  3.93 us
    pallas_call x1, Pallas kernels, masked(): pl.pallas_call(mask_kernel, out_shape=[jax.ShapeDtypeStruct(v.shape, v.dt...  2.79 us
    pallas_call x1, Pallas kernels, c_products(): on_device(other_kernel, chunks.shape, chunks.dtype, [VMEM] * (len(passed)...  2.4 us
  transfers between devices with their start and end apart: 21, of which 9 were waited for; matrix products, arithmetic and copies ran while one was open for 0% of the time, Pallas kernels for 6%

profile of v11, /device:TPU:2, one launch (start us, length us, event | category | flops | bytes accessed | tf_op | source)
XLA Modules:
  0.0 111.3 jit_solution(6062703506312175005)
XLA Ops:
  0.0 2.8 %shard_map.46 = (bf16[768,128]{1,0:T(8,128)(2,1)}, bf16[768,768]{1,0:T(8,128)(2,1)}) custom-call(bf16[768,128]{1,0:T(8,128)(2,1)} %p_any.1, bf16[768,768]{1,0:T(8,128)(2,1)} %a_any.1, s32[1,6]{1,0:T(1,128)} %bitcast.14, s32[6,6]{1,0:T(8,128)} %a_pattern.1), custom_call_target="tpu_custom_call" | custom-call | flops 589824 | bytes 4194304 | tf_op jit(solution)/shard_map/pallas_call | solution.py:141
  2.8 1.6 %collective-permute-start = (bf16[768,128]{1,0:T(8,128)(2,1)}, bf16[768,128]{1,0:T(8,128)(2,1)S(1)}, u32[]{:S(2)}, u32[]{:S(2)}) collective-permute-start(bf16[768,128]{1,0:T(8,128)(2,1)} %get-tuple-element.27.one), channel_id=1, source_target_pairs={{0,0},{1,1},{2,2},{3,3},{4,224},{5,225},{6,226},{7,227},{8,192},{9... | collective-permute-start | bytes 589832 | tf_op jit(solution)/shard_map/ppermute | solution.py:31
  4.4 9.9 %collective-permute-start.1 = (bf16[768,128]{1,0:T(8,128)(2,1)}, bf16[768,128]{1,0:T(8,128)(2,1)S(1)}, u32[]{:S(2)}, u32[]{:S(2)}) collective-permute-start(bf16[768,128]{1,0:T(8,128)(2,1)} %get-tuple-element.27.one), channel_id=1, source_target_pairs={{0,128},{1,129},{2,130},{3,131},{4,96},{5,97},{6,98},{7,99},{8,64}... | collective-permute-start | bytes 589832 | tf_op jit(solution)/shard_map/ppermute | solution.py:31
  14.3 2.1 %collective-permute-start.4 = (bf16[768,128]{1,0:T(8,128)(2,1)}, bf16[768,128]{1,0:T(8,128)(2,1)S(1)}, u32[]{:S(2)}, u32[]{:S(2)}) collective-permute-start(bf16[768,128]{1,0:T(8,128)(2,1)} %get-tuple-element.27.one), channel_id=1, source_target_pairs={{0,2},{1,3},{2,0},{3,1},{4,6},{5,7},{6,4},{7,5},{8,10},{9,11},{10,... | collective-permute-start | bytes 589832 | tf_op jit(solution)/shard_map/ppermute | solution.py:31
  16.4 4.2 %collective-permute-start.9 = (bf16[768,768]{1,0:T(8,128)(2,1)}, bf16[768,768]{1,0:T(8,128)(2,1)S(1)}, u32[]{:S(2)}, u32[]{:S(2)}) collective-permute-start(bf16[768,768]{1,0:T(8,128)(2,1)} %get-tuple-element.33), channel_id=1, source_target_pairs={{0,0},{1,16},{2,2},{3,18},{4,4},{5,20},{6,6},{7,22},{8,8},{9,24},{... | collective-permute-start | bytes 3538952 | tf_op jit(solution)/shard_map/ppermute | solution.py:31
  20.7 2.0 %collective-permute-done.1.two = bf16[768,128]{1,0:T(8,128)(2,1)S(1)} collective-permute-done((bf16[768,128]{1,0:T(8,128)(2,1)}, bf16[768,128]{1,0:T(8,128)(2,1)S(1)}, u32[]{:S(2)}, u32[]{:S(2)}) %collective-permute-start.1) | collective-permute-done | bytes 196640 | tf_op jit(solution)/shard_map/ppermute | solution.py:31
  22.7 1.2 %collective-permute-start.2 = (bf16[2,768,128]{2,1,0:T(8,128)(2,1)S(1)}, bf16[2,768,128]{2,1,0:T(8,128)(2,1)S(1)}, u32[]{:S(2)}, u32[]{:S(2)}) collective-permute-start(bf16[2,768,128]{2,1,0:T(8,128)(2,1)S(1)} %shard_map.47.own), channel_id=1, source_target_pairs={{0,32},{1,33},{2,34},{3,35},{4,36},{5,37},{6,38},{7,39},{8,40},{9,... | collective-permute-start | bytes 1179656 | tf_op jit(solution)/shard_map/ppermute | solution.py:31
  23.9 2.5 %collective-permute-start.3 = (bf16[2,768,128]{2,1,0:T(8,128)(2,1)S(1)}, bf16[2,768,128]{2,1,0:T(8,128)(2,1)S(1)}, u32[]{:S(2)}, u32[]{:S(2)}) collective-permute-start(bf16[2,768,128]{2,1,0:T(8,128)(2,1)S(1)} %shard_map.47.own), channel_id=1, source_target_pairs={{0,224},{1,225},{2,226},{3,227},{4,228},{5,229},{6,230},{7,231},{8... | collective-permute-start | bytes 1179656 | tf_op jit(solution)/shard_map/ppermute | solution.py:31
  27.7 7.0 %collective-permute-done.2.below = bf16[2,768,128]{2,1,0:T(8,128)(2,1)S(1)} collective-permute-done((bf16[2,768,128]{2,1,0:T(8,128)(2,1)S(1)}, bf16[2,768,128]{2,1,0:T(8,128)(2,1)S(1)}, u32[]{:S(2)}, u32[]{:S(2)}) %collective-permute-start.2) | collective-permute-done | bytes 393248 | tf_op jit(solution)/shard_map/ppermute | solution.py:31
  34.7 2.7 %collective-permute-start.10 = (bf16[2,768,128]{2,1,0:T(8,128)(2,1)S(1)}, bf16[2,768,128]{2,1,0:T(8,128)(2,1)S(1)}, u32[]{:S(2)}, u32[]{:S(2)}) collective-permute-start(bf16[2,768,128]{2,1,0:T(8,128)(2,1)S(1)} %shard_map.48.refs_0_), channel_id=1, source_target_pairs={{0,12},{1,13},{2,14},{3,15},{4,0},{5,1},{6,2},{7,3},{8,4},{9,5},{1... | collective-permute-start | bytes 1179656 | tf_op jit(solution)/shard_map/ppermute | solution.py:31
  37.3 1.5 %collective-permute-done.5.refs_1_ = bf16[2,768,128]{2,1,0:T(8,128)(2,1)S(1)} collective-permute-done((bf16[2,768,128]{2,1,0:T(8,128)(2,1)S(1)}, bf16[2,768,128]{2,1,0:T(8,128)(2,1)S(1)}, u32[]{:S(2)}, u32[]{:S(2)}) %collective-permute-start.5) | collective-permute-done | bytes 393248 | tf_op jit(solution)/shard_map/ppermute | solution.py:31
  38.9 1.8 %collective-permute-start.6 = (bf16[768,128]{1,0:T(8,128)(2,1)S(1)}, bf16[768,128]{1,0:T(8,128)(2,1)S(1)}, u32[]{:S(2)}, u32[]{:S(2)}) collective-permute-start(bf16[768,128]{1,0:T(8,128)(2,1)S(1)} %slice_bitcast_fusion.3), channel_id=1, source_target_pairs={{0,32},{1,33},{2,34},{3,35},{4,36},{5,37},{6,38},{7,39},{8,40},{9,... | collective-permute-start | bytes 589832 | tf_op jit(solution)/shard_map/ppermute | solution.py:31
  40.7 1.6 %collective-permute-start.7 = (bf16[768,128]{1,0:T(8,128)(2,1)S(1)}, bf16[768,128]{1,0:T(8,128)(2,1)S(1)}, u32[]{:S(2)}, u32[]{:S(2)}) collective-permute-start(bf16[768,128]{1,0:T(8,128)(2,1)S(1)} %slice_bitcast_fusion.2), channel_id=1, source_target_pairs={{0,224},{1,225},{2,226},{3,227},{4,228},{5,229},{6,230},{7,231},{8... | collective-permute-start | bytes 589832 | tf_op jit(solution)/shard_map/ppermute | solution.py:31
  42.3 1.8 %collective-permute-done.10.refs_4_ = bf16[2,768,128]{2,1,0:T(8,128)(2,1)S(1)} collective-permute-done((bf16[2,768,128]{2,1,0:T(8,128)(2,1)S(1)}, bf16[2,768,128]{2,1,0:T(8,128)(2,1)S(1)}, u32[]{:S(2)}, u32[]{:S(2)}) %collective-permute-start.10) | collective-permute-done | bytes 393248 | tf_op jit(solution)/shard_map/ppermute | solution.py:31
  44.1 1.8 %collective-permute-done.6.up_two = bf16[768,128]{1,0:T(8,128)(2,1)S(1)} collective-permute-done((bf16[768,128]{1,0:T(8,128)(2,1)S(1)}, bf16[768,128]{1,0:T(8,128)(2,1)S(1)}, u32[]{:S(2)}, u32[]{:S(2)}) %collective-permute-start.6) | collective-permute-done | bytes 196640 | tf_op jit(solution)/shard_map/ppermute | solution.py:31
  47.9 1.7 %collective-permute-start.13 = (bf16[768,128]{1,0:T(8,128)(2,1)S(1)}, bf16[768,128]{1,0:T(8,128)(2,1)}, u32[]{:S(2)}, u32[]{:S(2)}) collective-permute-start(bf16[768,128]{1,0:T(8,128)(2,1)S(1)} %slice_bitcast_fusion.1), channel_id=1, source_target_pairs={{0,4},{1,5},{2,6},{3,7},{4,8},{5,9},{6,10},{7,11},{8,12},{9,13},{1... | collective-permute-start | bytes 589832 | tf_op jit(solution)/shard_map/ppermute | solution.py:31
  49.7 1.6 %collective-permute-start.14 = (bf16[768,128]{1,0:T(8,128)(2,1)S(1)}, bf16[768,128]{1,0:T(8,128)(2,1)}, u32[]{:S(2)}, u32[]{:S(2)}) collective-permute-start(bf16[768,128]{1,0:T(8,128)(2,1)S(1)} %slice_bitcast_fusion), channel_id=1, source_target_pairs={{0,12},{1,13},{2,14},{3,15},{4,0},{5,1},{6,2},{7,3},{8,4},{9,5},{1... | collective-permute-start | bytes 589832 | tf_op jit(solution)/shard_map/ppermute | solution.py:31
  52.2 1.4 %shard_map.50.rest_0_ = bf16[4,768,128]{2,1,0:T(8,128)(2,1)S(1)} custom-call(bf16[2,768,512]{2,1,0:T(8,128)(2,1)S(1)} %shard_map.49.p_ref, bf16[768,768]{1,0:T(8,128)(2,1)S(1)} %collective-permute-done.9.one, bf16[768,768]{1,0:T(8,128)(2,1)S(1)} %collective-permute-done.8.two), custom_call_target="tpu_custom_call" | custom-call | flops 1207959552 | bytes 6291456 | tf_op jit(solution)/shard_map/pallas_call | solution.py:204
  53.6 2.6 %shard_map.51 = bf16[8,768,128]{2,1,0:T(8,128)(2,1)} custom-call(bf16[2,768,512]{2,1,0:T(8,128)(2,1)S(1)} %shard_map.49.p_ref, bf16[768,768]{1,0:T(8,128)(2,1)S(1)} %collective-permute-done.11.one, bf16[768,768]{1,0:T(8,128)(2,1)S(1)} %collective-permute-done.12.two, bf16[4,768,128]{2,1,0:T(8,128)(2,1)S(1)} %shard_map.50.rest_0_), custom_call_target="tpu_custom_call" | custom-call | flops 1207959552 | bytes 6291456 | tf_op jit(solution)/shard_map/pallas_call | solution.py:204
  56.4 5.5 %all-to-all-start = ((bf16[8,768,128]{2,1,0:T(8,128)(2,1)}), bf16[8,768,128]{2,1,0:T(8,128)(2,1)S(1)}, u32[]{:S(2)}, u32[]{:S(2)}) async-start(bf16[8,768,128]{2,1,0:T(8,128)(2,1)} %shard_map.51), calls=%async_computation | async-start | bytes 3145728 | tf_op jit(solution)/shard_map/all_to_all | solution.py:299
  62.9 17.4 %all-to-all-done.parts_ref = bf16[8,768,128]{2,1,0:T(8,128)(2,1)S(1)} async-done(((bf16[8,768,128]{2,1,0:T(8,128)(2,1)}), bf16[8,768,128]{2,1,0:T(8,128)(2,1)S(1)}, u32[]{:S(2)}, u32[]{:S(2)}) %all-to-all-start) | async-done | bytes 1572896 | tf_op jit(solution)/shard_map/all_to_all | solution.py:299
  80.3 2.3 %shard_map.52 = (f32[8,136,128]{2,1,0:T(8,128)S(1)}, bf16[256,768]{1,0:T(8,128)(2,1)S(1)}) custom-call(bf16[8,768,128]{2,1,0:T(8,128)(2,1)S(1)} %all-to-all-done.parts_ref, bf16[2,768,128]{2,1,0:T(8,128)(2,1)S(1)} %shard_map.48.refs_0_, bf16[2,768,128]{2,1,0:T(8,128)(2,1)S(1)} %collective-permute-done.5.refs_1_, ...), custom_call_target="tpu_custom_call" | custom-call | flops 402653184 | bytes 4194304 | tf_op jit(solution)/shard_map/pallas_call | solution.py:254
  82.7 2.4 %shard_map.53 = f32[8,136,128]{2,1,0:T(8,128)S(1)} custom-call(bf16[256,768]{1,0:T(8,128)(2,1)S(1)} %get-tuple-element.48.w_ref, bf16[2,768,128]{2,1,0:T(8,128)(2,1)} %collective-permute-done.15.refs_0_, bf16[2,768,128]{2,1,0:T(8,128)(2,1)} %collective-permute-done.16.refs_1_, bf16[768,128]{1,0:T(8,128)(2,1)S(1)} %collective-permute-done.17.refs_2_, ...), custom_call_target="tpu_custom_call" | custom-call | flops 402653184 | bytes 4194304 | tf_op jit(solution)/shard_map/pallas_call | solution.py:262
  85.4 24.7 %all_to_all.10 = f16[16,136,128]{2,1,0:T(8,128)(2,1)S(1)} all-to-all(f16[16,136,128]{2,1,0:T(8,128)(2,1)S(1)} %pad_maximum_fusion), channel_id=1, replica_groups={{0,32,192,224,128,160,64,96,16,48,208,240,144,176,80,112},{17,49,209,24..., dimensions={0} | all-to-all | bytes 1114112 | tf_op jit(solution)/shard_map/all_to_all | solution.py:301
  (45 shorter events, 7.0 us)
Async XLA Ops:
  2.8 17.9 %collective-permute-start = (bf16[768,128]{1,0:T(8,128)(2,1)}, bf16[768,128]{1,0:T(8,128)(2,1)S(1)}, u32[]{:S(2)}, u32[]{:S(2)}) collective-permute-start(bf16[768,128]{1,0:T(8,128)(2,1)} %get-tuple-element.27.one), channel_id=1, source_target_pairs={{0,0},{1,1},{2,2},{3,3},{4,224},{5,225},{6,226},{7,227},{8,192},{9... | collective-permute-start | bytes 589832 | tf_op jit(solution)/shard_map/ppermute | solution.py:31
  4.4 18.3 %collective-permute-start.1 = (bf16[768,128]{1,0:T(8,128)(2,1)}, bf16[768,128]{1,0:T(8,128)(2,1)S(1)}, u32[]{:S(2)}, u32[]{:S(2)}) collective-permute-start(bf16[768,128]{1,0:T(8,128)(2,1)} %get-tuple-element.27.one), channel_id=1, source_target_pairs={{0,128},{1,129},{2,130},{3,131},{4,96},{5,97},{6,98},{7,99},{8,64}... | collective-permute-start | bytes 589832 | tf_op jit(solution)/shard_map/ppermute | solution.py:31
  14.3 12.2 %collective-permute-start.4 = (bf16[768,128]{1,0:T(8,128)(2,1)}, bf16[768,128]{1,0:T(8,128)(2,1)S(1)}, u32[]{:S(2)}, u32[]{:S(2)}) collective-permute-start(bf16[768,128]{1,0:T(8,128)(2,1)} %get-tuple-element.27.one), channel_id=1, source_target_pairs={{0,2},{1,3},{2,0},{3,1},{4,6},{5,7},{6,4},{7,5},{8,10},{9,11},{10,... | collective-permute-start | bytes 589832 | tf_op jit(solution)/shard_map/ppermute | solution.py:31
  16.4 31.0 %collective-permute-start.8 = (bf16[768,768]{1,0:T(8,128)(2,1)}, bf16[768,768]{1,0:T(8,128)(2,1)S(1)}, u32[]{:S(2)}, u32[]{:S(2)}) collective-permute-start(bf16[768,768]{1,0:T(8,128)(2,1)} %get-tuple-element.33), channel_id=1, source_target_pairs={{0,2},{1,18},{2,0},{3,16},{4,6},{5,22},{6,4},{7,20},{8,10},{9,26},... | collective-permute-start | bytes 3538952 | tf_op jit(solution)/shard_map/ppermute | solution.py:31
  16.4 31.0 %collective-permute-start.9 = (bf16[768,768]{1,0:T(8,128)(2,1)}, bf16[768,768]{1,0:T(8,128)(2,1)S(1)}, u32[]{:S(2)}, u32[]{:S(2)}) collective-permute-start(bf16[768,768]{1,0:T(8,128)(2,1)} %get-tuple-element.33), channel_id=1, source_target_pairs={{0,0},{1,16},{2,2},{3,18},{4,4},{5,20},{6,6},{7,22},{8,8},{9,24},{... | collective-permute-start | bytes 3538952 | tf_op jit(solution)/shard_map/ppermute | solution.py:31
  22.7 12.0 %collective-permute-start.2 = (bf16[2,768,128]{2,1,0:T(8,128)(2,1)S(1)}, bf16[2,768,128]{2,1,0:T(8,128)(2,1)S(1)}, u32[]{:S(2)}, u32[]{:S(2)}) collective-permute-start(bf16[2,768,128]{2,1,0:T(8,128)(2,1)S(1)} %shard_map.47.own), channel_id=1, source_target_pairs={{0,32},{1,33},{2,34},{3,35},{4,36},{5,37},{6,38},{7,39},{8,40},{9,... | collective-permute-start | bytes 1179656 | tf_op jit(solution)/shard_map/ppermute | solution.py:31
  23.9 13.4 %collective-permute-start.3 = (bf16[2,768,128]{2,1,0:T(8,128)(2,1)S(1)}, bf16[2,768,128]{2,1,0:T(8,128)(2,1)S(1)}, u32[]{:S(2)}, u32[]{:S(2)}) collective-permute-start(bf16[2,768,128]{2,1,0:T(8,128)(2,1)S(1)} %shard_map.47.own), channel_id=1, source_target_pairs={{0,224},{1,225},{2,226},{3,227},{4,228},{5,229},{6,230},{7,231},{8... | collective-permute-start | bytes 1179656 | tf_op jit(solution)/shard_map/ppermute | solution.py:31
  26.5 0.9 copy-start.2
  27.4 11.4 %collective-permute-start.5 = (bf16[2,768,128]{2,1,0:T(8,128)(2,1)S(1)}, bf16[2,768,128]{2,1,0:T(8,128)(2,1)S(1)}, u32[]{:S(2)}, u32[]{:S(2)}) collective-permute-start(bf16[2,768,128]{2,1,0:T(8,128)(2,1)S(1)} %shard_map.48.refs_0_), channel_id=1, source_target_pairs={{0,4},{1,5},{2,6},{3,7},{4,8},{5,9},{6,10},{7,11},{8,12},{9,13},{1... | collective-permute-start | bytes 1179656 | tf_op jit(solution)/shard_map/ppermute | solution.py:31
  34.7 9.4 %collective-permute-start.10 = (bf16[2,768,128]{2,1,0:T(8,128)(2,1)S(1)}, bf16[2,768,128]{2,1,0:T(8,128)(2,1)S(1)}, u32[]{:S(2)}, u32[]{:S(2)}) collective-permute-start(bf16[2,768,128]{2,1,0:T(8,128)(2,1)S(1)} %shard_map.48.refs_0_), channel_id=1, source_target_pairs={{0,12},{1,13},{2,14},{3,15},{4,0},{5,1},{6,2},{7,3},{8,4},{9,5},{1... | collective-permute-start | bytes 1179656 | tf_op jit(solution)/shard_map/ppermute | solution.py:31
  38.9 7.0 %collective-permute-start.6 = (bf16[768,128]{1,0:T(8,128)(2,1)S(1)}, bf16[768,128]{1,0:T(8,128)(2,1)S(1)}, u32[]{:S(2)}, u32[]{:S(2)}) collective-permute-start(bf16[768,128]{1,0:T(8,128)(2,1)S(1)} %slice_bitcast_fusion.3), channel_id=1, source_target_pairs={{0,32},{1,33},{2,34},{3,35},{4,36},{5,37},{6,38},{7,39},{8,40},{9,... | collective-permute-start | bytes 589832 | tf_op jit(solution)/shard_map/ppermute | solution.py:31
  40.7 5.7 %collective-permute-start.7 = (bf16[768,128]{1,0:T(8,128)(2,1)S(1)}, bf16[768,128]{1,0:T(8,128)(2,1)S(1)}, u32[]{:S(2)}, u32[]{:S(2)}) collective-permute-start(bf16[768,128]{1,0:T(8,128)(2,1)S(1)} %slice_bitcast_fusion.2), channel_id=1, source_target_pairs={{0,224},{1,225},{2,226},{3,227},{4,228},{5,229},{6,230},{7,231},{8... | collective-permute-start | bytes 589832 | tf_op jit(solution)/shard_map/ppermute | solution.py:31
  44.1 8.1 %copy-start = (bf16[2,768,128]{2,1,0:T(8,128)(2,1)}, bf16[2,768,128]{2,1,0:T(8,128)(2,1)S(1)}, u32[]{:S(2)}) copy-start(bf16[2,768,128]{2,1,0:T(8,128)(2,1)S(1)} %collective-permute-done.10.refs_4_) | copy-start | bytes 1179652
  47.4 6.2 %collective-permute-start.11 = (bf16[768,768]{1,0:T(8,128)(2,1)S(1)}, bf16[768,768]{1,0:T(8,128)(2,1)S(1)}, u32[]{:S(2)}, u32[]{:S(2)}) collective-permute-start(bf16[768,768]{1,0:T(8,128)(2,1)S(1)} %collective-permute-done.9.one), channel_id=1, source_target_pairs={{0,1},{1,0},{2,3},{3,2},{4,5},{5,4},{6,7},{7,6},{8,9},{9,8},{10,11... | collective-permute-start | bytes 3538952 | tf_op jit(solution)/shard_map/ppermute | solution.py:31
  47.4 6.2 %collective-permute-start.12 = (bf16[768,768]{1,0:T(8,128)(2,1)S(1)}, bf16[768,768]{1,0:T(8,128)(2,1)S(1)}, u32[]{:S(2)}, u32[]{:S(2)}) collective-permute-start(bf16[768,768]{1,0:T(8,128)(2,1)S(1)} %collective-permute-done.8.two), channel_id=1, source_target_pairs={{0,1},{1,0},{2,3},{3,2},{4,5},{5,4},{6,7},{7,6},{8,9},{9,8},{10,11... | collective-permute-start | bytes 3538952 | tf_op jit(solution)/shard_map/ppermute | solution.py:31
  47.9 8.2 %collective-permute-start.13 = (bf16[768,128]{1,0:T(8,128)(2,1)S(1)}, bf16[768,128]{1,0:T(8,128)(2,1)}, u32[]{:S(2)}, u32[]{:S(2)}) collective-permute-start(bf16[768,128]{1,0:T(8,128)(2,1)S(1)} %slice_bitcast_fusion.1), channel_id=1, source_target_pairs={{0,4},{1,5},{2,6},{3,7},{4,8},{5,9},{6,10},{7,11},{8,12},{9,13},{1... | collective-permute-start | bytes 589832 | tf_op jit(solution)/shard_map/ppermute | solution.py:31
  49.7 6.7 %collective-permute-start.14 = (bf16[768,128]{1,0:T(8,128)(2,1)S(1)}, bf16[768,128]{1,0:T(8,128)(2,1)}, u32[]{:S(2)}, u32[]{:S(2)}) collective-permute-start(bf16[768,128]{1,0:T(8,128)(2,1)S(1)} %slice_bitcast_fusion), channel_id=1, source_target_pairs={{0,12},{1,13},{2,14},{3,15},{4,0},{5,1},{6,2},{7,3},{8,4},{9,5},{1... | collective-permute-start | bytes 589832 | tf_op jit(solution)/shard_map/ppermute | solution.py:31
  56.1 6.3 %copy-start.1 = (bf16[2,768,128]{2,1,0:T(8,128)(2,1)S(1)}, bf16[2,768,128]{2,1,0:T(8,128)(2,1)}, u32[]{:S(2)}) copy-start(bf16[2,768,128]{2,1,0:T(8,128)(2,1)} %copy-done) | copy-start | bytes 1179652
  56.4 23.9 %all-to-all-start = ((bf16[8,768,128]{2,1,0:T(8,128)(2,1)}), bf16[8,768,128]{2,1,0:T(8,128)(2,1)S(1)}, u32[]{:S(2)}, u32[]{:S(2)}) async-start(bf16[8,768,128]{2,1,0:T(8,128)(2,1)} %shard_map.51), calls=%async_computation | async-start | bytes 3145728 | tf_op jit(solution)/shard_map/all_to_all | solution.py:299
  61.9 20.8 %collective-permute-start.15 = (bf16[2,768,128]{2,1,0:T(8,128)(2,1)S(1)}, bf16[2,768,128]{2,1,0:T(8,128)(2,1)}, u32[]{:S(2)}, u32[]{:S(2)}) collective-permute-start(bf16[2,768,128]{2,1,0:T(8,128)(2,1)S(1)} %shard_map.48.refs_0_), channel_id=1, source_target_pairs={{0,1},{1,0},{2,3},{3,2},{4,5},{5,4},{6,7},{7,6},{8,9},{9,8},{10,11... | collective-permute-start | bytes 1179656 | tf_op jit(solution)/shard_map/ppermute | solution.py:31
  61.9 20.8 %collective-permute-start.16 = (bf16[2,768,128]{2,1,0:T(8,128)(2,1)S(1)}, bf16[2,768,128]{2,1,0:T(8,128)(2,1)}, u32[]{:S(2)}, u32[]{:S(2)}) collective-permute-start(bf16[2,768,128]{2,1,0:T(8,128)(2,1)S(1)} %collective-permute-done.5.refs_1_), channel_id=1, source_target_pairs={{0,1},{1,0},{2,3},{3,2},{4,5},{5,4},{6,7},{7,6},{8,9},{9,8},{10,11... | collective-permute-start | bytes 1179656 | tf_op jit(solution)/shard_map/ppermute | solution.py:31
  62.4 20.3 %collective-permute-start.19 = (bf16[2,768,128]{2,1,0:T(8,128)(2,1)S(1)}, bf16[2,768,128]{2,1,0:T(8,128)(2,1)}, u32[]{:S(2)}, u32[]{:S(2)}) collective-permute-start(bf16[2,768,128]{2,1,0:T(8,128)(2,1)S(1)} %copy-done.1), channel_id=1, source_target_pairs={{0,1},{1,0},{2,3},{3,2},{4,5},{5,4},{6,7},{7,6},{8,9},{9,8},{10,11... | collective-permute-start | bytes 1179656 | tf_op jit(solution)/shard_map/ppermute | solution.py:31
  62.4 20.2 %collective-permute-start.17 = (bf16[768,128]{1,0:T(8,128)(2,1)}, bf16[768,128]{1,0:T(8,128)(2,1)S(1)}, u32[]{:S(2)}, u32[]{:S(2)}) collective-permute-start(bf16[768,128]{1,0:T(8,128)(2,1)} %collective-permute-done.13.refs_2_), channel_id=1, source_target_pairs={{0,1},{1,0},{2,3},{3,2},{4,5},{5,4},{6,7},{7,6},{8,9},{9,8},{10,11... | collective-permute-start | bytes 589832 | tf_op jit(solution)/shard_map/ppermute | solution.py:31
  62.9 19.8 %collective-permute-start.18 = (bf16[768,128]{1,0:T(8,128)(2,1)}, bf16[768,128]{1,0:T(8,128)(2,1)}, u32[]{:S(2)}, u32[]{:S(2)}) collective-permute-start(bf16[768,128]{1,0:T(8,128)(2,1)} %collective-permute-done.14.refs_3_), channel_id=1, source_target_pairs={{0,1},{1,0},{2,3},{3,2},{4,5},{5,4},{6,7},{7,6},{8,9},{9,8},{10,11... | collective-permute-start | bytes 589832 | tf_op jit(solution)/shard_map/ppermute | solution.py:31
